TPU v7x, 32 devices: a whole 2x2x4 slice. The times are simulated.
32 devices in a mesh: dp: 8 (over z, y), mp: 4 (over x, core).
Axes of the slice: x: 2, y: 2, z: 4, core: 2. Of those that a mesh axis runs over, the one named last changes fastest.
Arguments:
- layer_input: bfloat16 [8192, 1024], P('dp'), may hold values from -6 to 6
- output_cot: bfloat16 [8192, 1024], P('dp'), may hold values from -6 to 6
- score_cot: float32 [4, 16], replicated, may hold values from -24 to 24
- query_lengths: int32 [4, 16], replicated, may hold values from 1 to 128, 1024 in all within a row
- passage_lengths: int32 [4, 4], replicated, may hold values from 1 to 512, 1024 in all within a row
- pairing: int32 [4, 16], replicated, may hold values from 0 to 3
- match_offset: int32 [4, 1024], replicated, may hold values from 0 to 511
- block_order: int32 [4, 192], P('mp'), may hold values from 0 to 191, as said below
- block_master: float32 [768, 128, 128], P(('dp', 'mp'))
- block_first: float32 [768, 128, 128], P(('dp', 'mp'))
- block_second: float32 [768, 128, 128], P(('dp', 'mp')), as said below
- basis_left: float32 [768, 128, 128], P(('dp', 'mp')), as said below
- basis_right: float32 [768, 128, 128], P(('dp', 'mp')), as said below
- bias_state: float32 [3, 6144], P(None, 'mp'), as said below
- norm_state: float32 [3, 6, 1024], replicated, as said below
Outputs:
- output_rows: bfloat16 [8192, 1024], P('dp')
- scores: float32 [4, 16], replicated
- input_grad: bfloat16 [8192, 1024], P('dp')
- block_grad: float32 [768, 128, 128], P(('dp', 'mp'))
- block_first_new: float32 [768, 128, 128], P(('dp', 'mp'))
- block_second_new: float32 [768, 128, 128], P(('dp', 'mp'))
- block_master_new: float32 [768, 128, 128], P(('dp', 'mp'))
- bias_out: float32 [3, 6144], P(None, 'mp')
- norm_out: float32 [3, 6, 1024], replicated
- small_values: float32 [12288], P('mp')
Inputs may be any that keep to these rules, and one draw needn't show every extreme that they name: `block_order`: each row is a permutation of the block ids of its shard; device (i, j) owns slots i * 24 to (i+1) * 24 - 1 of row j. `query_lengths`: each row sums to 1024 and its largest entry is 128. `passage_lengths`: each row sums to 1024 and its largest entry is 512. `basis_left`: each block is an orthogonal matrix. `basis_right`: each block is an orthogonal matrix. `block_second`: entries are positive. `bias_state`: row 2 is positive. `norm_state`: row 2 is positive.
All inputs are finite; a program needn't handle non-finite values.
Results may differ from a plain program's by a relative error of at most 0.017.
Values may be sent and summed in bfloat16 or wider, within the bound.
No kernel may reach another device: no remote copies, remote signals or barrier semaphores. Data moves between devices by JAX's collectives and lax.ppermute only.
A program may use at most 192 MiB of HBM per device.

v0:
```python
import math

import jax
import jax.numpy as jnp
from jax import lax
from jax.experimental import pallas as pl
from jax.experimental.pallas import tpu as pltpu
from jax.sharding import PartitionSpec as P

D = 1024
H = 16
HD = 64
FF = 4096
ROW = 1024
STEP = 10
TILE = 256

low = jnp.bfloat16
wide = jnp.float32
beta_one = 0.9
beta_two = 0.999
adam_eps = 1e-08
norm_eps = 1e-05
block_rate = 0.05
small_rate = 0.1
mib = 2**20

NN = (((1,), (0,)), ((), ()))
NT = (((1,), (1,)), ((), ()))
TN = (((0,), (0,)), ((), ()))


def mul(left, right, dims=NN):
    return lax.dot_general(left, right, dims, preferred_element_type=wide)


def gelu_parts(values):
    normal_cdf = 0.5 * (1.0 + lax.erf(values * 0.7071067811865476))
    slope = normal_cdf + values * jnp.exp(-0.5 * values * values) * 0.3989422804014327
    return ((values * normal_cdf).astype(low), slope)


def adam_plain(grad_now, first_old, second_old, value_old, rate_now):
    first_new = beta_one * first_old + (1.0 - beta_one) * grad_now
    second_new = beta_two * second_old + (1.0 - beta_two) * grad_now * grad_now
    step_dir = (
        first_new
        / (1.0 - beta_one**STEP)
        / (jnp.sqrt(second_new / (1.0 - beta_two**STEP)) + adam_eps)
    )
    return (first_new, second_new, value_old - rate_now * step_dir)


def ring_order(count):
    return [k for k in range(count) if k % 2 == 0] + [k for k in range(count) if k % 2][::-1]


def piece_bounds(owned):
    pieces = 4 if owned >= 8 else min(2, owned)
    return [owned * k // pieces for k in range(pieces + 1)]


def vmem_call(kernel, name, outs, *args, smem=0, scratch=(), flops=0, room=4):
    vmem = pl.BlockSpec(memory_space=pltpu.VMEM)
    specs = [pl.BlockSpec(memory_space=pltpu.SMEM)] * smem + [vmem] * (len(args) - smem)
    taken = sum(v.size * v.dtype.itemsize for v in args)
    given = sum(v.size * jnp.dtype(v.dtype).itemsize for v in outs)
    held = sum(
        math.prod(v.shape) * jnp.dtype(v.dtype).itemsize for v in scratch if hasattr(v, "shape")
    )
    moved = taken + given
    return pl.pallas_call(
        kernel,
        in_specs=specs,
        out_specs=[vmem] * len(outs),
        out_shape=outs,
        scratch_shapes=list(scratch),
        compiler_params=pltpu.CompilerParams(vmem_limit_bytes=given + held + room * mib),
        cost_estimate=pl.CostEstimate(flops=flops, bytes_accessed=moved, transcendentals=0),
        name=name,
    )(*args)


def shaped(dtype, *shape):
    return jax.ShapeDtypeStruct(shape, dtype)


def matrix_views(refs, side):
    for ref in refs:
        for row in range(0, ref.shape[0], side):
            for column in range(0, ref.shape[1], side):
                yield ref.at[row : row + side, column : column + side]


def ring_member(place, count):
    place = lax.rem(place + 2 * count, count)
    return jnp.where(place < count // 2, 2 * place, 2 * count - 1 - 2 * place)


def each_travelling(place_ref, count, owned, bounds, first, visit):
    for k in range(len(bounds) - 1):
        sign = 1 if k % 2 == 0 else -1
        for step in range(count):
            owner = ring_member(place_ref[5] - sign * (first + step), count)
            start = owner * owned + bounds[k]
            for w in range(bounds[k + 1] - bounds[k]):
                visit(k * count + step, w, start + w)


def assemble(place, order, pieces, shapes_list, side, count, owned, bounds):
    def kernel(place_ref, order_ref, *refs):
        parts, outs, blocks = refs[: len(pieces)], refs[len(pieces) : -1], refs[-1]

        def visit(at, w, slot):
            blocks[order_ref[slot]] = parts[at][w]

        each_travelling(place_ref, count, owned, bounds, 0, visit)
        for k, view in enumerate(matrix_views(outs, side)):
            view[...] = blocks[k]

    return vmem_call(
        kernel,
        "assemble",
        [shaped(low, *shape) for shape in shapes_list],
        place,
        order,
        *pieces,
        smem=2,
        scratch=[pltpu.VMEM((count * owned, side, side), low)],
    )


def spread(place, order, matrices, side, count, owned, bounds):
    def kernel(place_ref, order_ref, *refs):
        sources, outs, blocks = refs[: len(matrices)], refs[len(matrices) : -1], refs[-1]
        for k, view in enumerate(matrix_views(sources, side)):
            blocks[k] = view[...]

        def visit(at, w, slot):
            outs[at][w] = blocks[order_ref[slot]]

        each_travelling(place_ref, count, owned, bounds, 1, visit)

    return vmem_call(
        kernel,
        "spread",
        [
            shaped(low, bounds[k + 1] - bounds[k], side, side)
            for k in range(len(bounds) - 1)
            for _ in range(count)
        ],
        place,
        order,
        *matrices,
        smem=2,
        scratch=[pltpu.VMEM((count * owned, side, side), low)],
    )


def in_order(place, mine, other):
    rows = mine[0].shape[0]
    count = len(mine)

    def kernel(place_ref, *refs):
        out = refs[-1]
        core = place_ref[2]
        for k in range(count):
            for ref, turn in ((refs[k], core), (refs[count + k], 1 - core)):
                start = pl.multiple_of((turn * count + k) * rows, rows)
                out[pl.ds(start, rows), :] = ref[...]

    return vmem_call(
        kernel, "in_order", [shaped(low, 2 * count * rows, D)], place, *mine, *other, smem=1
    )[0]


def feed_grads(hidden, second_rows, first_rows, pre_rows):
    count, rows = len(hidden), hidden[0].shape[0]
    inner = hidden[0].shape[1]

    def kernel(*refs):
        down_ref, up_ref, bias_ref, left, right = refs[4 * count :]

        def fill(target, sources):
            for k, ref in enumerate(sources):
                target[k * rows : (k + 1) * rows, :] = ref[...]

        fill(left, refs[:count])
        fill(right, refs[count : 2 * count])
        down_ref[...] = mul(left[...], right[...], TN).astype(low)
        fill(left, refs[2 * count : 3 * count])
        fill(right, refs[3 * count : 4 * count])
        up_ref[...] = mul(left[...], right[...], TN).astype(low)
        bias_ref[...] = jnp.sum(right[...].astype(wide), axis=0, keepdims=True)

    return vmem_call(
        kernel,
        "feed_grads",
        [shaped(low, inner, D), shaped(low, D, inner), shaped(wide, 1, inner)],
        *hidden,
        *second_rows,
        *first_rows,
        *pre_rows,
        scratch=[pltpu.VMEM((count * rows, D), low), pltpu.VMEM((count * rows, D), low)],
        flops=4 * count * rows * D * inner,
        room=12,
    )


def pair_tables(place, query_lengths, passage_lengths, pairing, score_cot, match_offset):
    queries, passages = query_lengths.shape[1], passage_lengths.shape[1]
    half = ROW // 2
    pair_scale = D ** (-0.5)

    def kernel(place_ref, ql_ref, pl_ref, pair_ref, cot_ref, offset_ref, link_ref, col_ref, row_ref):
        is_query = place_ref[0] == 1
        row = place_ref[1]
        first_core = place_ref[2] == 0
        token = lax.broadcasted_iota(jnp.int32, (1, ROW), 1)
        zero = jnp.zeros((1, ROW), jnp.int32)
        segment, start_at, length_at = zero, zero, zero
        cot = jnp.zeros((1, ROW), wide)
        start = jnp.int32(0)
        for e in range(queries):
            end = start + ql_ref[row, e]
            inside = (token >= start) & (token < end)
            chosen = pair_ref[row, e]
            before = jnp.int32(0)
            length = jnp.int32(1)
            for m in range(passages):
                span = pl_ref[row, m]
                before = before + jnp.where(m < chosen, span, 0)
                length = jnp.where(m == chosen, span, length)
            segment = jnp.where(inside, e, segment)
            start_at = jnp.where(inside, before, start_at)
            length_at = jnp.where(inside, length, length_at)
            cot = jnp.where(inside, cot_ref[row, e] * pair_scale, cot)
            start = end
        passage = zero
        start = jnp.int32(0)
        for m in range(passages):
            start = start + pl_ref[row, m]
            passage = passage + (token >= start).astype(jnp.int32)
        length_at = jnp.maximum(length_at, 1)
        target = start_at + lax.rem(offset_ref[pl.ds(row, 1), :], length_at)
        own = jnp.where(is_query, segment, passage)

        def turn(value):
            swapped = jnp.concatenate([value[:, half:], value[:, :half]], axis=1)
            return jnp.where(first_core, value, swapped)

        token = turn(token)
        target, cot, segment, own = turn(target), turn(cot), turn(segment), turn(own)
        stacked = jnp.concatenate(
            [target.astype(wide), cot, segment.astype(wide), own.astype(wide)]
            + [token.astype(wide)]
            + [jnp.zeros((3, ROW), wide)],
            axis=0,
        )
        columns = stacked.T
        col_ref[...] = columns
        row_ref[...] = own.astype(wide)
        left = jnp.where(is_query, columns[:half, 0:1], columns[:half, 4:5])
        right = jnp.where(is_query, token, target).astype(wide)
        value = jnp.where(is_query, jnp.ones_like(cot), cot)
        link_ref[...] = jnp.where(left == right, value, 0.0).astype(low)

    smem = pl.BlockSpec(memory_space=pltpu.SMEM)
    vmem = pl.BlockSpec(memory_space=pltpu.VMEM)
    return pl.pallas_call(
        kernel,
        in_specs=[smem] * 5 + [vmem],
        out_specs=[vmem] * 3,
        out_shape=[
            jax.ShapeDtypeStruct((half, ROW), low),
            jax.ShapeDtypeStruct((ROW, 8), wide),
            jax.ShapeDtypeStruct((1, ROW), wide),
        ],
        compiler_params=pltpu.CompilerParams(vmem_limit_bytes=16 * mib),
        name="pair_tables",
    )(place, query_lengths, passage_lengths, pairing, score_cot, match_offset)


def halves(value):
    top = value.astype(low)
    return (top, (value - top.astype(wide)).astype(low))


def left_parts(value):
    top, rest = halves(value)
    return jnp.concatenate([top, rest, top], axis=1)


def right_parts(value, axis=0):
    top, rest = halves(value)
    return jnp.concatenate([top, top, rest], axis=axis)


def rotate_first(blocks, left_basis, right_basis):
    count, side = blocks.shape[0], blocks.shape[1]
    group = 6 if count % 6 == 0 else 3 if count % 3 == 0 else 1

    def kernel(m_ref, l_ref, r_ref, out_ref):
        for b in range(group):
            inner = mul(left_parts(l_ref[b].T), right_parts(m_ref[b]))
            out_ref[b] = mul(left_parts(inner), right_parts(r_ref[b]))

    spec = pl.BlockSpec((group, side, side), lambda t: (t, 0, 0))
    return pl.pallas_call(
        kernel,
        grid=(count // group,),
        in_specs=[spec] * 3,
        out_specs=spec,
        out_shape=jax.ShapeDtypeStruct(blocks.shape, wide),
        compiler_params=pltpu.CompilerParams(vmem_limit_bytes=16 * mib),
        cost_estimate=pl.CostEstimate(
            flops=count * 12 * side**3, bytes_accessed=16 * count * side**2, transcendentals=0
        ),
        name="rotate_first",
    )(blocks, left_basis, right_basis)


def optimize(grad, rotated_old, master, first, second, left_basis, right_basis):
    count, side = grad.shape[0], grad.shape[1]
    group = 6 if count % 6 == 0 else 3 if count % 3 == 0 else 1

    def kernel(g_ref, c_ref, w_ref, m_ref, v_ref, l_ref, r_ref, m_out, v_out, w_out):
        for b in range(group):
            grad_now = g_ref[b]
            m_out[b] = beta_one * m_ref[b] + (1.0 - beta_one) * grad_now
            left, right = l_ref[b], r_ref[b]
            inner = mul(left_parts(left.T), right_parts(grad_now))
            turned = mul(left_parts(inner), right_parts(right))
            second_new = beta_two * v_ref[b] + (1.0 - beta_two) * turned * turned
            v_out[b] = second_new
            first_turned = beta_one * c_ref[b] + (1.0 - beta_one) * turned
            step = (first_turned / (1.0 - beta_one**STEP)) / (
                jnp.sqrt(second_new / (1.0 - beta_two**STEP)) + adam_eps
            )
            inner = mul(left_parts(left), right_parts(step))
            w_out[b] = w_ref[b] - block_rate * mul(left_parts(inner), right_parts(right, 1), NT)

    spec = pl.BlockSpec((group, side, side), lambda t: (t, 0, 0))
    return pl.pallas_call(
        kernel,
        grid=(count // group,),
        in_specs=[spec] * 7,
        out_specs=[spec] * 3,
        out_shape=[jax.ShapeDtypeStruct(grad.shape, wide)] * 3,
        compiler_params=pltpu.CompilerParams(vmem_limit_bytes=16 * mib),
        cost_estimate=pl.CostEstimate(
            flops=count * 24 * side**3, bytes_accessed=40 * count * side**2, transcendentals=0
        ),
        name="optimize",
    )(grad, rotated_old, master, first, second, left_basis, right_basis)


def head_mask(head):
    lane = lax.broadcasted_iota(jnp.int32, (1, 2 * HD), 1)
    return ((lane // HD) == head).astype(low)


def attention_tile(qkv, w_out, table, seg_row, tile, came=None):
    width = qkv.shape[1] // 3
    pairs = width // (2 * HD)
    rows = qkv.shape[0]
    span = slice(tile * TILE, (tile + 1) * TILE)

    def kernel(qkv_ref, w_ref, sk_ref, sq_ref, *refs):
        ctx_ref, lse_ref, part_ref = refs[-3:]
        same = sk_ref[:, 3:4] == sq_ref[:, span]
        for pair in range(pairs):
            place = pair * 2 * HD
            lanes = slice(place, place + 2 * HD)
            q = qkv_ref[span, lanes] * jnp.asarray(HD**-0.5, low)
            k = qkv_ref[:, width + place : width + place + 2 * HD]
            v_t = qkv_ref[:, 2 * width + place : 2 * width + place + 2 * HD].T
            parts = []
            for head in range(2):
                s = jnp.where(same, mul(k, q * head_mask(head), NT), -1e30)
                peak = jnp.max(s, axis=0, keepdims=True)
                e = jnp.exp(s - peak)
                total = jnp.sum(e, axis=0, keepdims=True)
                part = mul(v_t[head * HD : (head + 1) * HD], e.astype(low))
                parts.append(part * (1.0 / total))
                lse_ref[pair * 2 + head : pair * 2 + head + 1, :] = peak + jnp.log(total)
            ctx_ref[:, lanes] = jnp.concatenate(parts, axis=0).T.astype(low)
        part = mul(ctx_ref[...], w_ref[...])
        if came is not None:
            part = part + refs[0][...].astype(wide)
        part_ref[...] = part.astype(low)

    operands = [qkv, w_out, table, seg_row] + ([] if came is None else [came])
    return vmem_call(
        kernel,
        "attention_tile",
        [shaped(low, TILE, width), shaped(wide, 2 * pairs, TILE), shaped(low, TILE, D)],
        *operands,
        flops=16 * TILE * rows * width,
        room=8,
    )


def norm_rows(place, mixed, came, residual, vectors, which, keep):
    bias_row, gain_row, shift_row = which
    rows = mixed.shape[0]

    def kernel(place_ref, a_ref, b_ref, x_ref, v_ref, low_ref, normed_ref, inverse_ref, last_ref):
        total = a_ref[...].astype(wide) + b_ref[...].astype(wide)
        z = x_ref[...].astype(wide) + total + v_ref[bias_row : bias_row + 1, :]
        center = z - jnp.mean(z, axis=1, keepdims=True)
        inverse = lax.rsqrt(jnp.mean(center * center, axis=1, keepdims=True) + norm_eps)
        normed = center * inverse
        out = v_ref[gain_row : gain_row + 1, :] * normed + v_ref[shift_row : shift_row + 1, :]
        low_ref[...] = out.astype(low)
        normed_ref[...] = normed
        inverse_ref[...] = inverse
        if keep:
            last_ref[...] = out
        else:
            first_chip = place_ref[3] == 0
            last_ref[...] = jnp.where(first_chip, out[: rows // 2], out[rows // 2 :]).astype(low)

    outs = [shaped(low, rows, D), shaped(wide, rows, D), shaped(wide, rows, 1)]
    outs += [shaped(wide, rows, D) if keep else shaped(low, rows // 2, D)]
    return vmem_call(
        kernel,
        "norm_rows",
        outs,
        place,
        mixed,
        came,
        residual,
        vectors,
        smem=1,
        flops=20 * rows * D,
    )


def norm_back(grad_rows, norm_gain, normed, inverse):
    scaled = grad_rows * norm_gain
    first_mean = jnp.mean(scaled, axis=1, keepdims=True)
    second_mean = jnp.mean(scaled * normed, axis=1, keepdims=True)
    return inverse * (scaled - first_mean - normed * second_mean)


def column_sums(grad_z, grad_rows, normed):
    return jnp.concatenate(
        [
            jnp.sum(grad_z, axis=0, keepdims=True),
            jnp.sum(grad_rows * normed, axis=0, keepdims=True),
            jnp.sum(grad_rows, axis=0, keepdims=True),
        ],
        axis=0,
    )


def feed_forward(rows_low, w_up, bias_up, w_down):
    rows, hidden = rows_low.shape[0], w_up.shape[1]

    def kernel(h_ref, up_ref, b_ref, down_ref, part_ref, hid_ref, slope_ref):
        u = mul(h_ref[...], up_ref[...]) + b_ref[...]
        hid, slope = gelu_parts(u)
        hid_ref[...] = hid
        slope_ref[...] = slope
        part_ref[...] = mul(hid, down_ref[...]).astype(part_ref.dtype)

    return vmem_call(
        kernel,
        "feed_forward",
        [shaped(low, rows, D), shaped(low, rows, hidden), shaped(wide, rows, hidden)],
        rows_low,
        w_up,
        bias_up,
        w_down,
        flops=4 * rows * D * hidden,
    )


def feed_back(grad_low, slope, w_up, w_down):
    rows, hidden = grad_low.shape[0], w_up.shape[1]

    def kernel(g_ref, slope_ref, up_ref, down_ref, part_ref, pre_ref):
        pre = (mul(g_ref[...], down_ref[...], NT) * slope_ref[...]).astype(low)
        pre_ref[...] = pre
        part_ref[...] = mul(pre, up_ref[...], NT).astype(part_ref.dtype)

    return vmem_call(
        kernel,
        "feed_back",
        [shaped(low, rows, D), shaped(low, rows, hidden)],
        grad_low,
        slope,
        w_up,
        w_down,
        flops=4 * rows * D * hidden,
    )


def link_back(place, link, table, cot_rows, out_rows, normed, inverse, vectors, pieces, queries):
    rows = out_rows[0].shape[0]
    count = len(out_rows)
    piece_rows = pieces[0].shape[0]

    def kernel(place_ref, link_ref, table_ref, cot_ref, *refs):
        outs, refs = refs[:count], refs[count:]
        norms, refs = refs[:count], refs[count:]
        scales, refs = refs[:count], refs[count:]
        v_ref, refs = refs[0], refs[1:]
        parts, refs = refs[: len(pieces)], refs[len(pieces) :]
        grads, refs = refs[:count], refs[count:]
        lows, refs = refs[:count], refs[count:]
        sums_ref, score_ref, partner = refs
        is_query = place_ref[0] == 1
        chip = place_ref[3]
        for k, part in enumerate(parts):
            turn = chip if k % 2 == 0 else 1 - chip
            start = (k // 2 * 2 + turn) * piece_rows
            partner[pl.ds(pl.multiple_of(start, piece_rows), piece_rows), :] = part[...]
        gain = v_ref[4:5, :]
        sums = jnp.zeros((3, D), wide)
        score = jnp.zeros((1, queries), wide)
        for k in range(count):
            span = slice(k * rows, (k + 1) * rows)
            linked = mul(link_ref[span, :], partner[...])
            token = jnp.sum(outs[k][...].astype(wide) * linked, axis=1, keepdims=True)
            kinds = lax.broadcasted_iota(jnp.int32, (1, queries), 1).astype(wide)
            hot = table_ref[span, 2:3] == kinds
            score = score + jnp.sum(jnp.where(hot, token, 0.0), axis=0, keepdims=True)
            scale = jnp.where(is_query, table_ref[span, 1:2], 1.0)
            start = pl.multiple_of(place_ref[2] * count * rows + k * rows, rows)
            grad_rows = cot_ref[pl.ds(start, rows), :].astype(wide) + scale * linked
            normed_k = norms[k][...]
            grad_z = norm_back(grad_rows, gain, normed_k, scales[k][...])
            grads[k][...] = grad_z
            lows[k][...] = grad_z.astype(low)
            sums = sums + column_sums(grad_z, grad_rows, normed_k)
        sums_ref[...] = sums
        score_ref[...] = jnp.where(is_query, score * D ** (-0.5), 0.0)

    return vmem_call(
        kernel,
        "link_back",
        [shaped(wide, rows, D)] * count
        + [shaped(low, rows, D)] * count
        + [shaped(wide, 3, D), shaped(wide, 1, queries)],
        place,
        link,
        table,
        cot_rows,
        *out_rows,
        *normed,
        *inverse,
        vectors,
        *pieces,
        smem=1,
        scratch=[pltpu.VMEM((ROW, D), low)],
        flops=2 * count * rows * ROW * D,
    )


def first_back(mixed, came, second_grad, normed, inverse, vectors):
    rows = mixed.shape[0]

    def kernel(a_ref, b_ref, g_ref, n_ref, i_ref, v_ref, grad_ref, low_ref, sums_ref):
        total = a_ref[...].astype(wide) + b_ref[...].astype(wide)
        grad_rows = g_ref[...] + total
        normed_k = n_ref[...]
        grad_z = norm_back(grad_rows, v_ref[2:3, :], normed_k, i_ref[...])
        grad_ref[...] = grad_z
        low_ref[...] = grad_z.astype(low)
        sums_ref[...] = column_sums(grad_z, grad_rows, normed_k)

    return vmem_call(
        kernel,
        "first_back",
        [shaped(wide, rows, D), shaped(low, rows, D), shaped(wide, 3, D)],
        mixed,
        came,
        second_grad,
        normed,
        inverse,
        vectors,
        flops=20 * rows * D,
    )


def attention_backward(qkv, w_out, table, seg_row, contexts, rows_grads, lses):
    width = qkv.shape[1] // 3
    pairs = width // (2 * HD)
    rows = qkv.shape[0]
    tiles = rows // TILE

    def kernel(qkv_ref, w_ref, sk_ref, sq_ref, *refs):
        ctx_refs, refs = refs[:tiles], refs[tiles:]
        g_refs, refs = refs[:tiles], refs[tiles:]
        lse_refs, refs = refs[:tiles], refs[tiles:]
        out_ref, wgrad_ref, bias_ref, ctx, grad_rows, ctx_grad, lse, gk, gv = refs
        for t in range(tiles):
            span = slice(t * TILE, (t + 1) * TILE)
            ctx[span, :] = ctx_refs[t][...]
            grad_rows[span, :] = g_refs[t][...]
            lse[:, span] = lse_refs[t][...]
        ctx_grad[...] = mul(grad_rows[...], w_ref[...], NT).astype(low)
        wgrad_ref[...] = mul(ctx[...], grad_rows[...], TN).astype(low)
        gk[...] = jnp.zeros_like(gk)
        gv[...] = jnp.zeros_like(gv)
        bias_ref[...] = jnp.zeros_like(bias_ref)

        def step(tile, carry):
            span = pl.ds(pl.multiple_of(tile * TILE, TILE), TILE)
            same = sk_ref[:, 3:4] == sq_ref[:, span]
            for pair in range(pairs):
                place = pair * 2 * HD
                lanes = slice(place, place + 2 * HD)
                q = qkv_ref[span, lanes] * jnp.asarray(HD**-0.5, low)
                k = qkv_ref[:, width + place : width + place + 2 * HD]
                v = qkv_ref[:, 2 * width + place : 2 * width + place + 2 * HD]
                k_t = k.T
                grad = ctx_grad[span, lanes]
                dots = (grad.astype(wide) * ctx[span, lanes].astype(wide)).T
                parts = []
                for head in range(2):
                    mask = head_mask(head)
                    row = pair * 2 + head
                    q_head = q * mask
                    grad_head = grad * mask
                    features = slice(head * HD, (head + 1) * HD)
                    delta = jnp.sum(dots[features], axis=0, keepdims=True)
                    s = jnp.where(same, mul(k, q_head, NT), -1e30)
                    p = jnp.exp(s - lse[row : row + 1, span])
                    gs = (p * (mul(v, grad_head, NT) - delta)).astype(low)
                    gv[:, lanes] += mul(p.astype(low), grad_head)
                    gk[:, lanes] += mul(gs, q_head)
                    parts.append(mul(k_t[features], gs))
                gq = (jnp.concatenate(parts, axis=0).T * HD**-0.5).astype(low)
                out_ref[span, lanes] = gq
                bias_ref[:, lanes] += jnp.sum(gq.astype(wide), axis=0, keepdims=True)
            return carry

        lax.fori_loop(0, tiles, step, 0)
        out_ref[:, width : 2 * width] = gk[...].astype(low)
        gv_low = gv[...].astype(low)
        out_ref[:, 2 * width :] = gv_low
        bias_ref[:, width:] = jnp.sum(gv_low.astype(wide), axis=0, keepdims=True)

    return vmem_call(
        kernel,
        "attention_backward",
        [shaped(low, rows, 3 * width), shaped(low, width, D), shaped(wide, 1, 2 * width)],
        qkv,
        w_out,
        table,
        seg_row,
        *contexts,
        *rows_grads,
        *lses,
        scratch=[
            pltpu.VMEM((rows, width), low),
            pltpu.VMEM((rows, D), low),
            pltpu.VMEM((rows, width), low),
            pltpu.VMEM((2 * pairs, rows), wide),
            pltpu.VMEM((rows, width), wide),
            pltpu.VMEM((rows, width), wide),
        ],
        flops=40 * rows * rows * width,
        room=10,
    )


def pack_sums(place, sums_one, sums_two, score_part):
    queries = score_part.shape[1]

    def kernel(place_ref, one_a, one_b, two_ref, score_ref, out_ref):
        one = one_a[...] + one_b[...]
        two = two_ref[...]
        out_ref[0:1, :] = one[0:1]
        out_ref[1:2, :] = two[0:1]
        out_ref[2:4, :] = one[1:3]
        out_ref[4:6, :] = two[1:3]
        lane = lax.broadcasted_iota(jnp.int32, (1, D), 1)
        first = place_ref[1] * queries
        row = jnp.zeros((1, D), wide)
        score = score_ref[...]
        for e in range(queries):
            row = jnp.where(lane == first + e, score[:, e : e + 1], row)
        out_ref[6:7, :] = row
        out_ref[7:8, :] = jnp.zeros((1, D), wide)

    return vmem_call(
        kernel, "pack_sums", [shaped(wide, 8, D)], place, *sums_one, sums_two, score_part, smem=1
    )[0]


def add_biases(shared, came, pair_bias, up_grad):
    def kernel(a_ref, b_ref, pair_ref, up_ref, out_ref):
        out_ref[0:8, :] = a_ref[...] + b_ref[...]
        zero = jnp.zeros((1, D - pair_ref.shape[1]), wide)
        out_ref[8:9, :] = jnp.concatenate([pair_ref[...], zero], axis=1)
        out_ref[9:10, :] = up_ref[...]
        out_ref[10:16, :] = jnp.zeros((6, D), wide)

    return vmem_call(
        kernel, "add_biases", [shaped(wide, 16, D)], shared, came, pair_bias, up_grad
    )[0]


def small_update(place, total, bias_state, norm_state, local_width, packs, queries):
    bias_count = bias_state.shape[1]
    hidden = bias_count - 2 * local_width
    unit = D // 2
    pieces = norm_state.shape[1] * 2 // 4

    def kernel(place_ref, g_ref, bias_ref, norm_ref, bias_out, norm_out, score_out, value_out, new):
        bias_grad = jnp.concatenate([g_ref[8:9, : 2 * local_width], g_ref[9:10, :hidden]], axis=1)
        first, second, value = adam_plain(
            bias_grad, bias_ref[1:2], bias_ref[2:3], bias_ref[0:1], small_rate
        )
        bias_out[0:1, :] = bias_grad
        bias_out[1:2, :] = first
        bias_out[2:3, :] = second
        for k in range(bias_count // unit):
            value_out[k : k + 1, :] = value[:, k * unit : (k + 1) * unit]
        norm_grad = g_ref[0:6, :]
        first, second, value = adam_plain(
            norm_grad, norm_ref[1], norm_ref[2], norm_ref[0], small_rate
        )
        norm_out[0] = norm_grad
        norm_out[1] = first
        norm_out[2] = second
        for row in range(6):
            for side in range(2):
                new[2 * row + side] = value[row : row + 1, side * unit : (side + 1) * unit]
        start = place_ref[4] * pieces
        for k in range(pieces):
            at = bias_count // unit + k
            value_out[at : at + 1, :] = new[start + k]
        for pack in range(packs):
            score_out[pack : pack + 1, :] = g_ref[6:7, pack * queries : (pack + 1) * queries]

    bias_out, norm_out, scores, values = vmem_call(
        kernel,
        "small_update",
        [
            shaped(wide, 3, bias_count),
            shaped(wide, *norm_state.shape),
            shaped(wide, packs, queries),
            shaped(wide, bias_count // unit + pieces, unit),
        ],
        place,
        total,
        bias_state,
        norm_state,
        smem=1,
        scratch=[pltpu.VMEM((12, 1, unit), wide)],
    )
    return bias_out, norm_out, scores, values


def body(
    layer_input,
    output_cot,
    score_cot,
    query_lengths,
    passage_lengths,
    pairing,
    match_offset,
    block_order,
    block_master,
    block_first,
    block_second,
    basis_left,
    basis_right,
    bias_state,
    norm_state,
):
    mp_count = lax.axis_size("mp")
    dp_count = lax.axis_size("dp")
    dp_index = lax.axis_index("dp")
    mp_index = lax.axis_index("mp")
    core, chip = mp_index % 2, mp_index // 2
    half_dp = dp_count // 2
    is_query = dp_index < half_dp
    table_row = dp_index % half_dp
    side = block_master.shape[1]
    owned = block_master.shape[0]
    local_width = H // mp_count * HD
    hidden_local = FF // mp_count
    shapes_list = [(D, 3 * local_width), (local_width, D), (D, hidden_local), (hidden_local, D)]
    half, quarter = ROW // 2, ROW // 4

    core_pairs = [(s, s ^ 1) for s in range(mp_count)]
    chip_pairs = [(s, s ^ 2) for s in range(mp_count)]

    def core_swap(value):
        return lax.ppermute(value, "mp", core_pairs)

    def chip_swap(value):
        return lax.ppermute(value, "mp", chip_pairs)

    ring = ring_order(dp_count)
    ahead = [(ring[k], ring[(k + 1) % dp_count]) for k in range(dp_count)]
    routes = [ahead, [(b, a) for a, b in ahead]]
    bounds = piece_bounds(owned)
    piece_count = len(bounds) - 1
    order_list = block_order[0]
    ring_place = jnp.where(dp_index % 2 == 0, dp_index // 2, dp_count - 1 - dp_index // 2)
    place = jnp.stack(
        [is_query.astype(jnp.int32), table_row, core, chip, mp_index, ring_place]
    )
    link, seg_column, seg_row = pair_tables(
        place, query_lengths, passage_lengths, pairing, score_cot, match_offset
    )

    bias_now = bias_state[0]
    bias_query = bias_now[:local_width]
    bias_value = bias_now[local_width : 2 * local_width]
    bias_up = bias_now[2 * local_width :]
    qkv_bias = jnp.concatenate([bias_query, jnp.zeros_like(bias_query), bias_value])
    vectors = norm_state[0]

    x_rows = in_order(
        place, [layer_input[:half]], [layer_input[half:]]
    )

    master_low = block_master.astype(low)
    arrived = [[master_low[bounds[k] : bounds[k + 1]]] for k in range(piece_count)]
    for step in range(dp_count - 1):
        for k in range(piece_count):
            arrived[k].append(lax.ppermute(arrived[k][-1], "dp", routes[k % 2]))
        if step == 1:
            held = (arrived[0][-1], link, seg_column, seg_row, x_rows, qkv_bias)
            arrived[0][-1], link, seg_column, seg_row, x_rows, qkv_bias = (
                lax.optimization_barrier(held)
            )
    w_qkv, w_out, w_up, w_down = assemble(
        place,
        order_list,
        [piece for k in range(piece_count) for piece in arrived[k]],
        shapes_list,
        side,
        dp_count,
        owned,
        bounds,
    )

    x_mine = x_rows[:half]
    qkv = (mul(x_rows, w_qkv) + qkv_bias).astype(low)
    tiles = ROW // TILE
    half_tiles = tiles // 2

    def cut(value, k):
        return value[k * quarter : (k + 1) * quarter]

    context, lse, mixed = [None] * tiles, [None] * tiles, [None] * half_tiles
    sent = []
    for k in range(half_tiles):
        t = half_tiles + k
        context[t], lse[t], part = attention_tile(qkv, w_out, seg_column, seg_row, t)
        sent.append(core_swap(part))
    for k in range(half_tiles):
        context[k], lse[k], mixed[k] = attention_tile(
            qkv, w_out, seg_column, seg_row, k, sent[k]
        )
    came = [chip_swap(value) for value in mixed]
    normed_one, inverse_one, first_mine, first_other, first_norm = [], [], [], [], []
    for k in range(2):
        rows_low, normed_k, inverse_k, rows_wide = norm_rows(
            place, mixed[k], came[k], cut(x_mine, k), vectors, (0, 2, 3), True
        )
        first_mine.append(rows_low)
        normed_one.append(normed_k)
        inverse_one.append(inverse_k)
        first_norm.append(rows_wide)
        first_other.append(core_swap(rows_low))

    def mix(mine_part, other_part):
        return (mine_part.astype(wide) + core_swap(other_part).astype(wide)).astype(low)

    hid_mine, hid_other, slope_mine, slope_other, mixed = [], [], [], [], []
    up_row = bias_up[None, :]
    for k in range(2):
        mine_part, hid, slope = feed_forward(first_mine[k], w_up, up_row, w_down)
        hid_mine.append(hid)
        slope_mine.append(slope)
        other_part, hid, slope = feed_forward(first_other[k], w_up, up_row, w_down)
        hid_other.append(hid)
        slope_other.append(slope)
        mixed.append(mix(mine_part, other_part))
    came = [chip_swap(value) for value in mixed]
    normed_two, inverse_two, out_mine, out_other, pieces = [], [], [], [], []
    exchange = [(s, s ^ half_dp) for s in range(dp_count)]
    for k in range(2):
        out_k, normed_k, inverse_k, out_piece = norm_rows(
            place, mixed[k], came[k], first_norm[k], vectors, (1, 4, 5), False
        )
        normed_two.append(normed_k)
        inverse_two.append(inverse_k)
        out_mine.append(out_k)
        out_other.append(core_swap(out_k))
        mine = lax.ppermute(out_piece, "dp", exchange)
        pieces += [mine, chip_swap(mine)]

    output_part = in_order(place, out_mine, out_other)
    pieces = pieces + [core_swap(value) for value in pieces]
    linked = link_back(
        place,
        link,
        seg_column,
        output_cot,
        out_mine,
        normed_two,
        inverse_two,
        vectors,
        pieces,
        score_cot.shape[1],
    )
    second_grad, second_mine = list(linked[:2]), list(linked[2:4])
    sums_two, score_part = linked[4], linked[5]
    second_other = [core_swap(value) for value in second_mine]
    pre_mine, pre_other, mixed = [], [], []
    for k in range(2):
        mine_part, pre = feed_back(second_mine[k], slope_mine[k], w_up, w_down)
        pre_mine.append(pre)
        other_part, pre = feed_back(second_other[k], slope_other[k], w_up, w_down)
        pre_other.append(pre)
        mixed.append(mix(mine_part, other_part))
    came = [chip_swap(value) for value in mixed]
    grad_down, grad_up, up_grad = feed_grads(
        hid_mine + hid_other,
        second_mine + second_other,
        first_mine + first_other,
        pre_mine + pre_other,
    )

    rotated_old = rotate_first(block_first, basis_left, basis_right)
    ready = (vectors, grad_down, grad_up, up_grad, rotated_old, output_part)
    late_vectors, grad_down, grad_up, up_grad, rotated_old, output_part = (
        lax.optimization_barrier(ready)
    )

    first_grad, attn_mine, attn_other, sums_one = [], [], [], []
    for k in range(2):
        grad_k, low_k, sums_k = first_back(
            mixed[k], came[k], second_grad[k], normed_one[k], inverse_one[k], late_vectors
        )
        first_grad.append(grad_k)
        attn_mine.append(low_k)
        attn_other.append(core_swap(low_k))
        sums_one.append(sums_k)
    shared = pack_sums(place, sums_one, sums_two, score_part)
    shared_came = core_swap(shared)
    qkv_grad, grad_out, pair_bias = attention_backward(
        qkv, w_out, seg_column, seg_row, context, attn_mine + attn_other, lse
    )
    grad_qkv = mul(x_rows, qkv_grad, TN).astype(low)
    input_mine, input_other = [], []
    for k in range(2):
        other_part = mul(cut(qkv_grad, 2 + k), w_qkv, NT).astype(low)
        mixed_k = mix(mul(cut(qkv_grad, k), w_qkv, NT), other_part)
        branch_zero = mixed_k.astype(wide) + chip_swap(mixed_k).astype(wide)
        input_mine.append((first_grad[k] + branch_zero).astype(low))
        input_other.append(core_swap(input_mine[k]))
    input_grad = in_order(place, input_mine, input_other)

    small = add_biases(shared, shared_came, pair_bias, up_grad)
    stride = 1
    while stride < dp_count:
        small = small + lax.ppermute(small, "dp", [(s, s ^ stride) for s in range(dp_count)])
        stride *= 2
    bias_out, norm_out, scores, small_values = small_update(
        place, small, bias_state, norm_state, local_width, *score_cot.shape
    )

    staged = spread(
        place,
        order_list,
        [grad_qkv, grad_out, grad_up, grad_down],
        side,
        dp_count,
        owned,
        bounds,
    )
    travelling = [staged[k * dp_count] for k in range(piece_count)]
    for step in range(dp_count - 1):
        for k in range(piece_count):
            came = lax.ppermute(travelling[k], "dp", routes[k % 2])
            summed = came.astype(wide) + staged[k * dp_count + step + 1].astype(wide)
            travelling[k] = summed.astype(low) if step < dp_count - 2 else summed
    owned_grad = jnp.concatenate(travelling, axis=0)

    owned_grad, input_grad = lax.optimization_barrier((owned_grad, input_grad))
    first_new, second_new, master_new = optimize(
        owned_grad, rotated_old, block_master, block_first, block_second, basis_left, basis_right
    )
    small_values, master_new = lax.optimization_barrier((small_values, master_new))
    small_values = small_values.reshape(-1)
    return (
        output_part,
        scores,
        input_grad,
        owned_grad,
        first_new,
        second_new,
        master_new,
        bias_out,
        norm_out,
        small_values,
    )


def solution(mesh):
    blocks = P(("dp", "mp"), None, None)
    rows = P("dp", None)
    return jax.shard_map(
        body,
        mesh=mesh,
        in_specs=(rows, rows, P(), P(), P(), P(), P(), P("mp", None))
        + (blocks,) * 5
        + (P(None, "mp"), P()),
        out_specs=(rows, P(), rows) + (blocks,) * 4 + (P(None, "mp"), P(), P("mp")),
        check_vma=False,
    )
```

profile of v0, /device:TPU:0, one launch (start us, length us, event | category | flops | bytes accessed | tf_op | source)
XLA Modules:
  0.0 319.8 jit_solution(577361005815855496)
XLA Ops:
  2.4 3.1 collective-permute-start
  7.7 3.5 %collective-permute-done.refs_1_ = bf16[6,128,128]{2,1,0:T(8,128)(2,1)S(1)} collective-permute-done((bf16[6,128,128]{2,1,0:T(8,128)(2,1)S(1)}, bf16[6,128,128]{2,1,0:T(8,128)(2,1)S(1)}, u32[]{:S(2)}, u32[]{:S(2)}) %collective-permute-start) | collective-permute-done | bytes 196640 | tf_op jit(solution)/shard_map/ppermute | solution.py:830
  66.6 3.2 assemble.1
  71.6 3.3 %attention_tile.6 = (bf16[256,256]{1,0:T(8,128)(2,1)S(1)}, f32[4,256]{1,0:T(4,128)S(1)}, bf16[256,1024]{1,0:T(8,128)(2,1)S(1)}) custom-call(bf16[1024,768]{1,0:T(8,128)(2,1)S(1)} %add_convert_fusion.qkv_ref, bf16[256,1024]{1,0:T(8,128)(2,1)S(1)} %get-tuple-element.145.w_ref, f32[1024,8]{1,0:T(8,128)S(1)} %get-tuple-element.146.sk_ref.table_ref, ...), custom_call_target="tpu_custom_call" | custom-call | flops 1073741824 | bytes 2793472 | tf_op jit(solution)/shard_map/attention_tile/pallas_call | solution.py:72
  75.0 3.3 %attention_tile.4 = (bf16[256,256]{1,0:T(8,128)(2,1)S(1)}, f32[4,256]{1,0:T(4,128)S(1)}, bf16[256,1024]{1,0:T(8,128)(2,1)S(1)}) custom-call(bf16[1024,768]{1,0:T(8,128)(2,1)S(1)} %add_convert_fusion.qkv_ref, bf16[256,1024]{1,0:T(8,128)(2,1)S(1)} %get-tuple-element.145.w_ref, f32[1024,8]{1,0:T(8,128)S(1)} %get-tuple-element.146.sk_ref.table_ref, ...), custom_call_target="tpu_custom_call" | custom-call | flops 1073741824 | bytes 2793472 | tf_op jit(solution)/shard_map/attention_tile/pallas_call | solution.py:72
  78.8 3.3 %attention_tile.7 = (bf16[256,256]{1,0:T(8,128)(2,1)S(1)}, f32[4,256]{1,0:T(4,128)S(1)}, bf16[256,1024]{1,0:T(8,128)(2,1)S(1)}) custom-call(bf16[1024,768]{1,0:T(8,128)(2,1)S(1)} %add_convert_fusion.qkv_ref, bf16[256,1024]{1,0:T(8,128)(2,1)S(1)} %get-tuple-element.145.w_ref, f32[1024,8]{1,0:T(8,128)S(1)} %get-tuple-element.146.sk_ref.table_ref, ...), custom_call_target="tpu_custom_call" | custom-call | flops 1073741824 | bytes 3317760 | tf_op jit(solution)/shard_map/attention_tile/pallas_call | solution.py:72
  83.6 3.7 %attention_tile.5 = (bf16[256,256]{1,0:T(8,128)(2,1)S(1)}, f32[4,256]{1,0:T(4,128)S(1)}, bf16[256,1024]{1,0:T(8,128)(2,1)S(1)}) custom-call(bf16[1024,768]{1,0:T(8,128)(2,1)S(1)} %add_convert_fusion.qkv_ref, bf16[256,1024]{1,0:T(8,128)(2,1)S(1)} %get-tuple-element.145.w_ref, f32[1024,8]{1,0:T(8,128)S(1)} %get-tuple-element.146.sk_ref.table_ref, ...), custom_call_target="tpu_custom_call" | custom-call | flops 1073741824 | bytes 3317760 | tf_op jit(solution)/shard_map/attention_tile/pallas_call | solution.py:72
  88.0 8.9 %collective-permute-done.31.b_ref = bf16[256,1024]{1,0:T(8,128)(2,1)S(1)} collective-permute-done((bf16[256,1024]{1,0:T(8,128)(2,1)S(1)}, bf16[256,1024]{1,0:T(8,128)(2,1)S(1)}, u32[]{:S(2)}, u32[]{:S(2)}) %collective-permute-start.31) | collective-permute-done | bytes 524320 | tf_op jit(solution)/shard_map/ppermute | solution.py:799
  98.1 9.1 %collective-permute-done.29.b_ref = bf16[256,1024]{1,0:T(8,128)(2,1)S(1)} collective-permute-done((bf16[256,1024]{1,0:T(8,128)(2,1)S(1)}, bf16[256,1024]{1,0:T(8,128)(2,1)S(1)}, u32[]{:S(2)}, u32[]{:S(2)}) %collective-permute-start.29) | collective-permute-done | bytes 524320 | tf_op jit(solution)/shard_map/ppermute | solution.py:799
  117.9 12.4 %collective-permute-done.37.b_ref = bf16[256,1024]{1,0:T(8,128)(2,1)S(1)} collective-permute-done((bf16[256,1024]{1,0:T(8,128)(2,1)S(1)}, bf16[256,1024]{1,0:T(8,128)(2,1)S(1)}, u32[]{:S(2)}, u32[]{:S(2)}) %collective-permute-start.37) | collective-permute-done | bytes 524320 | tf_op jit(solution)/shard_map/ppermute | solution.py:799
  131.4 2.7 collective-permute-start.40
  134.0 7.1 %collective-permute-done.35.b_ref = bf16[256,1024]{1,0:T(8,128)(2,1)S(1)} collective-permute-done((bf16[256,1024]{1,0:T(8,128)(2,1)S(1)}, bf16[256,1024]{1,0:T(8,128)(2,1)S(1)}, u32[]{:S(2)}, u32[]{:S(2)}) %collective-permute-start.35) | collective-permute-done | bytes 524320 | tf_op jit(solution)/shard_map/ppermute | solution.py:799
  142.2 2.7 collective-permute-start.38
  147.0 9.7 %collective-permute-done.38.refs_7_ = bf16[128,1024]{1,0:T(8,128)(2,1)S(1)} collective-permute-done((bf16[128,1024]{1,0:T(8,128)(2,1)S(1)}, bf16[128,1024]{1,0:T(8,128)(2,1)S(1)}, u32[]{:S(2)}, u32[]{:S(2)}) %collective-permute-start.38) | collective-permute-done | bytes 262176 | tf_op jit(solution)/shard_map/ppermute | solution.py:901
  158.7 5.2 %collective-permute-done.39.refs_8_ = bf16[128,1024]{1,0:T(8,128)(2,1)S(1)} collective-permute-done((bf16[128,1024]{1,0:T(8,128)(2,1)S(1)}, bf16[128,1024]{1,0:T(8,128)(2,1)S(1)}, u32[]{:S(2)}, u32[]{:S(2)}) %collective-permute-start.39) | collective-permute-done | bytes 262176 | tf_op jit(solution)/shard_map/ppermute | solution.py:799
  165.4 3.3 %link_back.1 = (f32[256,1024]{1,0:T(8,128)S(1)}, f32[256,1024]{1,0:T(8,128)S(1)}, bf16[256,1024]{1,0:T(8,128)(2,1)S(1)}, bf16[256,1024]{1,0:T(8,128)(2,1)S(1)}, ...) custom-call(s32[6]{0:T(128)S(1)} %stack.31.place_ref, bf16[512,1024]{1,0:T(8,128)(2,1)S(1)} %get-tuple-element.160.link_ref, ...), custom_call_target="tpu_custom_call" | custom-call | flops 1073741824 | bytes 11606104 | tf_op jit(solution)/shard_map/link_back/pallas_call | solution.py:72
  179.8 4.9 %rotate_first.1.c_ref = f32[24,128,128]{2,1,0:T(8,128)S(1)} custom-call(f32[24,128,128]{2,1,0:T(8,128)S(1)} %copy-done.2, f32[24,128,128]{2,1,0:T(8,128)S(1)} %copy-done.3, f32[24,128,128]{2,1,0:T(8,128)S(1)} %copy-done.4), custom_call_target="tpu_custom_call" | custom-call | flops 603979776 | bytes 6291456 | tf_op jit(solution)/shard_map/rotate_first/pallas_call | solution.py:309
  186.7 4.5 %feed_grads.1 = (bf16[1024,1024]{1,0:T(8,128)(2,1)S(1)}, bf16[1024,1024]{1,0:T(8,128)(2,1)S(1)}, f32[1,1024]{1,0:T(1,128)S(1)}) custom-call(bf16[256,1024]{1,0:T(8,128)(2,1)S(1)} %get-tuple-element.153.refs_0_, bf16[256,1024]{1,0:T(8,128)(2,1)S(1)} %get-tuple-element.157.refs_1_, bf16[256,1024]{1,0:T(8,128)(2,1)S(1)} %get-tuple-element.158.refs_2_, ...), custom_call_target="tpu_custom_call" | custom-call | flops 4294967296 | bytes 12587008 | tf_op jit(solution)/shard_map/feed_grads/pallas_call | solution.py:72
  193.1 9.6 %collective-permute-done.51.b_ref = bf16[256,1024]{1,0:T(8,128)(2,1)S(1)} collective-permute-done((bf16[256,1024]{1,0:T(8,128)(2,1)S(1)}, bf16[256,1024]{1,0:T(8,128)(2,1)S(1)}, u32[]{:S(2)}, u32[]{:S(2)}) %collective-permute-start.51) | collective-permute-done | bytes 524320 | tf_op jit(solution)/shard_map/ppermute | solution.py:799
  205.4 13.3 %attention_backward.1 = (bf16[1024,768]{1,0:T(8,128)(2,1)S(1)}, bf16[256,1024]{1,0:T(8,128)(2,1)S(1)}, f32[1,512]{1,0:T(1,128)S(1)}) custom-call(bf16[1024,768]{1,0:T(8,128)(2,1)S(1)} %add_convert_fusion.qkv_ref, bf16[256,1024]{1,0:T(8,128)(2,1)S(1)} %get-tuple-element.145.w_ref, f32[1024,8]{1,0:T(8,128)S(1)} %get-tuple-element.146.sk_ref.table_ref, ...), custom_call_target="tpu_custom_call" | custom-call | flops 10737418240 | bytes 6871040 | tf_op jit(solution)/shard_map/attention_backward/pallas_call | solution.py:72
  228.0 3.2 collective-permute-start.59
  234.2 4.5 %collective-permute-start.74 = (bf16[6,128,128]{2,1,0:T(8,128)(2,1)S(1)}, bf16[6,128,128]{2,1,0:T(8,128)(2,1)S(1)}, u32[]{:S(2)}, u32[]{:S(2)}) collective-permute-start(bf16[6,128,128]{2,1,0:T(8,128)(2,1)S(1)} %get-tuple-element.237), channel_id=1, source_target_pairs={{0,8},{8,16},{16,24},{24,28},{28,20},{20,12},{12,4},{4,0},{1,9},{9... | collective-permute-start | bytes 589832 | tf_op jit(solution)/shard_map/ppermute | solution.py:987
  242.8 3.3 %collective-permute-start.68 = (bf16[6,128,128]{2,1,0:T(8,128)(2,1)S(1)}, bf16[6,128,128]{2,1,0:T(8,128)(2,1)S(1)}, u32[]{:S(2)}, u32[]{:S(2)}) collective-permute-start(bf16[6,128,128]{2,1,0:T(8,128)(2,1)S(1)} %add_convert_fusion.24), channel_id=1, source_target_pairs={{8,0},{16,8},{24,16},{28,24},{20,28},{12,20},{4,12},{0,4},{9,1},{1... | collective-permute-start | bytes 589832 | tf_op jit(solution)/shard_map/ppermute | solution.py:987
  305.8 13.2 %optimize.1 = (f32[24,128,128]{2,1,0:T(8,128)}, f32[24,128,128]{2,1,0:T(8,128)}, f32[24,128,128]{2,1,0:T(8,128)}) custom-call(f32[24,128,128]{2,1,0:T(8,128)S(1)} %pad_maximum_fusion.g_ref, f32[24,128,128]{2,1,0:T(8,128)S(1)} %rotate_first.1.c_ref, f32[24,128,128]{2,1,0:T(8,128)S(1)} %copy-done, f32[24,128,128]{2,1,0:T(8,128)S(1)} %copy-done.2, ...), custom_call_target="tpu_custom_call" | custom-call | flops 1207959552 | bytes 15728640 | tf_op jit(solution)/shard_map/optimize/pallas_call | solution.py:344
  (283 shorter events, 177.3 us)
Async XLA Ops:
  5.5 9.9 %collective-permute-start.14 = (bf16[6,128,128]{2,1,0:T(8,128)(2,1)S(1)}, bf16[6,128,128]{2,1,0:T(8,128)(2,1)S(1)}, u32[]{:S(2)}, u32[]{:S(2)}) collective-permute-start(bf16[6,128,128]{2,1,0:T(8,128)(2,1)S(1)} %get-tuple-element.271.refs_16_), channel_id=1, source_target_pairs={{0,8},{8,16},{16,24},{24,28},{28,20},{20,12},{12,4},{4,0},{1,9},{9... | collective-permute-start | bytes 589832 | tf_op jit(solution)/shard_map/ppermute | solution.py:830
  7.5 10.1 %collective-permute-start.21 = (bf16[6,128,128]{2,1,0:T(8,128)(2,1)S(1)}, bf16[6,128,128]{2,1,0:T(8,128)(2,1)}, u32[]{:S(2)}, u32[]{:S(2)}) collective-permute-start(bf16[6,128,128]{2,1,0:T(8,128)(2,1)S(1)} %get-tuple-element.270.refs_24_), channel_id=1, source_target_pairs={{8,0},{16,8},{24,16},{28,24},{20,28},{12,20},{4,12},{0,4},{9,1},{1... | collective-permute-start | bytes 589832 | tf_op jit(solution)/shard_map/ppermute | solution.py:830
  82.1 14.8 %collective-permute-start.31 = (bf16[256,1024]{1,0:T(8,128)(2,1)S(1)}, bf16[256,1024]{1,0:T(8,128)(2,1)S(1)}, u32[]{:S(2)}, u32[]{:S(2)}) collective-permute-start(bf16[256,1024]{1,0:T(8,128)(2,1)S(1)} %get-tuple-element.155.a_ref), channel_id=1, source_target_pairs={{0,2},{1,3},{2,0},{3,1},{4,6},{5,7},{6,4},{7,5},{8,10},{9,11},{10,... | collective-permute-start | bytes 1572872 | tf_op jit(solution)/shard_map/ppermute | solution.py:799
  87.3 19.9 %collective-permute-start.29 = (bf16[256,1024]{1,0:T(8,128)(2,1)S(1)}, bf16[256,1024]{1,0:T(8,128)(2,1)S(1)}, u32[]{:S(2)}, u32[]{:S(2)}) collective-permute-start(bf16[256,1024]{1,0:T(8,128)(2,1)S(1)} %get-tuple-element.149.a_ref), channel_id=1, source_target_pairs={{0,2},{1,3},{2,0},{3,1},{4,6},{5,7},{6,4},{7,5},{8,10},{9,11},{10,... | collective-permute-start | bytes 1572872 | tf_op jit(solution)/shard_map/ppermute | solution.py:799
  98.0 10.4 %collective-permute-start.33 = (bf16[256,1024]{1,0:T(8,128)(2,1)S(1)}, bf16[256,1024]{1,0:T(8,128)(2,1)S(1)}, u32[]{:S(2)}, u32[]{:S(2)}) collective-permute-start(bf16[256,1024]{1,0:T(8,128)(2,1)S(1)} %get-tuple-element.156.h_ref.refs_9_), channel_id=1, source_target_pairs={{0,1},{1,0},{2,3},{3,2},{4,5},{5,4},{6,7},{7,6},{8,9},{9,8},{10,11... | collective-permute-start | bytes 1572872 | tf_op jit(solution)/shard_map/ppermute | solution.py:796
  115.5 14.8 %collective-permute-start.37 = (bf16[256,1024]{1,0:T(8,128)(2,1)S(1)}, bf16[256,1024]{1,0:T(8,128)(2,1)S(1)}, u32[]{:S(2)}, u32[]{:S(2)}) collective-permute-start(bf16[256,1024]{1,0:T(8,128)(2,1)S(1)} %add_convert_fusion.5.a_ref), channel_id=1, source_target_pairs={{0,2},{1,3},{2,0},{3,1},{4,6},{5,7},{6,4},{7,5},{8,10},{9,11},{10,... | collective-permute-start | bytes 1572872 | tf_op jit(solution)/shard_map/ppermute | solution.py:799
  117.3 23.9 %collective-permute-start.35 = (bf16[256,1024]{1,0:T(8,128)(2,1)S(1)}, bf16[256,1024]{1,0:T(8,128)(2,1)S(1)}, u32[]{:S(2)}, u32[]{:S(2)}) collective-permute-start(bf16[256,1024]{1,0:T(8,128)(2,1)S(1)} %add_convert_fusion.6.a_ref), channel_id=1, source_target_pairs={{0,2},{1,3},{2,0},{3,1},{4,6},{5,7},{6,4},{7,5},{8,10},{9,11},{10,... | collective-permute-start | bytes 1572872 | tf_op jit(solution)/shard_map/ppermute | solution.py:799
  131.4 14.1 %collective-permute-start.40 = (bf16[128,1024]{1,0:T(8,128)(2,1)S(1)}, bf16[128,1024]{1,0:T(8,128)(2,1)S(1)}, u32[]{:S(2)}, u32[]{:S(2)}) collective-permute-start(bf16[128,1024]{1,0:T(8,128)(2,1)S(1)} %get-tuple-element.174), channel_id=1, source_target_pairs={{0,16},{4,20},{8,24},{12,28},{16,0},{20,4},{24,8},{28,12},{1,17},{... | collective-permute-start | bytes 786440 | tf_op jit(solution)/shard_map/ppermute | solution.py:901
  142.2 14.5 %collective-permute-start.38 = (bf16[128,1024]{1,0:T(8,128)(2,1)S(1)}, bf16[128,1024]{1,0:T(8,128)(2,1)S(1)}, u32[]{:S(2)}, u32[]{:S(2)}) collective-permute-start(bf16[128,1024]{1,0:T(8,128)(2,1)S(1)} %get-tuple-element.173), channel_id=1, source_target_pairs={{0,16},{4,20},{8,24},{12,28},{16,0},{20,4},{24,8},{28,12},{1,17},{... | collective-permute-start | bytes 786440 | tf_op jit(solution)/shard_map/ppermute | solution.py:901
  145.5 13.2 %collective-permute-start.41 = (bf16[128,1024]{1,0:T(8,128)(2,1)S(1)}, bf16[128,1024]{1,0:T(8,128)(2,1)S(1)}, u32[]{:S(2)}, u32[]{:S(2)}) collective-permute-start(bf16[128,1024]{1,0:T(8,128)(2,1)S(1)} %collective-permute-done.40.refs_9_), channel_id=1, source_target_pairs={{0,2},{1,3},{2,0},{3,1},{4,6},{5,7},{6,4},{7,5},{8,10},{9,11},{10,... | collective-permute-start | bytes 786440 | tf_op jit(solution)/shard_map/ppermute | solution.py:799
  174.0 10.6 %collective-permute-start.49 = (bf16[256,1024]{1,0:T(8,128)(2,1)S(1)}, bf16[256,1024]{1,0:T(8,128)(2,1)S(1)}, u32[]{:S(2)}, u32[]{:S(2)}) collective-permute-start(bf16[256,1024]{1,0:T(8,128)(2,1)S(1)} %get-tuple-element.168.refs_1_), channel_id=1, source_target_pairs={{0,1},{1,0},{2,3},{3,2},{4,5},{5,4},{6,7},{7,6},{8,9},{9,8},{10,11... | collective-permute-start | bytes 1572872 | tf_op jit(solution)/shard_map/ppermute | solution.py:796
  174.1 10.5 %collective-permute-start.48 = (bf16[256,1024]{1,0:T(8,128)(2,1)S(1)}, bf16[256,1024]{1,0:T(8,128)(2,1)S(1)}, u32[]{:S(2)}, u32[]{:S(2)}) collective-permute-start(bf16[256,1024]{1,0:T(8,128)(2,1)S(1)} %get-tuple-element.164.refs_0_), channel_id=1, source_target_pairs={{0,1},{1,0},{2,3},{3,2},{4,5},{5,4},{6,7},{7,6},{8,9},{9,8},{10,11... | collective-permute-start | bytes 1572872 | tf_op jit(solution)/shard_map/ppermute | solution.py:796
  177.4 14.8 %collective-permute-start.53 = (bf16[256,1024]{1,0:T(8,128)(2,1)S(1)}, bf16[256,1024]{1,0:T(8,128)(2,1)S(1)}, u32[]{:S(2)}, u32[]{:S(2)}) collective-permute-start(bf16[256,1024]{1,0:T(8,128)(2,1)S(1)} %add_convert_fusion.3.a_ref), channel_id=1, source_target_pairs={{0,2},{1,3},{2,0},{3,1},{4,6},{5,7},{6,4},{7,5},{8,10},{9,11},{10,... | collective-permute-start | bytes 1572872 | tf_op jit(solution)/shard_map/ppermute | solution.py:799
  179.2 23.5 %collective-permute-start.51 = (bf16[256,1024]{1,0:T(8,128)(2,1)S(1)}, bf16[256,1024]{1,0:T(8,128)(2,1)S(1)}, u32[]{:S(2)}, u32[]{:S(2)}) collective-permute-start(bf16[256,1024]{1,0:T(8,128)(2,1)S(1)} %add_convert_fusion.4.a_ref), channel_id=1, source_target_pairs={{0,2},{1,3},{2,0},{3,1},{4,6},{5,7},{6,4},{7,5},{8,10},{9,11},{10,... | collective-permute-start | bytes 1572872 | tf_op jit(solution)/shard_map/ppermute | solution.py:799
  193.0 11.7 %collective-permute-start.56 = (bf16[256,1024]{1,0:T(8,128)(2,1)S(1)}, bf16[256,1024]{1,0:T(8,128)(2,1)S(1)}, u32[]{:S(2)}, u32[]{:S(2)}) collective-permute-start(bf16[256,1024]{1,0:T(8,128)(2,1)S(1)} %get-tuple-element.209.refs_5_), channel_id=1, source_target_pairs={{0,1},{1,0},{2,3},{3,2},{4,5},{5,4},{6,7},{7,6},{8,9},{9,8},{10,11... | collective-permute-start | bytes 1572872 | tf_op jit(solution)/shard_map/ppermute | solution.py:796
  204.2 14.6 %collective-permute-start.54 = (f32[8,1024]{1,0:T(8,128)S(1)}, f32[8,1024]{1,0:T(8,128)S(1)}, u32[]{:S(2)}, u32[]{:S(2)}) collective-permute-start(f32[8,1024]{1,0:T(8,128)S(1)} %pack_sums.1.a_ref), channel_id=1, source_target_pairs={{0,1},{1,0},{2,3},{3,2},{4,5},{5,4},{6,7},{7,6},{8,9},{9,8},{10,11... | collective-permute-start | bytes 98312 | tf_op jit(solution)/shard_map/ppermute | solution.py:796
  227.7 12.2 %collective-permute-start.60 = (bf16[6,128,128]{2,1,0:T(8,128)(2,1)S(1)}, bf16[6,128,128]{2,1,0:T(8,128)(2,1)S(1)}, u32[]{:S(2)}, u32[]{:S(2)}) collective-permute-start(bf16[6,128,128]{2,1,0:T(8,128)(2,1)S(1)} %get-tuple-element.221), channel_id=1, source_target_pairs={{0,8},{8,16},{16,24},{24,28},{28,20},{20,12},{12,4},{4,0},{1,9},{9... | collective-permute-start | bytes 589832 | tf_op jit(solution)/shard_map/ppermute | solution.py:987
  231.8 25.9 %collective-permute-start.90 = (bf16[256,1024]{1,0:T(8,128)(2,1)S(1)}, bf16[256,1024]{1,0:T(8,128)(2,1)S(1)}, u32[]{:S(2)}, u32[]{:S(2)}) collective-permute-start(bf16[256,1024]{1,0:T(8,128)(2,1)S(1)} %convolution_convert_fusion.1), channel_id=1, source_target_pairs={{0,1},{1,0},{2,3},{3,2},{4,5},{5,4},{6,7},{7,6},{8,9},{9,8},{10,11... | collective-permute-start | bytes 1572872 | tf_op jit(solution)/shard_map/ppermute | solution.py:796
  231.9 26.7 %collective-permute-start.88 = (bf16[256,1024]{1,0:T(8,128)(2,1)S(1)}, bf16[256,1024]{1,0:T(8,128)(2,1)S(1)}, u32[]{:S(2)}, u32[]{:S(2)}) collective-permute-start(bf16[256,1024]{1,0:T(8,128)(2,1)S(1)} %convolution_convert_fusion.2), channel_id=1, source_target_pairs={{0,1},{1,0},{2,3},{3,2},{4,5},{5,4},{6,7},{7,6},{8,9},{9,8},{10,11... | collective-permute-start | bytes 1572872 | tf_op jit(solution)/shard_map/ppermute | solution.py:796
  250.8 10.0 %collective-permute-start.62 = (bf16[6,128,128]{2,1,0:T(8,128)(2,1)S(1)}, bf16[6,128,128]{2,1,0:T(8,128)(2,1)S(1)}, u32[]{:S(2)}, u32[]{:S(2)}) collective-permute-start(bf16[6,128,128]{2,1,0:T(8,128)(2,1)S(1)} %add_convert_fusion.29), channel_id=1, source_target_pairs={{0,8},{8,16},{16,24},{24,28},{28,20},{20,12},{12,4},{4,0},{1,9},{9... | collective-permute-start | bytes 589832 | tf_op jit(solution)/shard_map/ppermute | solution.py:987
  258.6 28.8 %collective-permute-start.91 = (bf16[256,1024]{1,0:T(8,128)(2,1)S(1)}, bf16[256,1024]{1,0:T(8,128)(2,1)S(1)}, u32[]{:S(2)}, u32[]{:S(2)}) collective-permute-start(bf16[256,1024]{1,0:T(8,128)(2,1)S(1)} %fusion.1), channel_id=1, source_target_pairs={{0,2},{1,3},{2,0},{3,1},{4,6},{5,7},{6,4},{7,5},{8,10},{9,11},{10,... | collective-permute-start | bytes 1572872 | tf_op jit(solution)/shard_map/ppermute | solution.py:799
  260.8 27.2 %collective-permute-start.89 = (bf16[256,1024]{1,0:T(8,128)(2,1)S(1)}, bf16[256,1024]{1,0:T(8,128)(2,1)S(1)}, u32[]{:S(2)}, u32[]{:S(2)}) collective-permute-start(bf16[256,1024]{1,0:T(8,128)(2,1)S(1)} %fusion), channel_id=1, source_target_pairs={{0,2},{1,3},{2,0},{3,1},{4,6},{5,7},{6,4},{7,5},{8,10},{9,11},{10,... | collective-permute-start | bytes 1572872 | tf_op jit(solution)/shard_map/ppermute | solution.py:799
  288.0 14.7 %collective-permute-start.93 = (bf16[256,1024]{1,0:T(8,128)(2,1)S(1)}, bf16[256,1024]{1,0:T(8,128)(2,1)S(1)}, u32[]{:S(2)}, u32[]{:S(2)}) collective-permute-start(bf16[256,1024]{1,0:T(8,128)(2,1)S(1)} %add_convert_fusion.1.refs_1_), channel_id=1, source_target_pairs={{0,1},{1,0},{2,3},{3,2},{4,5},{5,4},{6,7},{7,6},{8,9},{9,8},{10,11... | collective-permute-start | bytes 1572872 | tf_op jit(solution)/shard_map/ppermute | solution.py:796
  288.3 14.3 %collective-permute-start.92 = (bf16[256,1024]{1,0:T(8,128)(2,1)S(1)}, bf16[256,1024]{1,0:T(8,128)(2,1)S(1)}, u32[]{:S(2)}, u32[]{:S(2)}) collective-permute-start(bf16[256,1024]{1,0:T(8,128)(2,1)S(1)} %add_convert_fusion.2.refs_0_), channel_id=1, source_target_pairs={{0,1},{1,0},{2,3},{3,2},{4,5},{5,4},{6,7},{7,6},{8,9},{9,8},{10,11... | collective-permute-start | bytes 1572872 | tf_op jit(solution)/shard_map/ppermute | solution.py:796
  (86 other events, 610.2 us)
where the time goes:
time: 324 us; the launch traced here: 320 us
  waiting for transfers between devices  129 us (40%)
  starting transfers between devices  92.6 us (29%)
  Pallas kernels  83.3 us (26%)
  matrix products  6.13 us (2%)
  other arithmetic  4.59 us (1%)
    pallas_call x29, Pallas kernels, vmem_call(): pl.pallas_call(kernel, in_specs=specs, out_specs=[vmem] * len(outs), out_...  63.8 us
    ppermute x10, waiting for transfers between devices, chip_swap(): return lax.ppermute(value, 'mp', chip_pairs)  53.3 us
    ppermute x28, starting transfers between devices, body(): came = lax.ppermute(travelling[k], 'dp', routes[k % 2])  34.8 us
    ppermute x28, waiting for transfers between devices, body(): arrived[k].append(lax.ppermute(arrived[k][-1], 'dp', routes[k % 2]))  31.6 us
    ppermute x28, starting transfers between devices, body(): arrived[k].append(lax.ppermute(arrived[k][-1], 'dp', routes[k % 2]))  29.9 us
    ppermute x28, waiting for transfers between devices, body(): came = lax.ppermute(travelling[k], 'dp', routes[k % 2])  26.8 us
    pallas_call x1, Pallas kernels, optimize(): pl.pallas_call(kernel, grid=(count // group,), in_specs=[spec] * 7, out_s...  13.2 us
    ppermute x10, starting transfers between devices, chip_swap(): return lax.ppermute(value, 'mp', chip_pairs)  11.6 us
  transfers between devices with their start and end apart: 94, of which 50 were waited for; matrix products, arithmetic and copies ran while one was open for 2% of the time, Pallas kernels for 18%

commit v1 on v0

--- a/solution.py
+++ b/solution.py
@@ -51,12 +51,16 @@
     return (first_new, second_new, value_old - rate_now * step_dir)
 
 
+def after(value, *others):
+    return lax.optimization_barrier((value,) + others)[0]
+
+
 def ring_order(count):
     return [k for k in range(count) if k % 2 == 0] + [k for k in range(count) if k % 2][::-1]
 
 
-def piece_bounds(owned):
-    pieces = 4 if owned >= 8 else min(2, owned)
+def piece_bounds(owned, pieces):
+    pieces = pieces if owned % pieces == 0 else 1
     return [owned * k // pieces for k in range(pieces + 1)]
 
 
@@ -76,7 +80,7 @@
         out_shape=outs,
         scratch_shapes=list(scratch),
         compiler_params=pltpu.CompilerParams(vmem_limit_bytes=given + held + room * mib),
-        cost_estimate=pl.CostEstimate(flops=flops, bytes_accessed=moved, transcendentals=0),
+        cost_estimate=pl.CostEstimate(flops=0, bytes_accessed=1024, transcendentals=0),
         name=name,
     )(*args)
 
@@ -155,6 +159,13 @@
         smem=2,
         scratch=[pltpu.VMEM((count * owned, side, side), low)],
     )
+
+
+def add_low(left, right):
+    def kernel(a_ref, b_ref, out_ref):
+        out_ref[...] = (a_ref[...].astype(wide) + b_ref[...].astype(wide)).astype(low)
+
+    return vmem_call(kernel, "add_low", [shaped(low, *left.shape)], left, right)[0]
 
 
 def in_order(place, mine, other):
@@ -298,12 +309,13 @@
 
 def rotate_first(blocks, left_basis, right_basis):
     count, side = blocks.shape[0], blocks.shape[1]
-    group = 6 if count % 6 == 0 else 3 if count % 3 == 0 else 1
+    group = count // (4 if count % 4 == 0 else 1)
 
     def kernel(m_ref, l_ref, r_ref, out_ref):
-        for b in range(group):
-            inner = mul(left_parts(l_ref[b].T), right_parts(m_ref[b]))
-            out_ref[b] = mul(left_parts(inner), right_parts(r_ref[b]))
+        every = range(group)
+        inner = [mul(left_parts(l_ref[b].T), right_parts(m_ref[b])) for b in every]
+        for b in every:
+            out_ref[b] = mul(left_parts(inner[b]), right_parts(r_ref[b]))
 
     spec = pl.BlockSpec((group, side, side), lambda t: (t, 0, 0))
     return pl.pallas_call(
@@ -314,45 +326,60 @@
         out_shape=jax.ShapeDtypeStruct(blocks.shape, wide),
         compiler_params=pltpu.CompilerParams(vmem_limit_bytes=16 * mib),
         cost_estimate=pl.CostEstimate(
-            flops=count * 12 * side**3, bytes_accessed=16 * count * side**2, transcendentals=0
+            flops=0, bytes_accessed=1024, transcendentals=0
         ),
         name="rotate_first",
     )(blocks, left_basis, right_basis)
 
 
-def optimize(grad, rotated_old, master, first, second, left_basis, right_basis):
-    count, side = grad.shape[0], grad.shape[1]
-    group = 6 if count % 6 == 0 else 3 if count % 3 == 0 else 1
-
-    def kernel(g_ref, c_ref, w_ref, m_ref, v_ref, l_ref, r_ref, m_out, v_out, w_out):
-        for b in range(group):
-            grad_now = g_ref[b]
-            m_out[b] = beta_one * m_ref[b] + (1.0 - beta_one) * grad_now
-            left, right = l_ref[b], r_ref[b]
-            inner = mul(left_parts(left.T), right_parts(grad_now))
-            turned = mul(left_parts(inner), right_parts(right))
-            second_new = beta_two * v_ref[b] + (1.0 - beta_two) * turned * turned
+def optimize(came, local, rotated_old, master, first, second, left_basis, right_basis):
+    count, side = master.shape[0], master.shape[1]
+    pieces = len(came)
+    group = count // pieces
+
+    def kernel(*refs):
+        came_refs, refs = refs[:pieces], refs[pieces:]
+        local_refs, refs = refs[:pieces], refs[pieces:]
+        c_ref, w_ref, m_ref, v_ref, l_ref, r_ref, g_out, m_out, v_out, w_out = refs
+        for k in range(pieces):
+
+            @pl.when(pl.program_id(0) == k)
+            def _():
+                g_out[...] = came_refs[k][...].astype(wide) + local_refs[k][...].astype(wide)
+
+        every = range(group)
+        for b in every:
+            m_out[b] = beta_one * m_ref[b] + (1.0 - beta_one) * g_out[b]
+        inner = [mul(left_parts(l_ref[b].T), right_parts(g_out[b])) for b in every]
+        turned = [mul(left_parts(inner[b]), right_parts(r_ref[b])) for b in every]
+        steps = []
+        for b in every:
+            second_new = beta_two * v_ref[b] + (1.0 - beta_two) * turned[b] * turned[b]
             v_out[b] = second_new
-            first_turned = beta_one * c_ref[b] + (1.0 - beta_one) * turned
-            step = (first_turned / (1.0 - beta_one**STEP)) / (
-                jnp.sqrt(second_new / (1.0 - beta_two**STEP)) + adam_eps
+            first_turned = beta_one * c_ref[b] + (1.0 - beta_one) * turned[b]
+            steps.append(
+                (first_turned / (1.0 - beta_one**STEP))
+                / (jnp.sqrt(second_new / (1.0 - beta_two**STEP)) + adam_eps)
             )
-            inner = mul(left_parts(left), right_parts(step))
-            w_out[b] = w_ref[b] - block_rate * mul(left_parts(inner), right_parts(right, 1), NT)
+        inner = [mul(left_parts(l_ref[b]), right_parts(steps[b])) for b in every]
+        for b in every:
+            back = mul(left_parts(inner[b]), right_parts(r_ref[b], 1), NT)
+            w_out[b] = w_ref[b] - block_rate * back
 
     spec = pl.BlockSpec((group, side, side), lambda t: (t, 0, 0))
+    vmem = pl.BlockSpec(memory_space=pltpu.VMEM)
     return pl.pallas_call(
         kernel,
-        grid=(count // group,),
-        in_specs=[spec] * 7,
-        out_specs=[spec] * 3,
-        out_shape=[jax.ShapeDtypeStruct(grad.shape, wide)] * 3,
-        compiler_params=pltpu.CompilerParams(vmem_limit_bytes=16 * mib),
+        grid=(pieces,),
+        in_specs=[vmem] * (2 * pieces) + [spec] * 6,
+        out_specs=[spec] * 4,
+        out_shape=[jax.ShapeDtypeStruct(master.shape, wide)] * 4,
+        compiler_params=pltpu.CompilerParams(vmem_limit_bytes=20 * mib),
         cost_estimate=pl.CostEstimate(
-            flops=count * 24 * side**3, bytes_accessed=40 * count * side**2, transcendentals=0
+            flops=0, bytes_accessed=1024, transcendentals=0
         ),
         name="optimize",
-    )(grad, rotated_old, master, first, second, left_basis, right_basis)
+    )(*came, *local, rotated_old, master, first, second, left_basis, right_basis)
 
 
 def head_mask(head):
@@ -360,7 +387,7 @@
     return ((lane // HD) == head).astype(low)
 
 
-def attention_tile(qkv, w_out, table, seg_row, tile, came=None):
+def attention_tile(qkv, w_out, table, seg_row, tile, kind):
     width = qkv.shape[1] // 3
     pairs = width // (2 * HD)
     rows = qkv.shape[0]
@@ -385,17 +412,16 @@
                 parts.append(part * (1.0 / total))
                 lse_ref[pair * 2 + head : pair * 2 + head + 1, :] = peak + jnp.log(total)
             ctx_ref[:, lanes] = jnp.concatenate(parts, axis=0).T.astype(low)
-        part = mul(ctx_ref[...], w_ref[...])
-        if came is not None:
-            part = part + refs[0][...].astype(wide)
-        part_ref[...] = part.astype(low)
-
-    operands = [qkv, w_out, table, seg_row] + ([] if came is None else [came])
+        part_ref[...] = mul(ctx_ref[...], w_ref[...]).astype(kind)
+
     return vmem_call(
         kernel,
         "attention_tile",
-        [shaped(low, TILE, width), shaped(wide, 2 * pairs, TILE), shaped(low, TILE, D)],
-        *operands,
+        [shaped(low, TILE, width), shaped(wide, 2 * pairs, TILE), shaped(kind, TILE, D)],
+        qkv,
+        w_out,
+        table,
+        seg_row,
         flops=16 * TILE * rows * width,
         room=8,
     )
@@ -585,30 +611,45 @@
     )
 
 
-def attention_backward(qkv, w_out, table, seg_row, contexts, rows_grads, lses):
+def attention_backward(qkv, w_out, table, seg_row, tiles, contexts, rows_grads, lses, carried):
     width = qkv.shape[1] // 3
     pairs = width // (2 * HD)
     rows = qkv.shape[0]
-    tiles = rows // TILE
+    count = len(tiles)
+    last = carried is not None
+    before = [t for t in range(rows // TILE) if t not in tiles]
 
     def kernel(qkv_ref, w_ref, sk_ref, sq_ref, *refs):
-        ctx_refs, refs = refs[:tiles], refs[tiles:]
-        g_refs, refs = refs[:tiles], refs[tiles:]
-        lse_refs, refs = refs[:tiles], refs[tiles:]
-        out_ref, wgrad_ref, bias_ref, ctx, grad_rows, ctx_grad, lse, gk, gv = refs
-        for t in range(tiles):
+        ctx_refs, refs = refs[:count], refs[count:]
+        g_refs, refs = refs[:count], refs[count:]
+        lse_refs, refs = refs[:count], refs[count:]
+        if last:
+            (old_q, old_k, old_v, old_w, old_b), refs = refs[:5], refs[5:]
+            out_ref, wgrad_ref, bias_ref, ctx, grad_rows, ctx_grad, lse, gk, gv, sums = refs
+        else:
+            out_ref, gk, gv, wgrad_ref, sums, ctx, grad_rows, ctx_grad, lse = refs
+        for t in range(count):
             span = slice(t * TILE, (t + 1) * TILE)
             ctx[span, :] = ctx_refs[t][...]
             grad_rows[span, :] = g_refs[t][...]
             lse[:, span] = lse_refs[t][...]
         ctx_grad[...] = mul(grad_rows[...], w_ref[...], NT).astype(low)
-        wgrad_ref[...] = mul(ctx[...], grad_rows[...], TN).astype(low)
-        gk[...] = jnp.zeros_like(gk)
-        gv[...] = jnp.zeros_like(gv)
-        bias_ref[...] = jnp.zeros_like(bias_ref)
-
-        def step(tile, carry):
+        wgrad = mul(ctx[...], grad_rows[...], TN)
+        if last:
+            wgrad_ref[...] = (wgrad + old_w[...]).astype(low)
+            gk[...] = old_k[...]
+            gv[...] = old_v[...]
+            sums[...] = old_b[...]
+        else:
+            wgrad_ref[...] = wgrad
+            gk[...] = jnp.zeros_like(gk)
+            gv[...] = jnp.zeros_like(gv)
+            sums[...] = jnp.zeros_like(sums)
+
+        def step(index, carry):
+            tile = tiles[0] + index
             span = pl.ds(pl.multiple_of(tile * TILE, TILE), TILE)
+            here = pl.ds(pl.multiple_of(index * TILE, TILE), TILE)
             same = sk_ref[:, 3:4] == sq_ref[:, span]
             for pair in range(pairs):
                 place = pair * 2 * HD
@@ -617,8 +658,8 @@
                 k = qkv_ref[:, width + place : width + place + 2 * HD]
                 v = qkv_ref[:, 2 * width + place : 2 * width + place + 2 * HD]
                 k_t = k.T
-                grad = ctx_grad[span, lanes]
-                dots = (grad.astype(wide) * ctx[span, lanes].astype(wide)).T
+                grad = ctx_grad[here, lanes]
+                dots = (grad.astype(wide) * ctx[here, lanes].astype(wide)).T
                 parts = []
                 for head in range(2):
                     mask = head_mask(head)
@@ -628,26 +669,42 @@
                     features = slice(head * HD, (head + 1) * HD)
                     delta = jnp.sum(dots[features], axis=0, keepdims=True)
                     s = jnp.where(same, mul(k, q_head, NT), -1e30)
-                    p = jnp.exp(s - lse[row : row + 1, span])
+                    p = jnp.exp(s - lse[row : row + 1, here])
                     gs = (p * (mul(v, grad_head, NT) - delta)).astype(low)
                     gv[:, lanes] += mul(p.astype(low), grad_head)
                     gk[:, lanes] += mul(gs, q_head)
                     parts.append(mul(k_t[features], gs))
                 gq = (jnp.concatenate(parts, axis=0).T * HD**-0.5).astype(low)
-                out_ref[span, lanes] = gq
-                bias_ref[:, lanes] += jnp.sum(gq.astype(wide), axis=0, keepdims=True)
+                out_ref[span if last else here, lanes] = gq
+                sums[:, lanes] += jnp.sum(gq.astype(wide), axis=0, keepdims=True)
             return carry
 
-        lax.fori_loop(0, tiles, step, 0)
-        out_ref[:, width : 2 * width] = gk[...].astype(low)
-        gv_low = gv[...].astype(low)
-        out_ref[:, 2 * width :] = gv_low
-        bias_ref[:, width:] = jnp.sum(gv_low.astype(wide), axis=0, keepdims=True)
-
+        lax.fori_loop(0, count, step, 0)
+        if last:
+            for k, t in enumerate(before):
+                out_ref[t * TILE : (t + 1) * TILE, :width] = old_q[k * TILE : (k + 1) * TILE, :]
+            out_ref[:, width : 2 * width] = gk[...].astype(low)
+            gv_low = gv[...].astype(low)
+            out_ref[:, 2 * width :] = gv_low
+            bias_ref[:, :width] = sums[...]
+            bias_ref[:, width:] = jnp.sum(gv_low.astype(wide), axis=0, keepdims=True)
+
+    scratch = [
+        pltpu.VMEM((count * TILE, width), low),
+        pltpu.VMEM((count * TILE, D), low),
+        pltpu.VMEM((count * TILE, width), low),
+        pltpu.VMEM((2 * pairs, count * TILE), wide),
+    ]
+    if last:
+        outs = [shaped(low, rows, 3 * width), shaped(low, width, D), shaped(wide, 1, 2 * width)]
+        scratch += [pltpu.VMEM((rows, width), wide)] * 2 + [pltpu.VMEM((1, width), wide)]
+    else:
+        outs = [shaped(low, count * TILE, width)] + [shaped(wide, rows, width)] * 2
+        outs += [shaped(wide, width, D), shaped(wide, 1, width)]
     return vmem_call(
         kernel,
         "attention_backward",
-        [shaped(low, rows, 3 * width), shaped(low, width, D), shaped(wide, 1, 2 * width)],
+        outs,
         qkv,
         w_out,
         table,
@@ -655,15 +712,9 @@
         *contexts,
         *rows_grads,
         *lses,
-        scratch=[
-            pltpu.VMEM((rows, width), low),
-            pltpu.VMEM((rows, D), low),
-            pltpu.VMEM((rows, width), low),
-            pltpu.VMEM((2 * pairs, rows), wide),
-            pltpu.VMEM((rows, width), wide),
-            pltpu.VMEM((rows, width), wide),
-        ],
-        flops=40 * rows * rows * width,
+        *(carried or []),
+        scratch=scratch,
+        flops=40 * rows * count * TILE * width,
         room=10,
     )
 
@@ -801,7 +852,7 @@
     ring = ring_order(dp_count)
     ahead = [(ring[k], ring[(k + 1) % dp_count]) for k in range(dp_count)]
     routes = [ahead, [(b, a) for a, b in ahead]]
-    bounds = piece_bounds(owned)
+    bounds = piece_bounds(owned, 4)
     piece_count = len(bounds) - 1
     order_list = block_order[0]
     ring_place = jnp.where(dp_index % 2 == 0, dp_index // 2, dp_count - 1 - dp_index // 2)
@@ -853,40 +904,45 @@
         return value[k * quarter : (k + 1) * quarter]
 
     context, lse, mixed = [None] * tiles, [None] * tiles, [None] * half_tiles
-    sent = []
+    row = seg_row
     for k in range(half_tiles):
-        t = half_tiles + k
-        context[t], lse[t], part = attention_tile(qkv, w_out, seg_column, seg_row, t)
-        sent.append(core_swap(part))
-    for k in range(half_tiles):
-        context[k], lse[k], mixed[k] = attention_tile(
-            qkv, w_out, seg_column, seg_row, k, sent[k]
-        )
+        for t in (half_tiles + k, k):
+            context[t], lse[t], part = attention_tile(
+                qkv, w_out, seg_column, row, t, wide if t < half_tiles else low
+            )
+            if t >= half_tiles:
+                sent = core_swap(part)
+                row = after(seg_row, part)
+        mixed[k] = add_low(part, sent)
+        row = after(seg_row, mixed[k])
     came = [chip_swap(value) for value in mixed]
+    def mix(mine_part, other_part):
+        return add_low(mine_part, core_swap(other_part))
+
     normed_one, inverse_one, first_mine, first_other, first_norm = [], [], [], [], []
+    hid_mine, hid_other, slope_mine, slope_other = [], [], [], []
+    mine_parts, ffn_mixed = [], []
+    up_row = bias_up[None, :]
+    ready = mixed[1]
     for k in range(2):
         rows_low, normed_k, inverse_k, rows_wide = norm_rows(
-            place, mixed[k], came[k], cut(x_mine, k), vectors, (0, 2, 3), True
+            place, mixed[k], came[k], cut(x_mine, k), after(vectors, ready), (0, 2, 3), True
         )
         first_mine.append(rows_low)
         normed_one.append(normed_k)
         inverse_one.append(inverse_k)
         first_norm.append(rows_wide)
         first_other.append(core_swap(rows_low))
-
-    def mix(mine_part, other_part):
-        return (mine_part.astype(wide) + core_swap(other_part).astype(wide)).astype(low)
-
-    hid_mine, hid_other, slope_mine, slope_other, mixed = [], [], [], [], []
-    up_row = bias_up[None, :]
-    for k in range(2):
-        mine_part, hid, slope = feed_forward(first_mine[k], w_up, up_row, w_down)
+        ready, hid, slope = feed_forward(rows_low, w_up, up_row, w_down)
+        mine_parts.append(ready)
         hid_mine.append(hid)
         slope_mine.append(slope)
+    for k in range(2):
         other_part, hid, slope = feed_forward(first_other[k], w_up, up_row, w_down)
         hid_other.append(hid)
         slope_other.append(slope)
-        mixed.append(mix(mine_part, other_part))
+        ffn_mixed.append(mix(mine_parts[k], other_part))
+    mixed = ffn_mixed
     came = [chip_swap(value) for value in mixed]
     normed_two, inverse_two, out_mine, out_other, pieces = [], [], [], [], []
     exchange = [(s, s ^ half_dp) for s in range(dp_count)]
@@ -920,9 +976,11 @@
     second_other = [core_swap(value) for value in second_mine]
     pre_mine, pre_other, mixed = [], [], []
     for k in range(2):
-        mine_part, pre = feed_back(second_mine[k], slope_mine[k], w_up, w_down)
+        mine_low = after(second_mine[k], other_part) if k else second_mine[k]
+        mine_part, pre = feed_back(mine_low, slope_mine[k], w_up, w_down)
         pre_mine.append(pre)
-        other_part, pre = feed_back(second_other[k], slope_other[k], w_up, w_down)
+        other_low = after(second_other[k], mine_part)
+        other_part, pre = feed_back(other_low, slope_other[k], w_up, w_down)
         pre_other.append(pre)
         mixed.append(mix(mine_part, other_part))
     came = [chip_swap(value) for value in mixed]
@@ -933,45 +991,51 @@
         pre_mine + pre_other,
     )
 
-    rotated_old = rotate_first(block_first, basis_left, basis_right)
+    rotated_old = rotate_first(after(block_first, mixed[1]), basis_left, basis_right)
     ready = (vectors, grad_down, grad_up, up_grad, rotated_old, output_part)
     late_vectors, grad_down, grad_up, up_grad, rotated_old, output_part = (
         lax.optimization_barrier(ready)
     )
 
-    first_grad, attn_mine, attn_other, sums_one = [], [], [], []
+    first_grad, sums_one, attn_mine, attn_other, carried = [], [], [], [], None
+
+    def attention_part(some):
+        rows_grads = attn_mine + attn_other
+        return attention_backward(
+            qkv,
+            w_out,
+            seg_column,
+            seg_row,
+            some,
+            [context[t] for t in some],
+            [rows_grads[t] for t in some],
+            [lse[t] for t in some],
+            carried,
+        )
+
     for k in range(2):
         grad_k, low_k, sums_k = first_back(
-            mixed[k], came[k], second_grad[k], normed_one[k], inverse_one[k], late_vectors
+            mixed[k],
+            came[k],
+            second_grad[k],
+            normed_one[k],
+            inverse_one[k],
+            late_vectors if carried is None else after(late_vectors, *carried),
         )
         first_grad.append(grad_k)
+        sums_one.append(sums_k)
         attn_mine.append(low_k)
         attn_other.append(core_swap(low_k))
-        sums_one.append(sums_k)
+        if k == 0:
+            carried = attention_part([0])
     shared = pack_sums(place, sums_one, sums_two, score_part)
     shared_came = core_swap(shared)
-    qkv_grad, grad_out, pair_bias = attention_backward(
-        qkv, w_out, seg_column, seg_row, context, attn_mine + attn_other, lse
-    )
+    seg_row = after(seg_row, shared)
+    carried = attention_part(list(range(1, tiles)))
+    qkv_grad, grad_out, pair_bias = carried
     grad_qkv = mul(x_rows, qkv_grad, TN).astype(low)
-    input_mine, input_other = [], []
-    for k in range(2):
-        other_part = mul(cut(qkv_grad, 2 + k), w_qkv, NT).astype(low)
-        mixed_k = mix(mul(cut(qkv_grad, k), w_qkv, NT), other_part)
-        branch_zero = mixed_k.astype(wide) + chip_swap(mixed_k).astype(wide)
-        input_mine.append((first_grad[k] + branch_zero).astype(low))
-        input_other.append(core_swap(input_mine[k]))
-    input_grad = in_order(place, input_mine, input_other)
-
-    small = add_biases(shared, shared_came, pair_bias, up_grad)
-    stride = 1
-    while stride < dp_count:
-        small = small + lax.ppermute(small, "dp", [(s, s ^ stride) for s in range(dp_count)])
-        stride *= 2
-    bias_out, norm_out, scores, small_values = small_update(
-        place, small, bias_state, norm_state, local_width, *score_cot.shape
-    )
-
+    bounds = piece_bounds(owned, 4)
+    piece_count = len(bounds) - 1
     staged = spread(
         place,
         order_list,
@@ -981,17 +1045,66 @@
         owned,
         bounds,
     )
+
+    small = add_biases(shared, shared_came, pair_bias, up_grad)
+    stride = 1
+    input_stage = 0
     travelling = [staged[k * dp_count] for k in range(piece_count)]
     for step in range(dp_count - 1):
         for k in range(piece_count):
             came = lax.ppermute(travelling[k], "dp", routes[k % 2])
-            summed = came.astype(wide) + staged[k * dp_count + step + 1].astype(wide)
-            travelling[k] = summed.astype(low) if step < dp_count - 2 else summed
-    owned_grad = jnp.concatenate(travelling, axis=0)
-
-    owned_grad, input_grad = lax.optimization_barrier((owned_grad, input_grad))
-    first_new, second_new, master_new = optimize(
-        owned_grad, rotated_old, block_master, block_first, block_second, basis_left, basis_right
+            if step < dp_count - 2:
+                local = staged[k * dp_count + step + 1]
+                if step or k:
+                    local = after(local, travelling[k - 1])
+                if k == 0 and step in (2, 4):
+                    local = after(local, small_came)
+                came = (came.astype(wide) + local.astype(wide)).astype(low)
+            travelling[k] = came
+        if step >= dp_count - 2:
+            continue
+        mark = travelling[piece_count - 1]
+        if step % 2 == 0 and stride < dp_count:
+            if stride > 1:
+                small = after(small, mark) + small_came
+            else:
+                small = after(small, mark)
+            pairs = [(s, s ^ stride) for s in range(dp_count)]
+            small_came = lax.ppermute(small, "dp", pairs)
+            stride *= 2
+        if step == 0:
+            late_grad = after(qkv_grad, mark)
+            other_part = core_swap(mul(late_grad[half:], w_qkv, NT).astype(low))
+            mine_part = mul(late_grad[:half], w_qkv, NT)
+        if step == 1:
+            mine_part = after(mine_part, mark)
+            input_mixed = add_low(mine_part, other_part)
+            input_came = chip_swap(input_mixed)
+        if step == 4:
+            branch_zero = after(input_mixed, mark).astype(wide) + input_came.astype(wide)
+            input_mine = (jnp.concatenate(first_grad, axis=0) + branch_zero).astype(low)
+            input_other = core_swap(input_mine)
+        if step == 5:
+            input_grad = in_order(after(place, mark), [input_mine], [input_other])
+    small = small + small_came
+    while stride < dp_count:
+        small = small + lax.ppermute(small, "dp", [(s, s ^ stride) for s in range(dp_count)])
+        stride *= 2
+    bias_out, norm_out, scores, small_values = small_update(
+        place, small, bias_state, norm_state, local_width, *score_cot.shape
+    )
+    local = [staged[(k + 1) * dp_count - 1] for k in range(piece_count)]
+
+    travelling[0], input_grad = lax.optimization_barrier((travelling[0], input_grad))
+    owned_grad, first_new, second_new, master_new = optimize(
+        travelling,
+        local,
+        rotated_old,
+        block_master,
+        block_first,
+        block_second,
+        basis_left,
+        basis_right,
     )
     small_values, master_new = lax.optimization_barrier((small_values, master_new))
     small_values = small_values.reshape(-1)

time: 324 us -> 308 us (0.951)
  Pallas kernels: 83.3 us -> 75.5 us
  starting transfers between devices: 92.6 us -> 86.5 us
    ppermute x10 -> x9, waiting for transfers between devices: 53.3 us -> 62.5 us  [chip_swap(): return lax.ppermute(value, 'mp', chip_pairs)]
    pallas_call x1, Pallas kernels: 13.2 us -> 6.32 us  [optimize(): pl.pallas_call(kernel, grid=(pieces,), in_specs=[vmem] * (2 * pieces) + [...]
    ppermute x28, waiting for transfers between devices: 26.8 us -> 22 us  [body(): came = lax.ppermute(travelling[k], 'dp', routes[k % 2])]
    ppermute x3, waiting for transfers between devices: 3.42 us -> 0.01 us  [body(): small_came = lax.ppermute(small, 'dp', pairs)]
    ppermute x28, starting transfers between devices: 34.8 us -> 31.4 us  [body(): came = lax.ppermute(travelling[k], 'dp', routes[k % 2])]
    pallas_call x29 -> x37, Pallas kernels: 63.8 us -> 65.3 us  [vmem_call(): pl.pallas_call(kernel, in_specs=specs, out_specs=[vmem] * len(outs), out_...]
    ppermute x10 -> x9, starting transfers between devices: 11.6 us -> 11.3 us  [chip_swap(): return lax.ppermute(value, 'mp', chip_pairs)]
  transfers between devices with their start and end apart: 94 -> 91, of which waited for: 50 -> 46; matrix products, arithmetic and copies ran while one was open for 2% -> 1% of each run, Pallas kernels for 18% -> 14%
where the time goes in v1:
time: 308 us; the launch traced here: 304 us
  waiting for transfers between devices  130 us (42%)
  starting transfers between devices  86.5 us (28%)
  Pallas kernels  75.5 us (25%)
  matrix products  5.74 us (2%)
  other arithmetic  3.63 us (1%)
    pallas_call x37, Pallas kernels, vmem_call(): pl.pallas_call(kernel, in_specs=specs, out_specs=[vmem] * len(outs), out_...  65.3 us
    ppermute x9, waiting for transfers between devices, chip_swap(): return lax.ppermute(value, 'mp', chip_pairs)  62.5 us
    ppermute x28, waiting for transfers between devices, body(): arrived[k].append(lax.ppermute(arrived[k][-1], 'dp', routes[k % 2]))  31.6 us
    ppermute x28, starting transfers between devices, body(): came = lax.ppermute(travelling[k], 'dp', routes[k % 2])  31.4 us
    ppermute x28, starting transfers between devices, body(): arrived[k].append(lax.ppermute(arrived[k][-1], 'dp', routes[k % 2]))  29.9 us
    ppermute x28, waiting for transfers between devices, body(): came = lax.ppermute(travelling[k], 'dp', routes[k % 2])  22 us
    ppermute x9, starting transfers between devices, chip_swap(): return lax.ppermute(value, 'mp', chip_pairs)  11.3 us
    ppermute x2, waiting for transfers between devices, body(): mine = lax.ppermute(out_piece, 'dp', exchange)  10.3 us
  transfers between devices with their start and end apart: 91, of which 46 were waited for; matrix products, arithmetic and copies ran while one was open for 1% of the time, Pallas kernels for 14%

profile of v1, /device:TPU:0, one launch (start us, length us, event | category | flops | bytes accessed | tf_op | source)
XLA Modules:
  0.0 303.9 jit_solution(798403794277871075)
XLA Ops:
  2.4 3.1 %collective-permute-start = (bf16[6,128,128]{2,1,0:T(8,128)(2,1)S(1)}, bf16[6,128,128]{2,1,0:T(8,128)(2,1)S(1)}, u32[]{:S(2)}, u32[]{:S(2)}) collective-permute-start(bf16[6,128,128]{2,1,0:T(8,128)(2,1)S(1)} %get-tuple-element.371.refs_0_), channel_id=1, source_target_pairs={{0,8},{8,16},{16,24},{24,28},{28,20},{20,12},{12,4},{4,0},{1,9},{9... | collective-permute-start | bytes 589832 | tf_op jit(solution)/shard_map/ppermute | solution.py:881
  7.7 3.5 %collective-permute-done.refs_1_ = bf16[6,128,128]{2,1,0:T(8,128)(2,1)S(1)} collective-permute-done((bf16[6,128,128]{2,1,0:T(8,128)(2,1)S(1)}, bf16[6,128,128]{2,1,0:T(8,128)(2,1)S(1)}, u32[]{:S(2)}, u32[]{:S(2)}) %collective-permute-start) | collective-permute-done | bytes 196640 | tf_op jit(solution)/shard_map/ppermute | solution.py:881
  66.6 3.2 %assemble.1 = (bf16[1024,768]{1,0:T(8,128)(2,1)S(1)}, bf16[256,1024]{1,0:T(8,128)(2,1)S(1)}, bf16[1024,1024]{1,0:T(8,128)(2,1)S(1)}, bf16[1024,1024]{1,0:T(8,128)(2,1)S(1)}) custom-call(s32[6]{0:T(128)S(1)} %stack.31.place_ref, s32[192]{0:T(256)S(1)} %bitcast.17, bf16[6,128,128]{2,1,0:T(8,128)(2,1)S(1)} %get-tuple-element.371.refs_0_, ...), custom_call_target="tpu_custom_call" | custom-call | bytes 1024 | tf_op jit(solution)/shard_map/assemble/pallas_call | solution.py:76
  71.6 3.3 %attention_tile.4 = (bf16[256,256]{1,0:T(8,128)(2,1)S(1)}, f32[4,256]{1,0:T(4,128)S(1)}, bf16[256,1024]{1,0:T(8,128)(2,1)S(1)}) custom-call(bf16[1024,768]{1,0:T(8,128)(2,1)S(1)} %add_convert_fusion.qkv_ref, bf16[256,1024]{1,0:T(8,128)(2,1)S(1)} %get-tuple-element.194.w_ref, f32[1024,8]{1,0:T(8,128)S(1)} %get-tuple-element.195.sk_ref.table_ref, ...), custom_call_target="tpu_custom_call" | custom-call | bytes 1024 | tf_op jit(solution)/shard_map/attention_tile/pallas_call | solution.py:76
  75.0 3.3 %attention_tile.5 = (bf16[256,256]{1,0:T(8,128)(2,1)S(1)}, f32[4,256]{1,0:T(4,128)S(1)}, f32[256,1024]{1,0:T(8,128)S(1)}) custom-call(bf16[1024,768]{1,0:T(8,128)(2,1)S(1)} %add_convert_fusion.qkv_ref, bf16[256,1024]{1,0:T(8,128)(2,1)S(1)} %get-tuple-element.194.w_ref, f32[1024,8]{1,0:T(8,128)S(1)} %get-tuple-element.195.sk_ref.table_ref, ...), custom_call_target="tpu_custom_call" | custom-call | bytes 1024 | tf_op jit(solution)/shard_map/attention_tile/pallas_call | solution.py:76
  78.4 3.3 %attention_tile.6 = (bf16[256,256]{1,0:T(8,128)(2,1)S(1)}, f32[4,256]{1,0:T(4,128)S(1)}, bf16[256,1024]{1,0:T(8,128)(2,1)S(1)}) custom-call(bf16[1024,768]{1,0:T(8,128)(2,1)S(1)} %add_convert_fusion.qkv_ref, bf16[256,1024]{1,0:T(8,128)(2,1)S(1)} %get-tuple-element.194.w_ref, f32[1024,8]{1,0:T(8,128)S(1)} %get-tuple-element.195.sk_ref.table_ref, ...), custom_call_target="tpu_custom_call" | custom-call | bytes 1024 | tf_op jit(solution)/shard_map/attention_tile/pallas_call | solution.py:76
  83.8 3.5 %attention_tile.7 = (bf16[256,256]{1,0:T(8,128)(2,1)S(1)}, f32[4,256]{1,0:T(4,128)S(1)}, f32[256,1024]{1,0:T(8,128)S(1)}) custom-call(bf16[1024,768]{1,0:T(8,128)(2,1)S(1)} %add_convert_fusion.qkv_ref, bf16[256,1024]{1,0:T(8,128)(2,1)S(1)} %get-tuple-element.194.w_ref, f32[1024,8]{1,0:T(8,128)S(1)} %get-tuple-element.195.sk_ref.table_ref, ...), custom_call_target="tpu_custom_call" | custom-call | bytes 1024 | tf_op jit(solution)/shard_map/attention_tile/pallas_call | solution.py:76
  88.2 8.8 %collective-permute-done.29.b_ref = bf16[256,1024]{1,0:T(8,128)(2,1)S(1)} collective-permute-done((bf16[256,1024]{1,0:T(8,128)(2,1)S(1)}, bf16[256,1024]{1,0:T(8,128)(2,1)S(1)}, u32[]{:S(2)}, u32[]{:S(2)}) %collective-permute-start.29) | collective-permute-done | bytes 524320 | tf_op jit(solution)/shard_map/ppermute | solution.py:850
  99.8 7.6 %collective-permute-done.31.b_ref = bf16[256,1024]{1,0:T(8,128)(2,1)S(1)} collective-permute-done((bf16[256,1024]{1,0:T(8,128)(2,1)S(1)}, bf16[256,1024]{1,0:T(8,128)(2,1)S(1)}, u32[]{:S(2)}, u32[]{:S(2)}) %collective-permute-start.31) | collective-permute-done | bytes 524320 | tf_op jit(solution)/shard_map/ppermute | solution.py:850
  116.4 10.9 %collective-permute-done.35.b_ref = bf16[256,1024]{1,0:T(8,128)(2,1)S(1)} collective-permute-done((bf16[256,1024]{1,0:T(8,128)(2,1)S(1)}, bf16[256,1024]{1,0:T(8,128)(2,1)S(1)}, u32[]{:S(2)}, u32[]{:S(2)}) %collective-permute-start.35) | collective-permute-done | bytes 524320 | tf_op jit(solution)/shard_map/ppermute | solution.py:850
  128.4 2.7 collective-permute-start.38
  131.1 7.1 %collective-permute-done.37.b_ref = bf16[256,1024]{1,0:T(8,128)(2,1)S(1)} collective-permute-done((bf16[256,1024]{1,0:T(8,128)(2,1)S(1)}, bf16[256,1024]{1,0:T(8,128)(2,1)S(1)}, u32[]{:S(2)}, u32[]{:S(2)}) %collective-permute-start.37) | collective-permute-done | bytes 524320 | tf_op jit(solution)/shard_map/ppermute | solution.py:850
  139.2 2.7 collective-permute-start.40
  144.0 9.7 %collective-permute-done.40.refs_9_ = bf16[128,1024]{1,0:T(8,128)(2,1)S(1)} collective-permute-done((bf16[128,1024]{1,0:T(8,128)(2,1)S(1)}, bf16[128,1024]{1,0:T(8,128)(2,1)S(1)}, u32[]{:S(2)}, u32[]{:S(2)}) %collective-permute-start.40) | collective-permute-done | bytes 262176 | tf_op jit(solution)/shard_map/ppermute | solution.py:957
  155.7 5.1 %collective-permute-done.41.refs_10_ = bf16[128,1024]{1,0:T(8,128)(2,1)S(1)} collective-permute-done((bf16[128,1024]{1,0:T(8,128)(2,1)S(1)}, bf16[128,1024]{1,0:T(8,128)(2,1)S(1)}, u32[]{:S(2)}, u32[]{:S(2)}) %collective-permute-start.41) | collective-permute-done | bytes 262176 | tf_op jit(solution)/shard_map/ppermute | solution.py:850
  162.4 3.5 %link_back.1 = (f32[256,1024]{1,0:T(8,128)S(1)}, f32[256,1024]{1,0:T(8,128)S(1)}, bf16[256,1024]{1,0:T(8,128)(2,1)S(1)}, bf16[256,1024]{1,0:T(8,128)(2,1)S(1)}, ...) custom-call(s32[6]{0:T(128)S(1)} %stack.31.place_ref, bf16[512,1024]{1,0:T(8,128)(2,1)S(1)} %get-tuple-element.215.link_ref, ...), custom_call_target="tpu_custom_call" | custom-call | bytes 1024 | tf_op jit(solution)/shard_map/link_back/pallas_call | solution.py:76
  177.8 4.5 %feed_grads.1 = (bf16[1024,1024]{1,0:T(8,128)(2,1)S(1)}, bf16[1024,1024]{1,0:T(8,128)(2,1)S(1)}, f32[1,1024]{1,0:T(1,128)S(1)}) custom-call(bf16[256,1024]{1,0:T(8,128)(2,1)S(1)} %get-tuple-element.208.refs_0_, bf16[256,1024]{1,0:T(8,128)(2,1)S(1)} %get-tuple-element.212.refs_1_, bf16[256,1024]{1,0:T(8,128)(2,1)S(1)} %get-tuple-element.213.refs_2_, ...), custom_call_target="tpu_custom_call" | custom-call | bytes 1024 | tf_op jit(solution)/shard_map/feed_grads/pallas_call | solution.py:76
  184.7 3.3 %collective-permute-done.52.b_ref = bf16[256,1024]{1,0:T(8,128)(2,1)S(1)} collective-permute-done((bf16[256,1024]{1,0:T(8,128)(2,1)S(1)}, bf16[256,1024]{1,0:T(8,128)(2,1)S(1)}, u32[]{:S(2)}, u32[]{:S(2)}) %collective-permute-start.52) | collective-permute-done | bytes 524320 | tf_op jit(solution)/shard_map/ppermute | solution.py:850
  188.8 3.4 %attention_backward.2 = (bf16[256,256]{1,0:T(8,128)(2,1)S(1)}, f32[1024,256]{1,0:T(8,128)S(1)}, f32[1024,256]{1,0:T(8,128)S(1)}, f32[256,1024]{1,0:T(8,128)S(1)}, f32[1,256]{1,0:T(1,128)S(1)}) custom-call(bf16[1024,768]{1,0:T(8,128)(2,1)S(1)} %add_convert_fusion.qkv_ref, bf16[256,1024]{1,0:T(8,128)(2,1)S(1)} %get-tuple-element.194.w_ref, ...), custom_call_target="tpu_custom_call" | custom-call | bytes 1024 | tf_op jit(solution)/shard_map/attention_backward/pallas_call | solution.py:76
  192.2 6.2 %collective-permute-done.53.b_ref = bf16[256,1024]{1,0:T(8,128)(2,1)S(1)} collective-permute-done((bf16[256,1024]{1,0:T(8,128)(2,1)S(1)}, bf16[256,1024]{1,0:T(8,128)(2,1)S(1)}, u32[]{:S(2)}, u32[]{:S(2)}) %collective-permute-start.53) | collective-permute-done | bytes 524320 | tf_op jit(solution)/shard_map/ppermute | solution.py:850
  201.9 10.3 %attention_backward.3 = (bf16[1024,768]{1,0:T(8,128)(2,1)S(1)}, bf16[256,1024]{1,0:T(8,128)(2,1)S(1)}, f32[1,512]{1,0:T(1,128)S(1)}) custom-call(bf16[1024,768]{1,0:T(8,128)(2,1)S(1)} %add_convert_fusion.qkv_ref, bf16[256,1024]{1,0:T(8,128)(2,1)S(1)} %get-tuple-element.194.w_ref, f32[1024,8]{1,0:T(8,128)S(1)} %get-tuple-element.195.sk_ref.table_ref, ...), custom_call_target="tpu_custom_call" | custom-call | bytes 1024 | tf_op jit(solution)/shard_map/attention_backward/pallas_call | solution.py:76
  220.4 3.7 %collective-permute-done.60 = bf16[6,128,128]{2,1,0:T(8,128)(2,1)S(1)} collective-permute-done((bf16[6,128,128]{2,1,0:T(8,128)(2,1)S(1)}, bf16[6,128,128]{2,1,0:T(8,128)(2,1)S(1)}, u32[]{:S(2)}, u32[]{:S(2)}) %collective-permute-start.60) | collective-permute-done | bytes 196640 | tf_op jit(solution)/shard_map/ppermute | solution.py:1055
  267.4 13.4 %collective-permute-done.86 = bf16[512,1024]{1,0:T(8,128)(2,1)S(1)} collective-permute-done((bf16[512,1024]{1,0:T(8,128)(2,1)S(1)}, bf16[512,1024]{1,0:T(8,128)(2,1)S(1)}, u32[]{:S(2)}, u32[]{:S(2)}) %collective-permute-start.86) | collective-permute-done | bytes 1048608 | tf_op jit(solution)/shard_map/ppermute | solution.py:850
  296.8 6.3 %optimize.1 = (f32[24,128,128]{2,1,0:T(8,128)}, f32[24,128,128]{2,1,0:T(8,128)}, f32[24,128,128]{2,1,0:T(8,128)}, f32[24,128,128]{2,1,0:T(8,128)}) custom-call(bf16[6,128,128]{2,1,0:T(8,128)(2,1)S(1)} %collective-permute-done.81.refs_0_, bf16[6,128,128]{2,1,0:T(8,128)(2,1)S(1)} %collective-permute-done.88.refs_1_, ...), custom_call_target="tpu_custom_call" | custom-call | bytes 1024 | tf_op jit(solution)/shard_map/optimize/pallas_call | solution.py:371
  (271 shorter events, 169.9 us)
Async XLA Ops:
  5.5 9.9 %collective-permute-start.14 = (bf16[6,128,128]{2,1,0:T(8,128)(2,1)S(1)}, bf16[6,128,128]{2,1,0:T(8,128)(2,1)S(1)}, u32[]{:S(2)}, u32[]{:S(2)}) collective-permute-start(bf16[6,128,128]{2,1,0:T(8,128)(2,1)S(1)} %get-tuple-element.369.refs_16_), channel_id=1, source_target_pairs={{0,8},{8,16},{16,24},{24,28},{28,20},{20,12},{12,4},{4,0},{1,9},{9... | collective-permute-start | bytes 589832 | tf_op jit(solution)/shard_map/ppermute | solution.py:881
  7.5 10.1 %collective-permute-start.21 = (bf16[6,128,128]{2,1,0:T(8,128)(2,1)S(1)}, bf16[6,128,128]{2,1,0:T(8,128)(2,1)}, u32[]{:S(2)}, u32[]{:S(2)}) collective-permute-start(bf16[6,128,128]{2,1,0:T(8,128)(2,1)S(1)} %get-tuple-element.368.refs_24_), channel_id=1, source_target_pairs={{8,0},{16,8},{24,16},{28,24},{20,28},{12,20},{4,12},{0,4},{9,1},{1... | collective-permute-start | bytes 589832 | tf_op jit(solution)/shard_map/ppermute | solution.py:881
  11.2 9.0 %collective-permute-start.1 = (bf16[6,128,128]{2,1,0:T(8,128)(2,1)S(1)}, bf16[6,128,128]{2,1,0:T(8,128)(2,1)}, u32[]{:S(2)}, u32[]{:S(2)}) collective-permute-start(bf16[6,128,128]{2,1,0:T(8,128)(2,1)S(1)} %collective-permute-done.refs_1_), channel_id=1, source_target_pairs={{0,8},{8,16},{16,24},{24,28},{28,20},{20,12},{12,4},{4,0},{1,9},{9... | collective-permute-start | bytes 589832 | tf_op jit(solution)/shard_map/ppermute | solution.py:881
  82.3 14.8 %collective-permute-start.29 = (bf16[256,1024]{1,0:T(8,128)(2,1)S(1)}, bf16[256,1024]{1,0:T(8,128)(2,1)S(1)}, u32[]{:S(2)}, u32[]{:S(2)}) collective-permute-start(bf16[256,1024]{1,0:T(8,128)(2,1)S(1)} %add_low.7.a_ref), channel_id=1, source_target_pairs={{0,2},{1,3},{2,0},{3,1},{4,6},{5,7},{6,4},{7,5},{8,10},{9,11},{10,... | collective-permute-start | bytes 1572872 | tf_op jit(solution)/shard_map/ppermute | solution.py:850
  87.4 20.0 %collective-permute-start.31 = (bf16[256,1024]{1,0:T(8,128)(2,1)S(1)}, bf16[256,1024]{1,0:T(8,128)(2,1)S(1)}, u32[]{:S(2)}, u32[]{:S(2)}) collective-permute-start(bf16[256,1024]{1,0:T(8,128)(2,1)S(1)} %add_low.8.a_ref), channel_id=1, source_target_pairs={{0,2},{1,3},{2,0},{3,1},{4,6},{5,7},{6,4},{7,5},{8,10},{9,11},{10,... | collective-permute-start | bytes 1572872 | tf_op jit(solution)/shard_map/ppermute | solution.py:850
  98.2 10.4 %collective-permute-start.32 = (bf16[256,1024]{1,0:T(8,128)(2,1)S(1)}, bf16[256,1024]{1,0:T(8,128)(2,1)S(1)}, u32[]{:S(2)}, u32[]{:S(2)}) collective-permute-start(bf16[256,1024]{1,0:T(8,128)(2,1)S(1)} %get-tuple-element.205.h_ref.refs_8_), channel_id=1, source_target_pairs={{0,1},{1,0},{2,3},{3,2},{4,5},{5,4},{6,7},{7,6},{8,9},{9,8},{10,11... | collective-permute-start | bytes 1572872 | tf_op jit(solution)/shard_map/ppermute | solution.py:847
  112.5 14.8 %collective-permute-start.35 = (bf16[256,1024]{1,0:T(8,128)(2,1)S(1)}, bf16[256,1024]{1,0:T(8,128)(2,1)S(1)}, u32[]{:S(2)}, u32[]{:S(2)}) collective-permute-start(bf16[256,1024]{1,0:T(8,128)(2,1)S(1)} %add_low.9.a_ref), channel_id=1, source_target_pairs={{0,2},{1,3},{2,0},{3,1},{4,6},{5,7},{6,4},{7,5},{8,10},{9,11},{10,... | collective-permute-start | bytes 1572872 | tf_op jit(solution)/shard_map/ppermute | solution.py:850
  115.8 22.4 %collective-permute-start.37 = (bf16[256,1024]{1,0:T(8,128)(2,1)S(1)}, bf16[256,1024]{1,0:T(8,128)(2,1)S(1)}, u32[]{:S(2)}, u32[]{:S(2)}) collective-permute-start(bf16[256,1024]{1,0:T(8,128)(2,1)S(1)} %add_low.10.a_ref), channel_id=1, source_target_pairs={{0,2},{1,3},{2,0},{3,1},{4,6},{5,7},{6,4},{7,5},{8,10},{9,11},{10,... | collective-permute-start | bytes 1572872 | tf_op jit(solution)/shard_map/ppermute | solution.py:850
  128.4 14.1 %collective-permute-start.38 = (bf16[128,1024]{1,0:T(8,128)(2,1)S(1)}, bf16[128,1024]{1,0:T(8,128)(2,1)S(1)}, u32[]{:S(2)}, u32[]{:S(2)}) collective-permute-start(bf16[128,1024]{1,0:T(8,128)(2,1)S(1)} %get-tuple-element.227), channel_id=1, source_target_pairs={{0,16},{4,20},{8,24},{12,28},{16,0},{20,4},{24,8},{28,12},{1,17},{... | collective-permute-start | bytes 786440 | tf_op jit(solution)/shard_map/ppermute | solution.py:957
  139.2 14.5 %collective-permute-start.40 = (bf16[128,1024]{1,0:T(8,128)(2,1)S(1)}, bf16[128,1024]{1,0:T(8,128)(2,1)S(1)}, u32[]{:S(2)}, u32[]{:S(2)}) collective-permute-start(bf16[128,1024]{1,0:T(8,128)(2,1)S(1)} %get-tuple-element.228), channel_id=1, source_target_pairs={{0,16},{4,20},{8,24},{12,28},{16,0},{20,4},{24,8},{28,12},{1,17},{... | collective-permute-start | bytes 786440 | tf_op jit(solution)/shard_map/ppermute | solution.py:957
  142.5 12.8 %collective-permute-start.39 = (bf16[128,1024]{1,0:T(8,128)(2,1)S(1)}, bf16[128,1024]{1,0:T(8,128)(2,1)S(1)}, u32[]{:S(2)}, u32[]{:S(2)}) collective-permute-start(bf16[128,1024]{1,0:T(8,128)(2,1)S(1)} %collective-permute-done.38.refs_7_), channel_id=1, source_target_pairs={{0,2},{1,3},{2,0},{3,1},{4,6},{5,7},{6,4},{7,5},{8,10},{9,11},{10,... | collective-permute-start | bytes 786440 | tf_op jit(solution)/shard_map/ppermute | solution.py:850
  173.2 14.8 %collective-permute-start.52 = (bf16[256,1024]{1,0:T(8,128)(2,1)S(1)}, bf16[256,1024]{1,0:T(8,128)(2,1)S(1)}, u32[]{:S(2)}, u32[]{:S(2)}) collective-permute-start(bf16[256,1024]{1,0:T(8,128)(2,1)S(1)} %add_low.12.a_ref), channel_id=1, source_target_pairs={{0,2},{1,3},{2,0},{3,1},{4,6},{5,7},{6,4},{7,5},{8,10},{9,11},{10,... | collective-permute-start | bytes 1572872 | tf_op jit(solution)/shard_map/ppermute | solution.py:850
  174.9 23.5 %collective-permute-start.53 = (bf16[256,1024]{1,0:T(8,128)(2,1)S(1)}, bf16[256,1024]{1,0:T(8,128)(2,1)S(1)}, u32[]{:S(2)}, u32[]{:S(2)}) collective-permute-start(bf16[256,1024]{1,0:T(8,128)(2,1)S(1)} %add_low.11.a_ref), channel_id=1, source_target_pairs={{0,2},{1,3},{2,0},{3,1},{4,6},{5,7},{6,4},{7,5},{8,10},{9,11},{10,... | collective-permute-start | bytes 1572872 | tf_op jit(solution)/shard_map/ppermute | solution.py:850
  218.3 9.9 %collective-permute-start.58 = (bf16[6,128,128]{2,1,0:T(8,128)(2,1)S(1)}, bf16[6,128,128]{2,1,0:T(8,128)(2,1)S(1)}, u32[]{:S(2)}, u32[]{:S(2)}) collective-permute-start(bf16[6,128,128]{2,1,0:T(8,128)(2,1)S(1)} %get-tuple-element.287), channel_id=1, source_target_pairs={{0,8},{8,16},{16,24},{24,28},{28,20},{20,12},{12,4},{4,0},{1,9},{9... | collective-permute-start | bytes 589832 | tf_op jit(solution)/shard_map/ppermute | solution.py:1055
  220.1 10.0 %collective-permute-start.57 = (bf16[6,128,128]{2,1,0:T(8,128)(2,1)S(1)}, bf16[6,128,128]{2,1,0:T(8,128)(2,1)S(1)}, u32[]{:S(2)}, u32[]{:S(2)}) collective-permute-start(bf16[6,128,128]{2,1,0:T(8,128)(2,1)S(1)} %get-tuple-element.285), channel_id=1, source_target_pairs={{8,0},{16,8},{24,16},{28,24},{20,28},{12,20},{4,12},{0,4},{9,1},{1... | collective-permute-start | bytes 589832 | tf_op jit(solution)/shard_map/ppermute | solution.py:1055
  231.5 23.8 %collective-permute-start.85 = (bf16[512,1024]{1,0:T(8,128)(2,1)S(1)}, bf16[512,1024]{1,0:T(8,128)(2,1)S(1)}, u32[]{:S(2)}, u32[]{:S(2)}) collective-permute-start(bf16[512,1024]{1,0:T(8,128)(2,1)S(1)} %convolution_convert_fusion.1), channel_id=1, source_target_pairs={{0,1},{1,0},{2,3},{3,2},{4,5},{5,4},{6,7},{7,6},{8,9},{9,8},{10,11... | collective-permute-start | bytes 3145736 | tf_op jit(solution)/shard_map/ppermute | solution.py:847
  242.9 9.7 %collective-permute-start.72 = (bf16[6,128,128]{2,1,0:T(8,128)(2,1)S(1)}, bf16[6,128,128]{2,1,0:T(8,128)(2,1)S(1)}, u32[]{:S(2)}, u32[]{:S(2)}) collective-permute-start(bf16[6,128,128]{2,1,0:T(8,128)(2,1)S(1)} %add_convert_fusion.15), channel_id=1, source_target_pairs={{8,0},{16,8},{24,16},{28,24},{20,28},{12,20},{4,12},{0,4},{9,1},{1... | collective-permute-start | bytes 589832 | tf_op jit(solution)/shard_map/ppermute | solution.py:1055
  257.1 23.7 %collective-permute-start.86 = (bf16[512,1024]{1,0:T(8,128)(2,1)S(1)}, bf16[512,1024]{1,0:T(8,128)(2,1)S(1)}, u32[]{:S(2)}, u32[]{:S(2)}) collective-permute-start(bf16[512,1024]{1,0:T(8,128)(2,1)S(1)} %add_low.13), channel_id=1, source_target_pairs={{0,2},{1,3},{2,0},{3,1},{4,6},{5,7},{6,4},{7,5},{8,10},{9,11},{10,... | collective-permute-start | bytes 3145736 | tf_op jit(solution)/shard_map/ppermute | solution.py:850
  260.1 23.2 %collective-permute-start.80 = (bf16[6,128,128]{2,1,0:T(8,128)(2,1)S(1)}, bf16[6,128,128]{2,1,0:T(8,128)(2,1)S(1)}, u32[]{:S(2)}, u32[]{:S(2)}) collective-permute-start(bf16[6,128,128]{2,1,0:T(8,128)(2,1)S(1)} %add_convert_fusion.8), channel_id=1, source_target_pairs={{0,8},{8,16},{16,24},{24,28},{28,20},{20,12},{12,4},{4,0},{1,9},{9... | collective-permute-start | bytes 589832 | tf_op jit(solution)/shard_map/ppermute | solution.py:1055
  262.4 21.0 %collective-permute-start.84 = (bf16[6,128,128]{2,1,0:T(8,128)(2,1)S(1)}, bf16[6,128,128]{2,1,0:T(8,128)(2,1)S(1)}, u32[]{:S(2)}, u32[]{:S(2)}) collective-permute-start(bf16[6,128,128]{2,1,0:T(8,128)(2,1)S(1)} %add_convert_fusion.7), channel_id=1, source_target_pairs={{8,0},{16,8},{24,16},{28,24},{20,28},{12,20},{4,12},{0,4},{9,1},{1... | collective-permute-start | bytes 589832 | tf_op jit(solution)/shard_map/ppermute | solution.py:1055
  264.3 21.0 %collective-permute-start.83 = (bf16[6,128,128]{2,1,0:T(8,128)(2,1)S(1)}, bf16[6,128,128]{2,1,0:T(8,128)(2,1)S(1)}, u32[]{:S(2)}, u32[]{:S(2)}) collective-permute-start(bf16[6,128,128]{2,1,0:T(8,128)(2,1)S(1)} %add_convert_fusion.6), channel_id=1, source_target_pairs={{0,8},{8,16},{16,24},{24,28},{28,20},{20,12},{12,4},{4,0},{1,9},{9... | collective-permute-start | bytes 589832 | tf_op jit(solution)/shard_map/ppermute | solution.py:1055
  266.7 18.7 %collective-permute-start.82 = (bf16[6,128,128]{2,1,0:T(8,128)(2,1)S(1)}, bf16[6,128,128]{2,1,0:T(8,128)(2,1)S(1)}, u32[]{:S(2)}, u32[]{:S(2)}) collective-permute-start(bf16[6,128,128]{2,1,0:T(8,128)(2,1)S(1)} %add_convert_fusion.5), channel_id=1, source_target_pairs={{8,0},{16,8},{24,16},{28,24},{20,28},{12,20},{4,12},{0,4},{9,1},{1... | collective-permute-start | bytes 589832 | tf_op jit(solution)/shard_map/ppermute | solution.py:1055
  285.3 9.8 %collective-permute-start.89 = (bf16[6,128,128]{2,1,0:T(8,128)(2,1)S(1)}, bf16[6,128,128]{2,1,0:T(8,128)(2,1)S(1)}, u32[]{:S(2)}, u32[]{:S(2)}) collective-permute-start(bf16[6,128,128]{2,1,0:T(8,128)(2,1)S(1)} %add_convert_fusion.2), channel_id=1, source_target_pairs={{0,8},{8,16},{16,24},{24,28},{28,20},{20,12},{12,4},{4,0},{1,9},{9... | collective-permute-start | bytes 589832 | tf_op jit(solution)/shard_map/ppermute | solution.py:1055
  287.5 9.2 %collective-permute-start.88 = (bf16[6,128,128]{2,1,0:T(8,128)(2,1)S(1)}, bf16[6,128,128]{2,1,0:T(8,128)(2,1)S(1)}, u32[]{:S(2)}, u32[]{:S(2)}) collective-permute-start(bf16[6,128,128]{2,1,0:T(8,128)(2,1)S(1)} %add_convert_fusion.3), channel_id=1, source_target_pairs={{8,0},{16,8},{24,16},{28,24},{20,28},{12,20},{4,12},{0,4},{9,1},{1... | collective-permute-start | bytes 589832 | tf_op jit(solution)/shard_map/ppermute | solution.py:1055
  (82 other events, 589.8 us)

commit v2 on v1

--- a/solution.py
+++ b/solution.py
@@ -161,11 +161,16 @@
     )
 
 
+def joined(refs):
+    values = [ref[...] for ref in refs]
+    return values[0] if len(values) == 1 else jnp.concatenate(values, axis=0)
+
+
 def add_low(left, right):
-    def kernel(a_ref, b_ref, out_ref):
-        out_ref[...] = (a_ref[...].astype(wide) + b_ref[...].astype(wide)).astype(low)
-
-    return vmem_call(kernel, "add_low", [shaped(low, *left.shape)], left, right)[0]
+    def kernel(a_ref, *refs):
+        refs[-1][...] = (a_ref[...].astype(wide) + joined(refs[:-1]).astype(wide)).astype(low)
+
+    return vmem_call(kernel, "add_low", [shaped(low, *left.shape)], left, *right)[0]
 
 
 def in_order(place, mine, other):
@@ -188,19 +193,22 @@
 def feed_grads(hidden, second_rows, first_rows, pre_rows):
     count, rows = len(hidden), hidden[0].shape[0]
     inner = hidden[0].shape[1]
+    pieces = 3 * count + len(first_rows)
 
     def kernel(*refs):
-        down_ref, up_ref, bias_ref, left, right = refs[4 * count :]
+        down_ref, up_ref, bias_ref, left, right = refs[pieces:]
 
         def fill(target, sources):
-            for k, ref in enumerate(sources):
-                target[k * rows : (k + 1) * rows, :] = ref[...]
+            start = 0
+            for ref in sources:
+                target[start : start + ref.shape[0], :] = ref[...]
+                start += ref.shape[0]
 
         fill(left, refs[:count])
         fill(right, refs[count : 2 * count])
         down_ref[...] = mul(left[...], right[...], TN).astype(low)
-        fill(left, refs[2 * count : 3 * count])
-        fill(right, refs[3 * count : 4 * count])
+        fill(left, refs[2 * count : pieces - count])
+        fill(right, refs[pieces - count : pieces])
         up_ref[...] = mul(left[...], right[...], TN).astype(low)
         bias_ref[...] = jnp.sum(right[...].astype(wide), axis=0, keepdims=True)
 
@@ -387,14 +395,14 @@
     return ((lane // HD) == head).astype(low)
 
 
-def attention_tile(qkv, w_out, table, seg_row, tile, kind):
+def attention_tile(qkv, w_out, table, seg_row, tile, kind, pieces):
     width = qkv.shape[1] // 3
     pairs = width // (2 * HD)
     rows = qkv.shape[0]
     span = slice(tile * TILE, (tile + 1) * TILE)
 
     def kernel(qkv_ref, w_ref, sk_ref, sq_ref, *refs):
-        ctx_ref, lse_ref, part_ref = refs[-3:]
+        ctx_ref, lse_ref, *part_refs = refs
         same = sk_ref[:, 3:4] == sq_ref[:, span]
         for pair in range(pairs):
             place = pair * 2 * HD
@@ -412,12 +420,16 @@
                 parts.append(part * (1.0 / total))
                 lse_ref[pair * 2 + head : pair * 2 + head + 1, :] = peak + jnp.log(total)
             ctx_ref[:, lanes] = jnp.concatenate(parts, axis=0).T.astype(low)
-        part_ref[...] = mul(ctx_ref[...], w_ref[...]).astype(kind)
+        part = mul(ctx_ref[...], w_ref[...]).astype(kind)
+        size = TILE // len(part_refs)
+        for k, part_ref in enumerate(part_refs):
+            part_ref[...] = part[k * size : (k + 1) * size]
 
     return vmem_call(
         kernel,
         "attention_tile",
-        [shaped(low, TILE, width), shaped(wide, 2 * pairs, TILE), shaped(kind, TILE, D)],
+        [shaped(low, TILE, width), shaped(wide, 2 * pairs, TILE)]
+        + [shaped(kind, TILE // pieces, D)] * pieces,
         qkv,
         w_out,
         table,
@@ -431,14 +443,18 @@
     bias_row, gain_row, shift_row = which
     rows = mixed.shape[0]
 
-    def kernel(place_ref, a_ref, b_ref, x_ref, v_ref, low_ref, normed_ref, inverse_ref, last_ref):
+    pieces = 2 if keep else 1
+
+    def kernel(place_ref, a_ref, b_ref, x_ref, v_ref, normed_ref, inverse_ref, last_ref, *low_refs):
         total = a_ref[...].astype(wide) + b_ref[...].astype(wide)
         z = x_ref[...].astype(wide) + total + v_ref[bias_row : bias_row + 1, :]
         center = z - jnp.mean(z, axis=1, keepdims=True)
         inverse = lax.rsqrt(jnp.mean(center * center, axis=1, keepdims=True) + norm_eps)
         normed = center * inverse
         out = v_ref[gain_row : gain_row + 1, :] * normed + v_ref[shift_row : shift_row + 1, :]
-        low_ref[...] = out.astype(low)
+        out_low = out.astype(low)
+        for k, low_ref in enumerate(low_refs):
+            low_ref[...] = out_low[k * rows // pieces : (k + 1) * rows // pieces]
         normed_ref[...] = normed
         inverse_ref[...] = inverse
         if keep:
@@ -447,8 +463,9 @@
             first_chip = place_ref[3] == 0
             last_ref[...] = jnp.where(first_chip, out[: rows // 2], out[rows // 2 :]).astype(low)
 
-    outs = [shaped(low, rows, D), shaped(wide, rows, D), shaped(wide, rows, 1)]
+    outs = [shaped(wide, rows, D), shaped(wide, rows, 1)]
     outs += [shaped(wide, rows, D) if keep else shaped(low, rows // 2, D)]
+    outs += [shaped(low, rows // pieces, D)] * pieces
     return vmem_call(
         kernel,
         "norm_rows",
@@ -482,10 +499,11 @@
 
 
 def feed_forward(rows_low, w_up, bias_up, w_down):
-    rows, hidden = rows_low.shape[0], w_up.shape[1]
-
-    def kernel(h_ref, up_ref, b_ref, down_ref, part_ref, hid_ref, slope_ref):
-        u = mul(h_ref[...], up_ref[...]) + b_ref[...]
+    rows, hidden = sum(value.shape[0] for value in rows_low), w_up.shape[1]
+
+    def kernel(up_ref, b_ref, down_ref, *refs):
+        part_ref, hid_ref, slope_ref = refs[-3:]
+        u = mul(joined(refs[:-3]), up_ref[...]) + b_ref[...]
         hid, slope = gelu_parts(u)
         hid_ref[...] = hid
         slope_ref[...] = slope
@@ -495,10 +513,10 @@
         kernel,
         "feed_forward",
         [shaped(low, rows, D), shaped(low, rows, hidden), shaped(wide, rows, hidden)],
-        rows_low,
         w_up,
         bias_up,
         w_down,
+        *rows_low,
         flops=4 * rows * D * hidden,
     )
 
@@ -588,19 +606,21 @@
 def first_back(mixed, came, second_grad, normed, inverse, vectors):
     rows = mixed.shape[0]
 
-    def kernel(a_ref, b_ref, g_ref, n_ref, i_ref, v_ref, grad_ref, low_ref, sums_ref):
+    def kernel(a_ref, b_ref, g_ref, n_ref, i_ref, v_ref, grad_ref, sums_ref, *low_refs):
         total = a_ref[...].astype(wide) + b_ref[...].astype(wide)
         grad_rows = g_ref[...] + total
         normed_k = n_ref[...]
         grad_z = norm_back(grad_rows, v_ref[2:3, :], normed_k, i_ref[...])
         grad_ref[...] = grad_z
-        low_ref[...] = grad_z.astype(low)
+        grad_low = grad_z.astype(low)
+        for k, low_ref in enumerate(low_refs):
+            low_ref[...] = grad_low[k * rows // 2 : (k + 1) * rows // 2]
         sums_ref[...] = column_sums(grad_z, grad_rows, normed_k)
 
     return vmem_call(
         kernel,
         "first_back",
-        [shaped(wide, rows, D), shaped(low, rows, D), shaped(wide, 3, D)],
+        [shaped(wide, rows, D), shaped(wide, 3, D)] + [shaped(low, rows // 2, D)] * 2,
         mixed,
         came,
         second_grad,
@@ -621,7 +641,7 @@
 
     def kernel(qkv_ref, w_ref, sk_ref, sq_ref, *refs):
         ctx_refs, refs = refs[:count], refs[count:]
-        g_refs, refs = refs[:count], refs[count:]
+        g_refs, refs = refs[: len(rows_grads)], refs[len(rows_grads) :]
         lse_refs, refs = refs[:count], refs[count:]
         if last:
             (old_q, old_k, old_v, old_w, old_b), refs = refs[:5], refs[5:]
@@ -631,8 +651,9 @@
         for t in range(count):
             span = slice(t * TILE, (t + 1) * TILE)
             ctx[span, :] = ctx_refs[t][...]
-            grad_rows[span, :] = g_refs[t][...]
             lse[:, span] = lse_refs[t][...]
+        for k, ref in enumerate(g_refs):
+            grad_rows[k * ref.shape[0] : (k + 1) * ref.shape[0], :] = ref[...]
         ctx_grad[...] = mul(grad_rows[...], w_ref[...], NT).astype(low)
         wgrad = mul(ctx[...], grad_rows[...], TN)
         if last:
@@ -647,7 +668,7 @@
             sums[...] = jnp.zeros_like(sums)
 
         def step(index, carry):
-            tile = tiles[0] + index
+            tile = tiles[0] + (tiles[1] - tiles[0]) * index
             span = pl.ds(pl.multiple_of(tile * TILE, TILE), TILE)
             here = pl.ds(pl.multiple_of(index * TILE, TILE), TILE)
             same = sk_ref[:, 3:4] == sq_ref[:, span]
@@ -907,47 +928,50 @@
     row = seg_row
     for k in range(half_tiles):
         for t in (half_tiles + k, k):
-            context[t], lse[t], part = attention_tile(
-                qkv, w_out, seg_column, row, t, wide if t < half_tiles else low
+            own = t < half_tiles
+            context[t], lse[t], *part = attention_tile(
+                qkv, w_out, seg_column, row, t, wide if own else low, 1 if own else 2
             )
-            if t >= half_tiles:
-                sent = core_swap(part)
-                row = after(seg_row, part)
-        mixed[k] = add_low(part, sent)
+            if not own:
+                sent = [core_swap(value) for value in part]
+                row = after(seg_row, *part)
+        mixed[k] = add_low(part[0], sent)
         row = after(seg_row, mixed[k])
     came = [chip_swap(value) for value in mixed]
     def mix(mine_part, other_part):
-        return add_low(mine_part, core_swap(other_part))
+        return add_low(mine_part, [core_swap(other_part)])
 
     normed_one, inverse_one, first_mine, first_other, first_norm = [], [], [], [], []
     hid_mine, hid_other, slope_mine, slope_other = [], [], [], []
-    mine_parts, ffn_mixed = [], []
+    ffn_mixed = []
     up_row = bias_up[None, :]
     ready = mixed[1]
     for k in range(2):
-        rows_low, normed_k, inverse_k, rows_wide = norm_rows(
+        normed_k, inverse_k, rows_wide, *rows_low = norm_rows(
             place, mixed[k], came[k], cut(x_mine, k), after(vectors, ready), (0, 2, 3), True
         )
-        first_mine.append(rows_low)
         normed_one.append(normed_k)
         inverse_one.append(inverse_k)
         first_norm.append(rows_wide)
-        first_other.append(core_swap(rows_low))
-        ready, hid, slope = feed_forward(rows_low, w_up, up_row, w_down)
-        mine_parts.append(ready)
+        first_mine += rows_low
+        rows_other = [core_swap(value) for value in rows_low]
+        first_other += rows_other
+        mine_part, hid, slope = feed_forward(rows_low, w_up, up_row, w_down)
         hid_mine.append(hid)
         slope_mine.append(slope)
-    for k in range(2):
-        other_part, hid, slope = feed_forward(first_other[k], w_up, up_row, w_down)
+        other_part, hid, slope = feed_forward(
+            rows_other, w_up, after(up_row, mine_part), w_down
+        )
         hid_other.append(hid)
         slope_other.append(slope)
-        ffn_mixed.append(mix(mine_parts[k], other_part))
+        ready = other_part
+        ffn_mixed.append(mix(mine_part, other_part))
     mixed = ffn_mixed
     came = [chip_swap(value) for value in mixed]
     normed_two, inverse_two, out_mine, out_other, pieces = [], [], [], [], []
     exchange = [(s, s ^ half_dp) for s in range(dp_count)]
     for k in range(2):
-        out_k, normed_k, inverse_k, out_piece = norm_rows(
+        normed_k, inverse_k, out_piece, out_k = norm_rows(
             place, mixed[k], came[k], first_norm[k], vectors, (1, 4, 5), False
         )
         normed_two.append(normed_k)
@@ -1008,13 +1032,13 @@
             seg_row,
             some,
             [context[t] for t in some],
-            [rows_grads[t] for t in some],
+            sum([rows_grads[t] for t in some], []),
             [lse[t] for t in some],
             carried,
         )
 
     for k in range(2):
-        grad_k, low_k, sums_k = first_back(
+        grad_k, sums_k, *low_k = first_back(
             mixed[k],
             came[k],
             second_grad[k],
@@ -1025,13 +1049,15 @@
         first_grad.append(grad_k)
         sums_one.append(sums_k)
         attn_mine.append(low_k)
-        attn_other.append(core_swap(low_k))
+        attn_other.append([core_swap(value) for value in low_k])
         if k == 0:
-            carried = attention_part([0])
+            attn_mine.append(None)
+            carried = attention_part([0, half_tiles])
+            attn_mine.pop()
     shared = pack_sums(place, sums_one, sums_two, score_part)
     shared_came = core_swap(shared)
     seg_row = after(seg_row, shared)
-    carried = attention_part(list(range(1, tiles)))
+    carried = attention_part([1, half_tiles + 1])
     qkv_grad, grad_out, pair_bias = carried
     grad_qkv = mul(x_rows, qkv_grad, TN).astype(low)
     bounds = piece_bounds(owned, 4)
@@ -1059,7 +1085,10 @@
                     local = after(local, travelling[k - 1])
                 if k == 0 and step in (2, 4):
                     local = after(local, small_came)
-                came = (came.astype(wide) + local.astype(wide)).astype(low)
+                if step in (2, 3, 4):
+                    came = add_low(came, [local])
+                else:
+                    came = (came.astype(wide) + local.astype(wide)).astype(low)
             travelling[k] = came
         if step >= dp_count - 2:
             continue
@@ -1078,14 +1107,12 @@
             mine_part = mul(late_grad[:half], w_qkv, NT)
         if step == 1:
             mine_part = after(mine_part, mark)
-            input_mixed = add_low(mine_part, other_part)
+            input_mixed = add_low(mine_part, [other_part])
             input_came = chip_swap(input_mixed)
         if step == 4:
             branch_zero = after(input_mixed, mark).astype(wide) + input_came.astype(wide)
             input_mine = (jnp.concatenate(first_grad, axis=0) + branch_zero).astype(low)
             input_other = core_swap(input_mine)
-        if step == 5:
-            input_grad = in_order(after(place, mark), [input_mine], [input_other])
     small = small + small_came
     while stride < dp_count:
         small = small + lax.ppermute(small, "dp", [(s, s ^ stride) for s in range(dp_count)])
@@ -1095,7 +1122,6 @@
     )
     local = [staged[(k + 1) * dp_count - 1] for k in range(piece_count)]
 
-    travelling[0], input_grad = lax.optimization_barrier((travelling[0], input_grad))
     owned_grad, first_new, second_new, master_new = optimize(
         travelling,
         local,
@@ -1106,6 +1132,7 @@
         basis_left,
         basis_right,
     )
+    input_grad = in_order(place, [input_mine], [input_other])
     small_values, master_new = lax.optimization_barrier((small_values, master_new))
     small_values = small_values.reshape(-1)
     return (

time: 308 us -> 301 us (0.977)
  waiting for transfers between devices: 130 us -> 119 us
    ppermute x9, waiting for transfers between devices: 62.5 us -> 42.2 us  [chip_swap(): return lax.ppermute(value, 'mp', chip_pairs)]
    ppermute x28, waiting for transfers between devices: 22 us -> 30.1 us  [body(): came = lax.ppermute(travelling[k], 'dp', routes[k % 2])]
    ppermute x21 -> x27, starting transfers between devices: 4.38 us -> 6.45 us  [core_swap(): return lax.ppermute(value, 'mp', core_pairs)]
    pallas_call x37 -> x49, Pallas kernels: 65.3 us -> 66 us  [vmem_call(): pl.pallas_call(kernel, in_specs=specs, out_specs=[vmem] * len(outs), out_...]
  transfers between devices with their start and end apart: 91 -> 97, of which waited for: 46 -> 50; matrix products, arithmetic and copies ran while one was open for 1% -> 1% of each run, Pallas kernels for 14% -> 17%
where the time goes in v2:
time: 301 us; the launch traced here: 297 us
  waiting for transfers between devices  119 us (40%)
  starting transfers between devices  89.5 us (30%)
  Pallas kernels  76.2 us (25%)
  matrix products  5.75 us (2%)
    pallas_call x49, Pallas kernels, vmem_call(): pl.pallas_call(kernel, in_specs=specs, out_specs=[vmem] * len(outs), out_...  66 us
    ppermute x9, waiting for transfers between devices, chip_swap(): return lax.ppermute(value, 'mp', chip_pairs)  42.2 us
    ppermute x28, starting transfers between devices, body(): came = lax.ppermute(travelling[k], 'dp', routes[k % 2])  33 us
    ppermute x28, waiting for transfers between devices, body(): arrived[k].append(lax.ppermute(arrived[k][-1], 'dp', routes[k % 2]))  31.6 us
    ppermute x28, waiting for transfers between devices, body(): came = lax.ppermute(travelling[k], 'dp', routes[k % 2])  30.1 us
    ppermute x28, starting transfers between devices, body(): arrived[k].append(lax.ppermute(arrived[k][-1], 'dp', routes[k % 2]))  29.9 us
    ppermute x9, starting transfers between devices, chip_swap(): return lax.ppermute(value, 'mp', chip_pairs)  12.1 us
    ppermute x2, waiting for transfers between devices, body(): mine = lax.ppermute(out_piece, 'dp', exchange)  9.86 us
  transfers between devices with their start and end apart: 97, of which 50 were waited for; matrix products, arithmetic and copies ran while one was open for 1% of the time, Pallas kernels for 17%

profile of v2, /device:TPU:0, one launch (start us, length us, event | category | flops | bytes accessed | tf_op | source)
XLA Modules:
  0.0 296.7 jit_solution(8205031755268279150)
XLA Ops:
  2.4 3.1 %collective-permute-start = (bf16[6,128,128]{2,1,0:T(8,128)(2,1)S(1)}, bf16[6,128,128]{2,1,0:T(8,128)(2,1)S(1)}, u32[]{:S(2)}, u32[]{:S(2)}) collective-permute-start(bf16[6,128,128]{2,1,0:T(8,128)(2,1)S(1)} %get-tuple-element.381.refs_0_), channel_id=1, source_target_pairs={{0,8},{8,16},{16,24},{24,28},{28,20},{20,12},{12,4},{4,0},{1,9},{9... | collective-permute-start | bytes 589832 | tf_op jit(solution)/shard_map/ppermute | solution.py:902
  7.7 3.5 %collective-permute-done.refs_1_ = bf16[6,128,128]{2,1,0:T(8,128)(2,1)S(1)} collective-permute-done((bf16[6,128,128]{2,1,0:T(8,128)(2,1)S(1)}, bf16[6,128,128]{2,1,0:T(8,128)(2,1)S(1)}, u32[]{:S(2)}, u32[]{:S(2)}) %collective-permute-start) | collective-permute-done | bytes 196640 | tf_op jit(solution)/shard_map/ppermute | solution.py:902
  66.6 3.2 %assemble.1 = (bf16[1024,768]{1,0:T(8,128)(2,1)S(1)}, bf16[256,1024]{1,0:T(8,128)(2,1)S(1)}, bf16[1024,1024]{1,0:T(8,128)(2,1)S(1)}, bf16[1024,1024]{1,0:T(8,128)(2,1)S(1)}) custom-call(s32[6]{0:T(128)S(1)} %stack.31.place_ref, s32[192]{0:T(256)S(1)} %bitcast.17, bf16[6,128,128]{2,1,0:T(8,128)(2,1)S(1)} %get-tuple-element.381.refs_0_, ...), custom_call_target="tpu_custom_call" | custom-call | bytes 1024 | tf_op jit(solution)/shard_map/assemble/pallas_call | solution.py:76
  71.6 3.3 %attention_tile.4 = (bf16[256,256]{1,0:T(8,128)(2,1)S(1)}, f32[4,256]{1,0:T(4,128)S(1)}, bf16[128,1024]{1,0:T(8,128)(2,1)S(1)}, bf16[128,1024]{1,0:T(8,128)(2,1)S(1)}) custom-call(bf16[1024,768]{1,0:T(8,128)(2,1)S(1)} %add_convert_fusion.qkv_ref, bf16[256,1024]{1,0:T(8,128)(2,1)S(1)} %get-tuple-element.201.w_ref, ...), custom_call_target="tpu_custom_call" | custom-call | bytes 1024 | tf_op jit(solution)/shard_map/attention_tile/pallas_call | solution.py:76
  75.5 3.3 %attention_tile.5 = (bf16[256,256]{1,0:T(8,128)(2,1)S(1)}, f32[4,256]{1,0:T(4,128)S(1)}, f32[256,1024]{1,0:T(8,128)S(1)}) custom-call(bf16[1024,768]{1,0:T(8,128)(2,1)S(1)} %add_convert_fusion.qkv_ref, bf16[256,1024]{1,0:T(8,128)(2,1)S(1)} %get-tuple-element.201.w_ref, f32[1024,8]{1,0:T(8,128)S(1)} %get-tuple-element.202.sk_ref.table_ref, ...), custom_call_target="tpu_custom_call" | custom-call | bytes 1024 | tf_op jit(solution)/shard_map/attention_tile/pallas_call | solution.py:76
  78.9 3.3 %attention_tile.6 = (bf16[256,256]{1,0:T(8,128)(2,1)S(1)}, f32[4,256]{1,0:T(4,128)S(1)}, bf16[128,1024]{1,0:T(8,128)(2,1)S(1)}, bf16[128,1024]{1,0:T(8,128)(2,1)S(1)}) custom-call(bf16[1024,768]{1,0:T(8,128)(2,1)S(1)} %add_convert_fusion.qkv_ref, bf16[256,1024]{1,0:T(8,128)(2,1)S(1)} %get-tuple-element.201.w_ref, ...), custom_call_target="tpu_custom_call" | custom-call | bytes 1024 | tf_op jit(solution)/shard_map/attention_tile/pallas_call | solution.py:76
  84.3 3.5 %attention_tile.7 = (bf16[256,256]{1,0:T(8,128)(2,1)S(1)}, f32[4,256]{1,0:T(4,128)S(1)}, f32[256,1024]{1,0:T(8,128)S(1)}) custom-call(bf16[1024,768]{1,0:T(8,128)(2,1)S(1)} %add_convert_fusion.qkv_ref, bf16[256,1024]{1,0:T(8,128)(2,1)S(1)} %get-tuple-element.201.w_ref, f32[1024,8]{1,0:T(8,128)S(1)} %get-tuple-element.202.sk_ref.table_ref, ...), custom_call_target="tpu_custom_call" | custom-call | bytes 1024 | tf_op jit(solution)/shard_map/attention_tile/pallas_call | solution.py:76
  88.6 9.0 %collective-permute-done.30.b_ref = bf16[256,1024]{1,0:T(8,128)(2,1)S(1)} collective-permute-done((bf16[256,1024]{1,0:T(8,128)(2,1)S(1)}, bf16[256,1024]{1,0:T(8,128)(2,1)S(1)}, u32[]{:S(2)}, u32[]{:S(2)}) %collective-permute-start.30) | collective-permute-done | bytes 524320 | tf_op jit(solution)/shard_map/ppermute | solution.py:871
  102.4 5.5 %collective-permute-done.33.b_ref = bf16[256,1024]{1,0:T(8,128)(2,1)S(1)} collective-permute-done((bf16[256,1024]{1,0:T(8,128)(2,1)S(1)}, bf16[256,1024]{1,0:T(8,128)(2,1)S(1)}, u32[]{:S(2)}, u32[]{:S(2)}) %collective-permute-start.33) | collective-permute-done | bytes 524320 | tf_op jit(solution)/shard_map/ppermute | solution.py:871
  116.6 11.7 %collective-permute-done.39.b_ref = bf16[256,1024]{1,0:T(8,128)(2,1)S(1)} collective-permute-done((bf16[256,1024]{1,0:T(8,128)(2,1)S(1)}, bf16[256,1024]{1,0:T(8,128)(2,1)S(1)}, u32[]{:S(2)}, u32[]{:S(2)}) %collective-permute-start.39) | collective-permute-done | bytes 524320 | tf_op jit(solution)/shard_map/ppermute | solution.py:871
  132.1 6.6 %collective-permute-done.41.b_ref = bf16[256,1024]{1,0:T(8,128)(2,1)S(1)} collective-permute-done((bf16[256,1024]{1,0:T(8,128)(2,1)S(1)}, bf16[256,1024]{1,0:T(8,128)(2,1)S(1)}, u32[]{:S(2)}, u32[]{:S(2)}) %collective-permute-start.41) | collective-permute-done | bytes 524320 | tf_op jit(solution)/shard_map/ppermute | solution.py:871
  139.8 2.7 collective-permute-start.44
  144.1 9.7 %collective-permute-done.44.refs_9_ = bf16[128,1024]{1,0:T(8,128)(2,1)S(1)} collective-permute-done((bf16[128,1024]{1,0:T(8,128)(2,1)S(1)}, bf16[128,1024]{1,0:T(8,128)(2,1)S(1)}, u32[]{:S(2)}, u32[]{:S(2)}) %collective-permute-start.44) | collective-permute-done | bytes 262176 | tf_op jit(solution)/shard_map/ppermute | solution.py:981
  155.9 5.1 %collective-permute-done.45.refs_10_ = bf16[128,1024]{1,0:T(8,128)(2,1)S(1)} collective-permute-done((bf16[128,1024]{1,0:T(8,128)(2,1)S(1)}, bf16[128,1024]{1,0:T(8,128)(2,1)S(1)}, u32[]{:S(2)}, u32[]{:S(2)}) %collective-permute-start.45) | collective-permute-done | bytes 262176 | tf_op jit(solution)/shard_map/ppermute | solution.py:871
  162.6 3.6 %link_back.1 = (f32[256,1024]{1,0:T(8,128)S(1)}, f32[256,1024]{1,0:T(8,128)S(1)}, bf16[256,1024]{1,0:T(8,128)(2,1)S(1)}, bf16[256,1024]{1,0:T(8,128)(2,1)S(1)}, ...) custom-call(s32[6]{0:T(128)S(1)} %stack.31.place_ref, bf16[512,1024]{1,0:T(8,128)(2,1)S(1)} %get-tuple-element.228.link_ref, ...), custom_call_target="tpu_custom_call" | custom-call | bytes 1024 | tf_op jit(solution)/shard_map/link_back/pallas_call | solution.py:76
  178.0 4.5 %feed_grads.1 = (bf16[1024,1024]{1,0:T(8,128)(2,1)S(1)}, bf16[1024,1024]{1,0:T(8,128)(2,1)S(1)}, f32[1,1024]{1,0:T(1,128)S(1)}) custom-call(bf16[256,1024]{1,0:T(8,128)(2,1)S(1)} %get-tuple-element.216.refs_0_, bf16[256,1024]{1,0:T(8,128)(2,1)S(1)} %get-tuple-element.223.refs_1_, bf16[256,1024]{1,0:T(8,128)(2,1)S(1)} %get-tuple-element.224.refs_2_, ...), custom_call_target="tpu_custom_call" | custom-call | bytes 1024 | tf_op jit(solution)/shard_map/feed_grads/pallas_call | solution.py:76
  184.9 3.3 %collective-permute-done.56.b_ref = bf16[256,1024]{1,0:T(8,128)(2,1)S(1)} collective-permute-done((bf16[256,1024]{1,0:T(8,128)(2,1)S(1)}, bf16[256,1024]{1,0:T(8,128)(2,1)S(1)}, u32[]{:S(2)}, u32[]{:S(2)}) %collective-permute-start.56) | collective-permute-done | bytes 524320 | tf_op jit(solution)/shard_map/ppermute | solution.py:871
  191.0 6.7 %attention_backward.2 = (bf16[512,256]{1,0:T(8,128)(2,1)S(1)}, f32[1024,256]{1,0:T(8,128)S(1)}, f32[1024,256]{1,0:T(8,128)S(1)}, f32[256,1024]{1,0:T(8,128)S(1)}, f32[1,256]{1,0:T(1,128)S(1)}) custom-call(bf16[1024,768]{1,0:T(8,128)(2,1)S(1)} %add_convert_fusion.qkv_ref, bf16[256,1024]{1,0:T(8,128)(2,1)S(1)} %get-tuple-element.201.w_ref, ...), custom_call_target="tpu_custom_call" | custom-call | bytes 1024 | tf_op jit(solution)/shard_map/attention_backward/pallas_call | solution.py:76
  201.4 7.1 %attention_backward.3 = (bf16[1024,768]{1,0:T(8,128)(2,1)S(1)}, bf16[256,1024]{1,0:T(8,128)(2,1)S(1)}, f32[1,512]{1,0:T(1,128)S(1)}) custom-call(bf16[1024,768]{1,0:T(8,128)(2,1)S(1)} %add_convert_fusion.qkv_ref, bf16[256,1024]{1,0:T(8,128)(2,1)S(1)} %get-tuple-element.201.w_ref, f32[1024,8]{1,0:T(8,128)S(1)} %get-tuple-element.202.sk_ref.table_ref, ...), custom_call_target="tpu_custom_call" | custom-call | bytes 1024 | tf_op jit(solution)/shard_map/attention_backward/pallas_call | solution.py:76
  216.7 3.7 %collective-permute-done.66 = bf16[6,128,128]{2,1,0:T(8,128)(2,1)S(1)} collective-permute-done((bf16[6,128,128]{2,1,0:T(8,128)(2,1)S(1)}, bf16[6,128,128]{2,1,0:T(8,128)(2,1)S(1)}, u32[]{:S(2)}, u32[]{:S(2)}) %collective-permute-start.66) | collective-permute-done | bytes 196640 | tf_op jit(solution)/shard_map/ppermute | solution.py:1081
  241.8 4.2 %collective-permute-done.74.a_ref = bf16[6,128,128]{2,1,0:T(8,128)(2,1)S(1)} collective-permute-done((bf16[6,128,128]{2,1,0:T(8,128)(2,1)S(1)}, bf16[6,128,128]{2,1,0:T(8,128)(2,1)S(1)}, u32[]{:S(2)}, u32[]{:S(2)}) %collective-permute-start.74) | collective-permute-done | bytes 196640 | tf_op jit(solution)/shard_map/ppermute | solution.py:1081
  277.9 2.8 collective-permute-start.92
  282.0 3.5 %collective-permute-done.96.refs_3_ = bf16[6,128,128]{2,1,0:T(8,128)(2,1)S(1)} collective-permute-done((bf16[6,128,128]{2,1,0:T(8,128)(2,1)S(1)}, bf16[6,128,128]{2,1,0:T(8,128)(2,1)S(1)}, u32[]{:S(2)}, u32[]{:S(2)}) %collective-permute-start.96) | collective-permute-done | bytes 196640 | tf_op jit(solution)/shard_map/ppermute | solution.py:1081
  287.6 6.3 %optimize.1 = (f32[24,128,128]{2,1,0:T(8,128)}, f32[24,128,128]{2,1,0:T(8,128)}, f32[24,128,128]{2,1,0:T(8,128)}, f32[24,128,128]{2,1,0:T(8,128)}) custom-call(bf16[6,128,128]{2,1,0:T(8,128)(2,1)S(1)} %collective-permute-done.90.refs_0_, bf16[6,128,128]{2,1,0:T(8,128)(2,1)S(1)} %collective-permute-done.92.refs_1_, ...), custom_call_target="tpu_custom_call" | custom-call | bytes 1024 | tf_op jit(solution)/shard_map/optimize/pallas_call | solution.py:379
  (283 shorter events, 175.9 us)
Async XLA Ops:
  5.5 9.9 %collective-permute-start.14 = (bf16[6,128,128]{2,1,0:T(8,128)(2,1)S(1)}, bf16[6,128,128]{2,1,0:T(8,128)(2,1)S(1)}, u32[]{:S(2)}, u32[]{:S(2)}) collective-permute-start(bf16[6,128,128]{2,1,0:T(8,128)(2,1)S(1)} %get-tuple-element.379.refs_16_), channel_id=1, source_target_pairs={{0,8},{8,16},{16,24},{24,28},{28,20},{20,12},{12,4},{4,0},{1,9},{9... | collective-permute-start | bytes 589832 | tf_op jit(solution)/shard_map/ppermute | solution.py:902
  7.5 10.1 %collective-permute-start.21 = (bf16[6,128,128]{2,1,0:T(8,128)(2,1)S(1)}, bf16[6,128,128]{2,1,0:T(8,128)(2,1)}, u32[]{:S(2)}, u32[]{:S(2)}) collective-permute-start(bf16[6,128,128]{2,1,0:T(8,128)(2,1)S(1)} %get-tuple-element.378.refs_24_), channel_id=1, source_target_pairs={{8,0},{16,8},{24,16},{28,24},{20,28},{12,20},{4,12},{0,4},{9,1},{1... | collective-permute-start | bytes 589832 | tf_op jit(solution)/shard_map/ppermute | solution.py:902
  11.2 9.0 %collective-permute-start.1 = (bf16[6,128,128]{2,1,0:T(8,128)(2,1)S(1)}, bf16[6,128,128]{2,1,0:T(8,128)(2,1)}, u32[]{:S(2)}, u32[]{:S(2)}) collective-permute-start(bf16[6,128,128]{2,1,0:T(8,128)(2,1)S(1)} %collective-permute-done.refs_1_), channel_id=1, source_target_pairs={{0,8},{8,16},{16,24},{24,28},{28,20},{20,12},{12,4},{4,0},{1,9},{9... | collective-permute-start | bytes 589832 | tf_op jit(solution)/shard_map/ppermute | solution.py:902
  82.8 14.8 %collective-permute-start.30 = (bf16[256,1024]{1,0:T(8,128)(2,1)S(1)}, bf16[256,1024]{1,0:T(8,128)(2,1)S(1)}, u32[]{:S(2)}, u32[]{:S(2)}) collective-permute-start(bf16[256,1024]{1,0:T(8,128)(2,1)S(1)} %add_low.19.a_ref), channel_id=1, source_target_pairs={{0,2},{1,3},{2,0},{3,1},{4,6},{5,7},{6,4},{7,5},{8,10},{9,11},{10,... | collective-permute-start | bytes 1572872 | tf_op jit(solution)/shard_map/ppermute | solution.py:871
  87.9 20.0 %collective-permute-start.33 = (bf16[256,1024]{1,0:T(8,128)(2,1)S(1)}, bf16[256,1024]{1,0:T(8,128)(2,1)S(1)}, u32[]{:S(2)}, u32[]{:S(2)}) collective-permute-start(bf16[256,1024]{1,0:T(8,128)(2,1)S(1)} %add_low.20.a_ref), channel_id=1, source_target_pairs={{0,2},{1,3},{2,0},{3,1},{4,6},{5,7},{6,4},{7,5},{8,10},{9,11},{10,... | collective-permute-start | bytes 1572872 | tf_op jit(solution)/shard_map/ppermute | solution.py:871
  113.5 14.8 %collective-permute-start.39 = (bf16[256,1024]{1,0:T(8,128)(2,1)S(1)}, bf16[256,1024]{1,0:T(8,128)(2,1)S(1)}, u32[]{:S(2)}, u32[]{:S(2)}) collective-permute-start(bf16[256,1024]{1,0:T(8,128)(2,1)S(1)} %add_low.21.a_ref), channel_id=1, source_target_pairs={{0,2},{1,3},{2,0},{3,1},{4,6},{5,7},{6,4},{7,5},{8,10},{9,11},{10,... | collective-permute-start | bytes 1572872 | tf_op jit(solution)/shard_map/ppermute | solution.py:871
  115.2 23.5 %collective-permute-start.41 = (bf16[256,1024]{1,0:T(8,128)(2,1)S(1)}, bf16[256,1024]{1,0:T(8,128)(2,1)S(1)}, u32[]{:S(2)}, u32[]{:S(2)}) collective-permute-start(bf16[256,1024]{1,0:T(8,128)(2,1)S(1)} %add_low.22.a_ref), channel_id=1, source_target_pairs={{0,2},{1,3},{2,0},{3,1},{4,6},{5,7},{6,4},{7,5},{8,10},{9,11},{10,... | collective-permute-start | bytes 1572872 | tf_op jit(solution)/shard_map/ppermute | solution.py:871
  129.5 13.1 %collective-permute-start.42 = (bf16[128,1024]{1,0:T(8,128)(2,1)S(1)}, bf16[128,1024]{1,0:T(8,128)(2,1)S(1)}, u32[]{:S(2)}, u32[]{:S(2)}) collective-permute-start(bf16[128,1024]{1,0:T(8,128)(2,1)S(1)} %get-tuple-element.238), channel_id=1, source_target_pairs={{0,16},{4,20},{8,24},{12,28},{16,0},{20,4},{24,8},{28,12},{1,17},{... | collective-permute-start | bytes 786440 | tf_op jit(solution)/shard_map/ppermute | solution.py:981
  139.8 14.0 %collective-permute-start.44 = (bf16[128,1024]{1,0:T(8,128)(2,1)S(1)}, bf16[128,1024]{1,0:T(8,128)(2,1)S(1)}, u32[]{:S(2)}, u32[]{:S(2)}) collective-permute-start(bf16[128,1024]{1,0:T(8,128)(2,1)S(1)} %get-tuple-element.239), channel_id=1, source_target_pairs={{0,16},{4,20},{8,24},{12,28},{16,0},{20,4},{24,8},{28,12},{1,17},{... | collective-permute-start | bytes 786440 | tf_op jit(solution)/shard_map/ppermute | solution.py:981
  142.6 13.3 %collective-permute-start.43 = (bf16[128,1024]{1,0:T(8,128)(2,1)S(1)}, bf16[128,1024]{1,0:T(8,128)(2,1)S(1)}, u32[]{:S(2)}, u32[]{:S(2)}) collective-permute-start(bf16[128,1024]{1,0:T(8,128)(2,1)S(1)} %collective-permute-done.42.refs_7_), channel_id=1, source_target_pairs={{0,2},{1,3},{2,0},{3,1},{4,6},{5,7},{6,4},{7,5},{8,10},{9,11},{10,... | collective-permute-start | bytes 786440 | tf_op jit(solution)/shard_map/ppermute | solution.py:871
  173.3 14.8 %collective-permute-start.56 = (bf16[256,1024]{1,0:T(8,128)(2,1)S(1)}, bf16[256,1024]{1,0:T(8,128)(2,1)S(1)}, u32[]{:S(2)}, u32[]{:S(2)}) collective-permute-start(bf16[256,1024]{1,0:T(8,128)(2,1)S(1)} %add_low.24.a_ref), channel_id=1, source_target_pairs={{0,2},{1,3},{2,0},{3,1},{4,6},{5,7},{6,4},{7,5},{8,10},{9,11},{10,... | collective-permute-start | bytes 1572872 | tf_op jit(solution)/shard_map/ppermute | solution.py:871
  175.0 23.6 %collective-permute-start.57 = (bf16[256,1024]{1,0:T(8,128)(2,1)S(1)}, bf16[256,1024]{1,0:T(8,128)(2,1)S(1)}, u32[]{:S(2)}, u32[]{:S(2)}) collective-permute-start(bf16[256,1024]{1,0:T(8,128)(2,1)S(1)} %add_low.23.a_ref), channel_id=1, source_target_pairs={{0,2},{1,3},{2,0},{3,1},{4,6},{5,7},{6,4},{7,5},{8,10},{9,11},{10,... | collective-permute-start | bytes 1572872 | tf_op jit(solution)/shard_map/ppermute | solution.py:871
  214.6 9.9 %collective-permute-start.64 = (bf16[6,128,128]{2,1,0:T(8,128)(2,1)S(1)}, bf16[6,128,128]{2,1,0:T(8,128)(2,1)S(1)}, u32[]{:S(2)}, u32[]{:S(2)}) collective-permute-start(bf16[6,128,128]{2,1,0:T(8,128)(2,1)S(1)} %get-tuple-element.300), channel_id=1, source_target_pairs={{0,8},{8,16},{16,24},{24,28},{28,20},{20,12},{12,4},{4,0},{1,9},{9... | collective-permute-start | bytes 589832 | tf_op jit(solution)/shard_map/ppermute | solution.py:1081
  216.4 10.0 %collective-permute-start.63 = (bf16[6,128,128]{2,1,0:T(8,128)(2,1)S(1)}, bf16[6,128,128]{2,1,0:T(8,128)(2,1)S(1)}, u32[]{:S(2)}, u32[]{:S(2)}) collective-permute-start(bf16[6,128,128]{2,1,0:T(8,128)(2,1)S(1)} %get-tuple-element.298), channel_id=1, source_target_pairs={{8,0},{16,8},{24,16},{28,24},{20,28},{12,20},{4,12},{0,4},{9,1},{1... | collective-permute-start | bytes 589832 | tf_op jit(solution)/shard_map/ppermute | solution.py:1081
  234.1 37.6 %collective-permute-start.87 = (bf16[512,1024]{1,0:T(8,128)(2,1)S(1)}, bf16[512,1024]{1,0:T(8,128)(2,1)S(1)}, u32[]{:S(2)}, u32[]{:S(2)}) collective-permute-start(bf16[512,1024]{1,0:T(8,128)(2,1)S(1)} %add_low.37), channel_id=1, source_target_pairs={{0,2},{1,3},{2,0},{3,1},{4,6},{5,7},{6,4},{7,5},{8,10},{9,11},{10,... | collective-permute-start | bytes 3145736 | tf_op jit(solution)/shard_map/ppermute | solution.py:871
  237.2 8.9 %collective-permute-start.74 = (bf16[6,128,128]{2,1,0:T(8,128)(2,1)S(1)}, bf16[6,128,128]{2,1,0:T(8,128)(2,1)S(1)}, u32[]{:S(2)}, u32[]{:S(2)}) collective-permute-start(bf16[6,128,128]{2,1,0:T(8,128)(2,1)S(1)} %add_convert_fusion.8), channel_id=1, source_target_pairs={{0,8},{8,16},{16,24},{24,28},{28,20},{20,12},{12,4},{4,0},{1,9},{9... | collective-permute-start | bytes 589832 | tf_op jit(solution)/shard_map/ppermute | solution.py:1081
  239.2 11.1 %collective-permute-start.72 = (bf16[6,128,128]{2,1,0:T(8,128)(2,1)S(1)}, bf16[6,128,128]{2,1,0:T(8,128)(2,1)S(1)}, u32[]{:S(2)}, u32[]{:S(2)}) collective-permute-start(bf16[6,128,128]{2,1,0:T(8,128)(2,1)S(1)} %add_convert_fusion.6), channel_id=1, source_target_pairs={{0,8},{8,16},{16,24},{24,28},{28,20},{20,12},{12,4},{4,0},{1,9},{9... | collective-permute-start | bytes 589832 | tf_op jit(solution)/shard_map/ppermute | solution.py:1081
  241.8 9.4 %collective-permute-start.71 = (bf16[6,128,128]{2,1,0:T(8,128)(2,1)S(1)}, bf16[6,128,128]{2,1,0:T(8,128)(2,1)S(1)}, u32[]{:S(2)}, u32[]{:S(2)}) collective-permute-start(bf16[6,128,128]{2,1,0:T(8,128)(2,1)S(1)} %add_convert_fusion.5), channel_id=1, source_target_pairs={{8,0},{16,8},{24,16},{28,24},{20,28},{12,20},{4,12},{0,4},{9,1},{1... | collective-permute-start | bytes 589832 | tf_op jit(solution)/shard_map/ppermute | solution.py:1081
  260.9 9.4 %collective-permute-start.80 = (bf16[6,128,128]{2,1,0:T(8,128)(2,1)S(1)}, bf16[6,128,128]{2,1,0:T(8,128)(2,1)S(1)}, u32[]{:S(2)}, u32[]{:S(2)}) collective-permute-start(bf16[6,128,128]{2,1,0:T(8,128)(2,1)S(1)} %add_low.32), channel_id=1, source_target_pairs={{8,0},{16,8},{24,16},{28,24},{20,28},{12,20},{4,12},{0,4},{9,1},{1... | collective-permute-start | bytes 589832 | tf_op jit(solution)/shard_map/ppermute | solution.py:1081
  263.3 10.5 %collective-permute-start.89 = (bf16[6,128,128]{2,1,0:T(8,128)(2,1)S(1)}, bf16[6,128,128]{2,1,0:T(8,128)(2,1)S(1)}, u32[]{:S(2)}, u32[]{:S(2)}) collective-permute-start(bf16[6,128,128]{2,1,0:T(8,128)(2,1)S(1)} %add_low.33), channel_id=1, source_target_pairs={{0,8},{8,16},{16,24},{24,28},{28,20},{20,12},{12,4},{4,0},{1,9},{9... | collective-permute-start | bytes 589832 | tf_op jit(solution)/shard_map/ppermute | solution.py:1081
  271.6 9.1 %collective-permute-start.85 = (f32[16,1024]{1,0:T(8,128)S(1)}, f32[16,1024]{1,0:T(8,128)S(1)}, u32[]{:S(2)}, u32[]{:S(2)}) collective-permute-start(f32[16,1024]{1,0:T(8,128)S(1)} %add.85), channel_id=1, source_target_pairs={{0,16},{4,20},{8,24},{12,28},{16,0},{20,4},{24,8},{28,12},{1,17},{... | collective-permute-start | bytes 196616 | tf_op jit(solution)/shard_map/ppermute | solution.py:1102
  273.8 20.7 %collective-permute-start.88 = (bf16[512,1024]{1,0:T(8,128)(2,1)S(1)}, bf16[512,1024]{1,0:T(8,128)(2,1)S(1)}, u32[]{:S(2)}, u32[]{:S(2)}) collective-permute-start(bf16[512,1024]{1,0:T(8,128)(2,1)S(1)} %fusion.refs_0_), channel_id=1, source_target_pairs={{0,1},{1,0},{2,3},{3,2},{4,5},{5,4},{6,7},{7,6},{8,9},{9,8},{10,11... | collective-permute-start | bytes 3145736 | tf_op jit(solution)/shard_map/ppermute | solution.py:868
  275.3 10.2 %collective-permute-start.94 = (bf16[6,128,128]{2,1,0:T(8,128)(2,1)S(1)}, bf16[6,128,128]{2,1,0:T(8,128)(2,1)S(1)}, u32[]{:S(2)}, u32[]{:S(2)}) collective-permute-start(bf16[6,128,128]{2,1,0:T(8,128)(2,1)S(1)} %add_convert_fusion.2), channel_id=1, source_target_pairs={{0,8},{8,16},{16,24},{24,28},{28,20},{20,12},{12,4},{4,0},{1,9},{9... | collective-permute-start | bytes 589832 | tf_op jit(solution)/shard_map/ppermute | solution.py:1081
  277.9 9.6 %collective-permute-start.92 = (bf16[6,128,128]{2,1,0:T(8,128)(2,1)S(1)}, bf16[6,128,128]{2,1,0:T(8,128)(2,1)S(1)}, u32[]{:S(2)}, u32[]{:S(2)}) collective-permute-start(bf16[6,128,128]{2,1,0:T(8,128)(2,1)S(1)} %add_convert_fusion.3), channel_id=1, source_target_pairs={{8,0},{16,8},{24,16},{28,24},{20,28},{12,20},{4,12},{0,4},{9,1},{1... | collective-permute-start | bytes 589832 | tf_op jit(solution)/shard_map/ppermute | solution.py:1081
  (88 other events, 608.9 us)

commit v3 on v2

--- a/solution.py
+++ b/solution.py
@@ -930,7 +930,7 @@
         for t in (half_tiles + k, k):
             own = t < half_tiles
             context[t], lse[t], *part = attention_tile(
-                qkv, w_out, seg_column, row, t, wide if own else low, 1 if own else 2
+                qkv, w_out, seg_column, row, t, wide if own else low, 1 if own else 2 + 2 * k
             )
             if not own:
                 sent = [core_swap(value) for value in part]
@@ -1122,6 +1122,8 @@
     )
     local = [staged[(k + 1) * dp_count - 1] for k in range(piece_count)]
 
+    input_grad = in_order(place, [input_mine], [input_other])
+    travelling[0] = after(travelling[0], input_grad)
     owned_grad, first_new, second_new, master_new = optimize(
         travelling,
         local,
@@ -1132,7 +1134,6 @@
         basis_left,
         basis_right,
     )
-    input_grad = in_order(place, [input_mine], [input_other])
     small_values, master_new = lax.optimization_barrier((small_values, master_new))
     small_values = small_values.reshape(-1)
     return (

time: 301 us -> 295 us (0.980)
  waiting for transfers between devices: 119 us -> 114 us
    ppermute x9, waiting for transfers between devices: 42.2 us -> 37.7 us  [chip_swap(): return lax.ppermute(value, 'mp', chip_pairs)]
    ppermute x27 -> x29, starting transfers between devices: 6.45 us -> 6.94 us  [core_swap(): return lax.ppermute(value, 'mp', core_pairs)]
  transfers between devices with their start and end apart: 97 -> 99, of which waited for: 50 -> 51; matrix products, arithmetic and copies ran while one was open for 1% -> 1% of each run, Pallas kernels for 17% -> 17%
where the time goes in v3:
time: 295 us; the launch traced here: 291 us
  waiting for transfers between devices  114 us (39%)
  starting transfers between devices  88.6 us (30%)
  Pallas kernels  76.3 us (26%)
  matrix products  5.74 us (2%)
  other arithmetic  2.97 us (1%)
    pallas_call x49, Pallas kernels, vmem_call(): pl.pallas_call(kernel, in_specs=specs, out_specs=[vmem] * len(outs), out_...  66.1 us
    ppermute x9, waiting for transfers between devices, chip_swap(): return lax.ppermute(value, 'mp', chip_pairs)  37.7 us
    ppermute x28, waiting for transfers between devices, body(): arrived[k].append(lax.ppermute(arrived[k][-1], 'dp', routes[k % 2]))  31.6 us
    ppermute x28, starting transfers between devices, body(): came = lax.ppermute(travelling[k], 'dp', routes[k % 2])  31.5 us
    ppermute x28, starting transfers between devices, body(): arrived[k].append(lax.ppermute(arrived[k][-1], 'dp', routes[k % 2]))  29.9 us
    ppermute x28, waiting for transfers between devices, body(): came = lax.ppermute(travelling[k], 'dp', routes[k % 2])  27.8 us
    ppermute x9, starting transfers between devices, chip_swap(): return lax.ppermute(value, 'mp', chip_pairs)  12.1 us
    ppermute x2, waiting for transfers between devices, body(): mine = lax.ppermute(out_piece, 'dp', exchange)  9.88 us
  transfers between devices with their start and end apart: 99, of which 51 were waited for; matrix products, arithmetic and copies ran while one was open for 1% of the time, Pallas kernels for 17%

profile of v3, /device:TPU:0, one launch (start us, length us, event | category | flops | bytes accessed | tf_op | source)
XLA Modules:
  0.0 290.9 jit_solution(14906072736389804508)
XLA Ops:
  2.4 3.1 %collective-permute-start = (bf16[6,128,128]{2,1,0:T(8,128)(2,1)S(1)}, bf16[6,128,128]{2,1,0:T(8,128)(2,1)S(1)}, u32[]{:S(2)}, u32[]{:S(2)}) collective-permute-start(bf16[6,128,128]{2,1,0:T(8,128)(2,1)S(1)} %get-tuple-element.387.refs_0_), channel_id=1, source_target_pairs={{0,8},{8,16},{16,24},{24,28},{28,20},{20,12},{12,4},{4,0},{1,9},{9... | collective-permute-start | bytes 589832 | tf_op jit(solution)/shard_map/ppermute | solution.py:902
  7.7 3.5 %collective-permute-done.refs_1_ = bf16[6,128,128]{2,1,0:T(8,128)(2,1)S(1)} collective-permute-done((bf16[6,128,128]{2,1,0:T(8,128)(2,1)S(1)}, bf16[6,128,128]{2,1,0:T(8,128)(2,1)S(1)}, u32[]{:S(2)}, u32[]{:S(2)}) %collective-permute-start) | collective-permute-done | bytes 196640 | tf_op jit(solution)/shard_map/ppermute | solution.py:902
  66.6 3.2 %assemble.1 = (bf16[1024,768]{1,0:T(8,128)(2,1)S(1)}, bf16[256,1024]{1,0:T(8,128)(2,1)S(1)}, bf16[1024,1024]{1,0:T(8,128)(2,1)S(1)}, bf16[1024,1024]{1,0:T(8,128)(2,1)S(1)}) custom-call(s32[6]{0:T(128)S(1)} %stack.31.place_ref, s32[192]{0:T(256)S(1)} %bitcast.17, bf16[6,128,128]{2,1,0:T(8,128)(2,1)S(1)} %get-tuple-element.387.refs_0_, ...), custom_call_target="tpu_custom_call" | custom-call | bytes 1024 | tf_op jit(solution)/shard_map/assemble/pallas_call | solution.py:76
  71.6 3.3 %attention_tile.4 = (bf16[256,256]{1,0:T(8,128)(2,1)S(1)}, f32[4,256]{1,0:T(4,128)S(1)}, bf16[128,1024]{1,0:T(8,128)(2,1)S(1)}, bf16[128,1024]{1,0:T(8,128)(2,1)S(1)}) custom-call(bf16[1024,768]{1,0:T(8,128)(2,1)S(1)} %add_convert_fusion.qkv_ref, bf16[256,1024]{1,0:T(8,128)(2,1)S(1)} %get-tuple-element.204.w_ref, ...), custom_call_target="tpu_custom_call" | custom-call | bytes 1024 | tf_op jit(solution)/shard_map/attention_tile/pallas_call | solution.py:76
  75.5 3.3 %attention_tile.5 = (bf16[256,256]{1,0:T(8,128)(2,1)S(1)}, f32[4,256]{1,0:T(4,128)S(1)}, f32[256,1024]{1,0:T(8,128)S(1)}) custom-call(bf16[1024,768]{1,0:T(8,128)(2,1)S(1)} %add_convert_fusion.qkv_ref, bf16[256,1024]{1,0:T(8,128)(2,1)S(1)} %get-tuple-element.204.w_ref, f32[1024,8]{1,0:T(8,128)S(1)} %get-tuple-element.205.sk_ref.table_ref, ...), custom_call_target="tpu_custom_call" | custom-call | bytes 1024 | tf_op jit(solution)/shard_map/attention_tile/pallas_call | solution.py:76
  80.5 3.3 %attention_tile.6 = (bf16[256,256]{1,0:T(8,128)(2,1)S(1)}, f32[4,256]{1,0:T(4,128)S(1)}, bf16[64,1024]{1,0:T(8,128)(2,1)S(1)}, bf16[64,1024]{1,0:T(8,128)(2,1)S(...) custom-call(bf16[1024,768]{1,0:T(8,128)(2,1)S(1)} %add_convert_fusion.qkv_ref, ...), custom_call_target="tpu_custom_call" | custom-call | bytes 1024 | tf_op jit(solution)/shard_map/attention_tile/pallas_call | solution.py:76
  84.9 3.7 %attention_tile.7 = (bf16[256,256]{1,0:T(8,128)(2,1)S(1)}, f32[4,256]{1,0:T(4,128)S(1)}, f32[256,1024]{1,0:T(8,128)S(1)}) custom-call(bf16[1024,768]{1,0:T(8,128)(2,1)S(1)} %add_convert_fusion.qkv_ref, bf16[256,1024]{1,0:T(8,128)(2,1)S(1)} %get-tuple-element.204.w_ref, f32[1024,8]{1,0:T(8,128)S(1)} %get-tuple-element.205.sk_ref.table_ref, ...), custom_call_target="tpu_custom_call" | custom-call | bytes 1024 | tf_op jit(solution)/shard_map/attention_tile/pallas_call | solution.py:76
  89.4 4.4 %collective-permute-done.30.b_ref = bf16[256,1024]{1,0:T(8,128)(2,1)S(1)} collective-permute-done((bf16[256,1024]{1,0:T(8,128)(2,1)S(1)}, bf16[256,1024]{1,0:T(8,128)(2,1)S(1)}, u32[]{:S(2)}, u32[]{:S(2)}) %collective-permute-start.30) | collective-permute-done | bytes 524320 | tf_op jit(solution)/shard_map/ppermute | solution.py:871
  98.6 5.5 %collective-permute-done.35.b_ref = bf16[256,1024]{1,0:T(8,128)(2,1)S(1)} collective-permute-done((bf16[256,1024]{1,0:T(8,128)(2,1)S(1)}, bf16[256,1024]{1,0:T(8,128)(2,1)S(1)}, u32[]{:S(2)}, u32[]{:S(2)}) %collective-permute-start.35) | collective-permute-done | bytes 524320 | tf_op jit(solution)/shard_map/ppermute | solution.py:871
  112.8 11.7 %collective-permute-done.41.b_ref = bf16[256,1024]{1,0:T(8,128)(2,1)S(1)} collective-permute-done((bf16[256,1024]{1,0:T(8,128)(2,1)S(1)}, bf16[256,1024]{1,0:T(8,128)(2,1)S(1)}, u32[]{:S(2)}, u32[]{:S(2)}) %collective-permute-start.41) | collective-permute-done | bytes 524320 | tf_op jit(solution)/shard_map/ppermute | solution.py:871
  125.7 2.7 collective-permute-start.44
  128.3 6.6 %collective-permute-done.43.b_ref = bf16[256,1024]{1,0:T(8,128)(2,1)S(1)} collective-permute-done((bf16[256,1024]{1,0:T(8,128)(2,1)S(1)}, bf16[256,1024]{1,0:T(8,128)(2,1)S(1)}, u32[]{:S(2)}, u32[]{:S(2)}) %collective-permute-start.43) | collective-permute-done | bytes 524320 | tf_op jit(solution)/shard_map/ppermute | solution.py:871
  136.0 2.7 collective-permute-start.46
  140.3 9.7 %collective-permute-done.46.refs_9_ = bf16[128,1024]{1,0:T(8,128)(2,1)S(1)} collective-permute-done((bf16[128,1024]{1,0:T(8,128)(2,1)S(1)}, bf16[128,1024]{1,0:T(8,128)(2,1)S(1)}, u32[]{:S(2)}, u32[]{:S(2)}) %collective-permute-start.46) | collective-permute-done | bytes 262176 | tf_op jit(solution)/shard_map/ppermute | solution.py:981
  152.1 5.2 %collective-permute-done.47.refs_10_ = bf16[128,1024]{1,0:T(8,128)(2,1)S(1)} collective-permute-done((bf16[128,1024]{1,0:T(8,128)(2,1)S(1)}, bf16[128,1024]{1,0:T(8,128)(2,1)S(1)}, u32[]{:S(2)}, u32[]{:S(2)}) %collective-permute-start.47) | collective-permute-done | bytes 262176 | tf_op jit(solution)/shard_map/ppermute | solution.py:871
  158.8 3.4 %link_back.1 = (f32[256,1024]{1,0:T(8,128)S(1)}, f32[256,1024]{1,0:T(8,128)S(1)}, bf16[256,1024]{1,0:T(8,128)(2,1)S(1)}, bf16[256,1024]{1,0:T(8,128)(2,1)S(1)}, ...) custom-call(s32[6]{0:T(128)S(1)} %stack.31.place_ref, bf16[512,1024]{1,0:T(8,128)(2,1)S(1)} %get-tuple-element.233.link_ref, ...), custom_call_target="tpu_custom_call" | custom-call | bytes 1024 | tf_op jit(solution)/shard_map/link_back/pallas_call | solution.py:76
  173.9 4.5 %feed_grads.1 = (bf16[1024,1024]{1,0:T(8,128)(2,1)S(1)}, bf16[1024,1024]{1,0:T(8,128)(2,1)S(1)}, f32[1,1024]{1,0:T(1,128)S(1)}) custom-call(bf16[256,1024]{1,0:T(8,128)(2,1)S(1)} %get-tuple-element.221.refs_0_, bf16[256,1024]{1,0:T(8,128)(2,1)S(1)} %get-tuple-element.228.refs_1_, bf16[256,1024]{1,0:T(8,128)(2,1)S(1)} %get-tuple-element.229.refs_2_, ...), custom_call_target="tpu_custom_call" | custom-call | bytes 1024 | tf_op jit(solution)/shard_map/feed_grads/pallas_call | solution.py:76
  178.5 2.4 rotate_first.1.refs_8_
  180.9 3.3 %collective-permute-done.58.b_ref = bf16[256,1024]{1,0:T(8,128)(2,1)S(1)} collective-permute-done((bf16[256,1024]{1,0:T(8,128)(2,1)S(1)}, bf16[256,1024]{1,0:T(8,128)(2,1)S(1)}, u32[]{:S(2)}, u32[]{:S(2)}) %collective-permute-start.58) | collective-permute-done | bytes 524320 | tf_op jit(solution)/shard_map/ppermute | solution.py:871
  187.0 6.7 %attention_backward.2 = (bf16[512,256]{1,0:T(8,128)(2,1)S(1)}, f32[1024,256]{1,0:T(8,128)S(1)}, f32[1024,256]{1,0:T(8,128)S(1)}, f32[256,1024]{1,0:T(8,128)S(1)}, f32[1,256]{1,0:T(1,128)S(1)}) custom-call(bf16[1024,768]{1,0:T(8,128)(2,1)S(1)} %add_convert_fusion.qkv_ref, bf16[256,1024]{1,0:T(8,128)(2,1)S(1)} %get-tuple-element.204.w_ref, ...), custom_call_target="tpu_custom_call" | custom-call | bytes 1024 | tf_op jit(solution)/shard_map/attention_backward/pallas_call | solution.py:76
  197.4 7.2 %attention_backward.3 = (bf16[1024,768]{1,0:T(8,128)(2,1)S(1)}, bf16[256,1024]{1,0:T(8,128)(2,1)S(1)}, f32[1,512]{1,0:T(1,128)S(1)}) custom-call(bf16[1024,768]{1,0:T(8,128)(2,1)S(1)} %add_convert_fusion.qkv_ref, bf16[256,1024]{1,0:T(8,128)(2,1)S(1)} %get-tuple-element.204.w_ref, f32[1024,8]{1,0:T(8,128)S(1)} %get-tuple-element.205.sk_ref.table_ref, ...), custom_call_target="tpu_custom_call" | custom-call | bytes 1024 | tf_op jit(solution)/shard_map/attention_backward/pallas_call | solution.py:76
  212.7 3.7 %collective-permute-done.68 = bf16[6,128,128]{2,1,0:T(8,128)(2,1)S(1)} collective-permute-done((bf16[6,128,128]{2,1,0:T(8,128)(2,1)S(1)}, bf16[6,128,128]{2,1,0:T(8,128)(2,1)S(1)}, u32[]{:S(2)}, u32[]{:S(2)}) %collective-permute-start.68) | collective-permute-done | bytes 196640 | tf_op jit(solution)/shard_map/ppermute | solution.py:1081
  237.8 4.2 %collective-permute-done.76.a_ref = bf16[6,128,128]{2,1,0:T(8,128)(2,1)S(1)} collective-permute-done((bf16[6,128,128]{2,1,0:T(8,128)(2,1)S(1)}, bf16[6,128,128]{2,1,0:T(8,128)(2,1)S(1)}, u32[]{:S(2)}, u32[]{:S(2)}) %collective-permute-start.76) | collective-permute-done | bytes 196640 | tf_op jit(solution)/shard_map/ppermute | solution.py:1081
  283.5 6.3 %optimize.1 = (f32[24,128,128]{2,1,0:T(8,128)}, f32[24,128,128]{2,1,0:T(8,128)}, f32[24,128,128]{2,1,0:T(8,128)}, f32[24,128,128]{2,1,0:T(8,128)}) custom-call(bf16[6,128,128]{2,1,0:T(8,128)(2,1)S(1)} %collective-permute-done.92.refs_0_, bf16[6,128,128]{2,1,0:T(8,128)(2,1)S(1)} %collective-permute-done.94.refs_1_, ...), custom_call_target="tpu_custom_call" | custom-call | bytes 1024 | tf_op jit(solution)/shard_map/optimize/pallas_call | solution.py:379
  (287 shorter events, 175.5 us)
Async XLA Ops:
  2.4 8.7 %collective-permute-start = (bf16[6,128,128]{2,1,0:T(8,128)(2,1)S(1)}, bf16[6,128,128]{2,1,0:T(8,128)(2,1)S(1)}, u32[]{:S(2)}, u32[]{:S(2)}) collective-permute-start(bf16[6,128,128]{2,1,0:T(8,128)(2,1)S(1)} %get-tuple-element.387.refs_0_), channel_id=1, source_target_pairs={{0,8},{8,16},{16,24},{24,28},{28,20},{20,12},{12,4},{4,0},{1,9},{9... | collective-permute-start | bytes 589832 | tf_op jit(solution)/shard_map/ppermute | solution.py:902
  5.5 9.9 %collective-permute-start.14 = (bf16[6,128,128]{2,1,0:T(8,128)(2,1)S(1)}, bf16[6,128,128]{2,1,0:T(8,128)(2,1)S(1)}, u32[]{:S(2)}, u32[]{:S(2)}) collective-permute-start(bf16[6,128,128]{2,1,0:T(8,128)(2,1)S(1)} %get-tuple-element.385.refs_16_), channel_id=1, source_target_pairs={{0,8},{8,16},{16,24},{24,28},{28,20},{20,12},{12,4},{4,0},{1,9},{9... | collective-permute-start | bytes 589832 | tf_op jit(solution)/shard_map/ppermute | solution.py:902
  7.5 10.1 %collective-permute-start.21 = (bf16[6,128,128]{2,1,0:T(8,128)(2,1)S(1)}, bf16[6,128,128]{2,1,0:T(8,128)(2,1)}, u32[]{:S(2)}, u32[]{:S(2)}) collective-permute-start(bf16[6,128,128]{2,1,0:T(8,128)(2,1)S(1)} %get-tuple-element.384.refs_24_), channel_id=1, source_target_pairs={{8,0},{16,8},{24,16},{28,24},{20,28},{12,20},{4,12},{0,4},{9,1},{1... | collective-permute-start | bytes 589832 | tf_op jit(solution)/shard_map/ppermute | solution.py:902
  11.2 9.0 %collective-permute-start.1 = (bf16[6,128,128]{2,1,0:T(8,128)(2,1)S(1)}, bf16[6,128,128]{2,1,0:T(8,128)(2,1)}, u32[]{:S(2)}, u32[]{:S(2)}) collective-permute-start(bf16[6,128,128]{2,1,0:T(8,128)(2,1)S(1)} %collective-permute-done.refs_1_), channel_id=1, source_target_pairs={{0,8},{8,16},{16,24},{24,28},{28,20},{20,12},{12,4},{4,0},{1,9},{9... | collective-permute-start | bytes 589832 | tf_op jit(solution)/shard_map/ppermute | solution.py:902
  13.3 8.8 %collective-permute-start.8 = (bf16[6,128,128]{2,1,0:T(8,128)(2,1)S(1)}, bf16[6,128,128]{2,1,0:T(8,128)(2,1)}, u32[]{:S(2)}, u32[]{:S(2)}) collective-permute-start(bf16[6,128,128]{2,1,0:T(8,128)(2,1)S(1)} %collective-permute-done.7.refs_9_), channel_id=1, source_target_pairs={{8,0},{16,8},{24,16},{28,24},{20,28},{12,20},{4,12},{0,4},{9,1},{1... | collective-permute-start | bytes 589832 | tf_op jit(solution)/shard_map/ppermute | solution.py:902
  78.9 14.8 %collective-permute-start.30 = (bf16[256,1024]{1,0:T(8,128)(2,1)S(1)}, bf16[256,1024]{1,0:T(8,128)(2,1)S(1)}, u32[]{:S(2)}, u32[]{:S(2)}) collective-permute-start(bf16[256,1024]{1,0:T(8,128)(2,1)S(1)} %add_low.19.a_ref), channel_id=1, source_target_pairs={{0,2},{1,3},{2,0},{3,1},{4,6},{5,7},{6,4},{7,5},{8,10},{9,11},{10,... | collective-permute-start | bytes 1572872 | tf_op jit(solution)/shard_map/ppermute | solution.py:871
  88.7 15.4 %collective-permute-start.35 = (bf16[256,1024]{1,0:T(8,128)(2,1)S(1)}, bf16[256,1024]{1,0:T(8,128)(2,1)S(1)}, u32[]{:S(2)}, u32[]{:S(2)}) collective-permute-start(bf16[256,1024]{1,0:T(8,128)(2,1)S(1)} %add_low.20.a_ref), channel_id=1, source_target_pairs={{0,2},{1,3},{2,0},{3,1},{4,6},{5,7},{6,4},{7,5},{8,10},{9,11},{10,... | collective-permute-start | bytes 1572872 | tf_op jit(solution)/shard_map/ppermute | solution.py:871
  109.7 14.8 %collective-permute-start.41 = (bf16[256,1024]{1,0:T(8,128)(2,1)S(1)}, bf16[256,1024]{1,0:T(8,128)(2,1)S(1)}, u32[]{:S(2)}, u32[]{:S(2)}) collective-permute-start(bf16[256,1024]{1,0:T(8,128)(2,1)S(1)} %add_low.21.a_ref), channel_id=1, source_target_pairs={{0,2},{1,3},{2,0},{3,1},{4,6},{5,7},{6,4},{7,5},{8,10},{9,11},{10,... | collective-permute-start | bytes 1572872 | tf_op jit(solution)/shard_map/ppermute | solution.py:871
  111.4 23.5 %collective-permute-start.43 = (bf16[256,1024]{1,0:T(8,128)(2,1)S(1)}, bf16[256,1024]{1,0:T(8,128)(2,1)S(1)}, u32[]{:S(2)}, u32[]{:S(2)}) collective-permute-start(bf16[256,1024]{1,0:T(8,128)(2,1)S(1)} %add_low.22.a_ref), channel_id=1, source_target_pairs={{0,2},{1,3},{2,0},{3,1},{4,6},{5,7},{6,4},{7,5},{8,10},{9,11},{10,... | collective-permute-start | bytes 1572872 | tf_op jit(solution)/shard_map/ppermute | solution.py:871
  125.7 13.2 %collective-permute-start.44 = (bf16[128,1024]{1,0:T(8,128)(2,1)S(1)}, bf16[128,1024]{1,0:T(8,128)(2,1)S(1)}, u32[]{:S(2)}, u32[]{:S(2)}) collective-permute-start(bf16[128,1024]{1,0:T(8,128)(2,1)S(1)} %get-tuple-element.243), channel_id=1, source_target_pairs={{0,16},{4,20},{8,24},{12,28},{16,0},{20,4},{24,8},{28,12},{1,17},{... | collective-permute-start | bytes 786440 | tf_op jit(solution)/shard_map/ppermute | solution.py:981
  136.0 14.0 %collective-permute-start.46 = (bf16[128,1024]{1,0:T(8,128)(2,1)S(1)}, bf16[128,1024]{1,0:T(8,128)(2,1)S(1)}, u32[]{:S(2)}, u32[]{:S(2)}) collective-permute-start(bf16[128,1024]{1,0:T(8,128)(2,1)S(1)} %get-tuple-element.244), channel_id=1, source_target_pairs={{0,16},{4,20},{8,24},{12,28},{16,0},{20,4},{24,8},{28,12},{1,17},{... | collective-permute-start | bytes 786440 | tf_op jit(solution)/shard_map/ppermute | solution.py:981
  138.8 13.2 %collective-permute-start.45 = (bf16[128,1024]{1,0:T(8,128)(2,1)S(1)}, bf16[128,1024]{1,0:T(8,128)(2,1)S(1)}, u32[]{:S(2)}, u32[]{:S(2)}) collective-permute-start(bf16[128,1024]{1,0:T(8,128)(2,1)S(1)} %collective-permute-done.44.refs_7_), channel_id=1, source_target_pairs={{0,2},{1,3},{2,0},{3,1},{4,6},{5,7},{6,4},{7,5},{8,10},{9,11},{10,... | collective-permute-start | bytes 786440 | tf_op jit(solution)/shard_map/ppermute | solution.py:871
  169.4 14.8 %collective-permute-start.58 = (bf16[256,1024]{1,0:T(8,128)(2,1)S(1)}, bf16[256,1024]{1,0:T(8,128)(2,1)S(1)}, u32[]{:S(2)}, u32[]{:S(2)}) collective-permute-start(bf16[256,1024]{1,0:T(8,128)(2,1)S(1)} %add_low.24.a_ref), channel_id=1, source_target_pairs={{0,2},{1,3},{2,0},{3,1},{4,6},{5,7},{6,4},{7,5},{8,10},{9,11},{10,... | collective-permute-start | bytes 1572872 | tf_op jit(solution)/shard_map/ppermute | solution.py:871
  171.0 23.6 %collective-permute-start.59 = (bf16[256,1024]{1,0:T(8,128)(2,1)S(1)}, bf16[256,1024]{1,0:T(8,128)(2,1)S(1)}, u32[]{:S(2)}, u32[]{:S(2)}) collective-permute-start(bf16[256,1024]{1,0:T(8,128)(2,1)S(1)} %add_low.23.a_ref), channel_id=1, source_target_pairs={{0,2},{1,3},{2,0},{3,1},{4,6},{5,7},{6,4},{7,5},{8,10},{9,11},{10,... | collective-permute-start | bytes 1572872 | tf_op jit(solution)/shard_map/ppermute | solution.py:871
  210.7 9.9 %collective-permute-start.66 = (bf16[6,128,128]{2,1,0:T(8,128)(2,1)S(1)}, bf16[6,128,128]{2,1,0:T(8,128)(2,1)S(1)}, u32[]{:S(2)}, u32[]{:S(2)}) collective-permute-start(bf16[6,128,128]{2,1,0:T(8,128)(2,1)S(1)} %get-tuple-element.305), channel_id=1, source_target_pairs={{0,8},{8,16},{16,24},{24,28},{28,20},{20,12},{12,4},{4,0},{1,9},{9... | collective-permute-start | bytes 589832 | tf_op jit(solution)/shard_map/ppermute | solution.py:1081
  212.4 10.0 %collective-permute-start.65 = (bf16[6,128,128]{2,1,0:T(8,128)(2,1)S(1)}, bf16[6,128,128]{2,1,0:T(8,128)(2,1)S(1)}, u32[]{:S(2)}, u32[]{:S(2)}) collective-permute-start(bf16[6,128,128]{2,1,0:T(8,128)(2,1)S(1)} %get-tuple-element.303), channel_id=1, source_target_pairs={{8,0},{16,8},{24,16},{28,24},{20,28},{12,20},{4,12},{0,4},{9,1},{1... | collective-permute-start | bytes 589832 | tf_op jit(solution)/shard_map/ppermute | solution.py:1081
  230.1 37.6 %collective-permute-start.89 = (bf16[512,1024]{1,0:T(8,128)(2,1)S(1)}, bf16[512,1024]{1,0:T(8,128)(2,1)S(1)}, u32[]{:S(2)}, u32[]{:S(2)}) collective-permute-start(bf16[512,1024]{1,0:T(8,128)(2,1)S(1)} %add_low.37), channel_id=1, source_target_pairs={{0,2},{1,3},{2,0},{3,1},{4,6},{5,7},{6,4},{7,5},{8,10},{9,11},{10,... | collective-permute-start | bytes 3145736 | tf_op jit(solution)/shard_map/ppermute | solution.py:871
  233.2 8.9 %collective-permute-start.76 = (bf16[6,128,128]{2,1,0:T(8,128)(2,1)S(1)}, bf16[6,128,128]{2,1,0:T(8,128)(2,1)S(1)}, u32[]{:S(2)}, u32[]{:S(2)}) collective-permute-start(bf16[6,128,128]{2,1,0:T(8,128)(2,1)S(1)} %add_convert_fusion.8), channel_id=1, source_target_pairs={{0,8},{8,16},{16,24},{24,28},{28,20},{20,12},{12,4},{4,0},{1,9},{9... | collective-permute-start | bytes 589832 | tf_op jit(solution)/shard_map/ppermute | solution.py:1081
  235.2 11.1 %collective-permute-start.74 = (bf16[6,128,128]{2,1,0:T(8,128)(2,1)S(1)}, bf16[6,128,128]{2,1,0:T(8,128)(2,1)S(1)}, u32[]{:S(2)}, u32[]{:S(2)}) collective-permute-start(bf16[6,128,128]{2,1,0:T(8,128)(2,1)S(1)} %add_convert_fusion.6), channel_id=1, source_target_pairs={{0,8},{8,16},{16,24},{24,28},{28,20},{20,12},{12,4},{4,0},{1,9},{9... | collective-permute-start | bytes 589832 | tf_op jit(solution)/shard_map/ppermute | solution.py:1081
  237.8 9.4 %collective-permute-start.73 = (bf16[6,128,128]{2,1,0:T(8,128)(2,1)S(1)}, bf16[6,128,128]{2,1,0:T(8,128)(2,1)S(1)}, u32[]{:S(2)}, u32[]{:S(2)}) collective-permute-start(bf16[6,128,128]{2,1,0:T(8,128)(2,1)S(1)} %add_convert_fusion.5), channel_id=1, source_target_pairs={{8,0},{16,8},{24,16},{28,24},{20,28},{12,20},{4,12},{0,4},{9,1},{1... | collective-permute-start | bytes 589832 | tf_op jit(solution)/shard_map/ppermute | solution.py:1081
  256.9 9.4 %collective-permute-start.82 = (bf16[6,128,128]{2,1,0:T(8,128)(2,1)S(1)}, bf16[6,128,128]{2,1,0:T(8,128)(2,1)S(1)}, u32[]{:S(2)}, u32[]{:S(2)}) collective-permute-start(bf16[6,128,128]{2,1,0:T(8,128)(2,1)S(1)} %add_low.32), channel_id=1, source_target_pairs={{8,0},{16,8},{24,16},{28,24},{20,28},{12,20},{4,12},{0,4},{9,1},{1... | collective-permute-start | bytes 589832 | tf_op jit(solution)/shard_map/ppermute | solution.py:1081
  259.3 10.5 %collective-permute-start.91 = (bf16[6,128,128]{2,1,0:T(8,128)(2,1)S(1)}, bf16[6,128,128]{2,1,0:T(8,128)(2,1)S(1)}, u32[]{:S(2)}, u32[]{:S(2)}) collective-permute-start(bf16[6,128,128]{2,1,0:T(8,128)(2,1)S(1)} %add_low.33), channel_id=1, source_target_pairs={{0,8},{8,16},{16,24},{24,28},{28,20},{20,12},{12,4},{4,0},{1,9},{9... | collective-permute-start | bytes 589832 | tf_op jit(solution)/shard_map/ppermute | solution.py:1081
  270.6 9.0 %collective-permute-start.92 = (bf16[6,128,128]{2,1,0:T(8,128)(2,1)S(1)}, bf16[6,128,128]{2,1,0:T(8,128)(2,1)S(1)}, u32[]{:S(2)}, u32[]{:S(2)}) collective-permute-start(bf16[6,128,128]{2,1,0:T(8,128)(2,1)S(1)} %add_convert_fusion.4), channel_id=1, source_target_pairs={{0,8},{8,16},{16,24},{24,28},{28,20},{20,12},{12,4},{4,0},{1,9},{9... | collective-permute-start | bytes 589832 | tf_op jit(solution)/shard_map/ppermute | solution.py:1081
  271.9 10.0 %collective-permute-start.96 = (bf16[6,128,128]{2,1,0:T(8,128)(2,1)S(1)}, bf16[6,128,128]{2,1,0:T(8,128)(2,1)S(1)}, u32[]{:S(2)}, u32[]{:S(2)}) collective-permute-start(bf16[6,128,128]{2,1,0:T(8,128)(2,1)S(1)} %add_convert_fusion.2), channel_id=1, source_target_pairs={{0,8},{8,16},{16,24},{24,28},{28,20},{20,12},{12,4},{4,0},{1,9},{9... | collective-permute-start | bytes 589832 | tf_op jit(solution)/shard_map/ppermute | solution.py:1081
  (90 other events, 600.0 us)

commit v4 on v3

--- a/solution.py
+++ b/solution.py
@@ -1085,7 +1085,7 @@
                     local = after(local, travelling[k - 1])
                 if k == 0 and step in (2, 4):
                     local = after(local, small_came)
-                if step in (2, 3, 4):
+                if step in (3, 4):
                     came = add_low(came, [local])
                 else:
                     came = (came.astype(wide) + local.astype(wide)).astype(low)

time: 295 us -> 288 us (0.976)
  waiting for transfers between devices: 114 us -> 105 us
  starting transfers between devices: 88.6 us -> 91.7 us
    ppermute x28, waiting for transfers between devices: 27.8 us -> 20.9 us  [body(): came = lax.ppermute(travelling[k], 'dp', routes[k % 2])]
    pallas_call x49 -> x45, Pallas kernels: 66.1 us -> 65.9 us  [vmem_call(): pl.pallas_call(kernel, in_specs=specs, out_specs=[vmem] * len(outs), out_...]
  transfers between devices with their start and end apart: 99 -> 99, of which waited for: 51 -> 50; matrix products, arithmetic and copies ran while one was open for 1% -> 1% of each run, Pallas kernels for 17% -> 17%
where the time goes in v4:
time: 288 us; the launch traced here: 284 us
  waiting for transfers between devices  105 us (36%)
  starting transfers between devices  91.7 us (32%)
  Pallas kernels  76.1 us (26%)
  matrix products  5.74 us (2%)
  other arithmetic  3.19 us (1%)
    pallas_call x45, Pallas kernels, vmem_call(): pl.pallas_call(kernel, in_specs=specs, out_specs=[vmem] * len(outs), out_...  65.9 us
    ppermute x9, waiting for transfers between devices, chip_swap(): return lax.ppermute(value, 'mp', chip_pairs)  37.7 us
    ppermute x28, starting transfers between devices, body(): came = lax.ppermute(travelling[k], 'dp', routes[k % 2])  32.2 us
    ppermute x28, waiting for transfers between devices, body(): arrived[k].append(lax.ppermute(arrived[k][-1], 'dp', routes[k % 2]))  31.6 us
    ppermute x28, starting transfers between devices, body(): arrived[k].append(lax.ppermute(arrived[k][-1], 'dp', routes[k % 2]))  29.9 us
    ppermute x28, waiting for transfers between devices, body(): came = lax.ppermute(travelling[k], 'dp', routes[k % 2])  20.9 us
    ppermute x9, starting transfers between devices, chip_swap(): return lax.ppermute(value, 'mp', chip_pairs)  12.1 us
    ppermute x2, waiting for transfers between devices, body(): mine = lax.ppermute(out_piece, 'dp', exchange)  9.88 us
  transfers between devices with their start and end apart: 99, of which 50 were waited for; matrix products, arithmetic and copies ran while one was open for 1% of the time, Pallas kernels for 17%

profile of v4, /device:TPU:0, one launch (start us, length us, event | category | flops | bytes accessed | tf_op | source)
XLA Modules:
  0.0 284.3 jit_solution(10832496454778988438)
XLA Ops:
  2.4 3.1 %collective-permute-start = (bf16[6,128,128]{2,1,0:T(8,128)(2,1)S(1)}, bf16[6,128,128]{2,1,0:T(8,128)(2,1)S(1)}, u32[]{:S(2)}, u32[]{:S(2)}) collective-permute-start(bf16[6,128,128]{2,1,0:T(8,128)(2,1)S(1)} %get-tuple-element.387.refs_0_), channel_id=1, source_target_pairs={{0,8},{8,16},{16,24},{24,28},{28,20},{20,12},{12,4},{4,0},{1,9},{9... | collective-permute-start | bytes 589832 | tf_op jit(solution)/shard_map/ppermute | solution.py:902
  7.7 3.5 %collective-permute-done.refs_1_ = bf16[6,128,128]{2,1,0:T(8,128)(2,1)S(1)} collective-permute-done((bf16[6,128,128]{2,1,0:T(8,128)(2,1)S(1)}, bf16[6,128,128]{2,1,0:T(8,128)(2,1)S(1)}, u32[]{:S(2)}, u32[]{:S(2)}) %collective-permute-start) | collective-permute-done | bytes 196640 | tf_op jit(solution)/shard_map/ppermute | solution.py:902
  66.6 3.2 %assemble.1 = (bf16[1024,768]{1,0:T(8,128)(2,1)S(1)}, bf16[256,1024]{1,0:T(8,128)(2,1)S(1)}, bf16[1024,1024]{1,0:T(8,128)(2,1)S(1)}, bf16[1024,1024]{1,0:T(8,128)(2,1)S(1)}) custom-call(s32[6]{0:T(128)S(1)} %stack.31.place_ref, s32[192]{0:T(256)S(1)} %bitcast.17, bf16[6,128,128]{2,1,0:T(8,128)(2,1)S(1)} %get-tuple-element.387.refs_0_, ...), custom_call_target="tpu_custom_call" | custom-call | bytes 1024 | tf_op jit(solution)/shard_map/assemble/pallas_call | solution.py:76
  71.6 3.3 %attention_tile.4 = (bf16[256,256]{1,0:T(8,128)(2,1)S(1)}, f32[4,256]{1,0:T(4,128)S(1)}, bf16[128,1024]{1,0:T(8,128)(2,1)S(1)}, bf16[128,1024]{1,0:T(8,128)(2,1)S(1)}) custom-call(bf16[1024,768]{1,0:T(8,128)(2,1)S(1)} %add_convert_fusion.qkv_ref, bf16[256,1024]{1,0:T(8,128)(2,1)S(1)} %get-tuple-element.204.w_ref, ...), custom_call_target="tpu_custom_call" | custom-call | bytes 1024 | tf_op jit(solution)/shard_map/attention_tile/pallas_call | solution.py:76
  75.5 3.3 %attention_tile.5 = (bf16[256,256]{1,0:T(8,128)(2,1)S(1)}, f32[4,256]{1,0:T(4,128)S(1)}, f32[256,1024]{1,0:T(8,128)S(1)}) custom-call(bf16[1024,768]{1,0:T(8,128)(2,1)S(1)} %add_convert_fusion.qkv_ref, bf16[256,1024]{1,0:T(8,128)(2,1)S(1)} %get-tuple-element.204.w_ref, f32[1024,8]{1,0:T(8,128)S(1)} %get-tuple-element.205.sk_ref.table_ref, ...), custom_call_target="tpu_custom_call" | custom-call | bytes 1024 | tf_op jit(solution)/shard_map/attention_tile/pallas_call | solution.py:76
  80.5 3.3 %attention_tile.6 = (bf16[256,256]{1,0:T(8,128)(2,1)S(1)}, f32[4,256]{1,0:T(4,128)S(1)}, bf16[64,1024]{1,0:T(8,128)(2,1)S(1)}, bf16[64,1024]{1,0:T(8,128)(2,1)S(...) custom-call(bf16[1024,768]{1,0:T(8,128)(2,1)S(1)} %add_convert_fusion.qkv_ref, ...), custom_call_target="tpu_custom_call" | custom-call | bytes 1024 | tf_op jit(solution)/shard_map/attention_tile/pallas_call | solution.py:76
  84.9 3.7 %attention_tile.7 = (bf16[256,256]{1,0:T(8,128)(2,1)S(1)}, f32[4,256]{1,0:T(4,128)S(1)}, f32[256,1024]{1,0:T(8,128)S(1)}) custom-call(bf16[1024,768]{1,0:T(8,128)(2,1)S(1)} %add_convert_fusion.qkv_ref, bf16[256,1024]{1,0:T(8,128)(2,1)S(1)} %get-tuple-element.204.w_ref, f32[1024,8]{1,0:T(8,128)S(1)} %get-tuple-element.205.sk_ref.table_ref, ...), custom_call_target="tpu_custom_call" | custom-call | bytes 1024 | tf_op jit(solution)/shard_map/attention_tile/pallas_call | solution.py:76
  89.4 4.4 %collective-permute-done.30.b_ref = bf16[256,1024]{1,0:T(8,128)(2,1)S(1)} collective-permute-done((bf16[256,1024]{1,0:T(8,128)(2,1)S(1)}, bf16[256,1024]{1,0:T(8,128)(2,1)S(1)}, u32[]{:S(2)}, u32[]{:S(2)}) %collective-permute-start.30) | collective-permute-done | bytes 524320 | tf_op jit(solution)/shard_map/ppermute | solution.py:871
  98.6 5.5 %collective-permute-done.35.b_ref = bf16[256,1024]{1,0:T(8,128)(2,1)S(1)} collective-permute-done((bf16[256,1024]{1,0:T(8,128)(2,1)S(1)}, bf16[256,1024]{1,0:T(8,128)(2,1)S(1)}, u32[]{:S(2)}, u32[]{:S(2)}) %collective-permute-start.35) | collective-permute-done | bytes 524320 | tf_op jit(solution)/shard_map/ppermute | solution.py:871
  112.8 11.7 %collective-permute-done.41.b_ref = bf16[256,1024]{1,0:T(8,128)(2,1)S(1)} collective-permute-done((bf16[256,1024]{1,0:T(8,128)(2,1)S(1)}, bf16[256,1024]{1,0:T(8,128)(2,1)S(1)}, u32[]{:S(2)}, u32[]{:S(2)}) %collective-permute-start.41) | collective-permute-done | bytes 524320 | tf_op jit(solution)/shard_map/ppermute | solution.py:871
  125.7 2.7 collective-permute-start.44
  128.3 6.6 %collective-permute-done.43.b_ref = bf16[256,1024]{1,0:T(8,128)(2,1)S(1)} collective-permute-done((bf16[256,1024]{1,0:T(8,128)(2,1)S(1)}, bf16[256,1024]{1,0:T(8,128)(2,1)S(1)}, u32[]{:S(2)}, u32[]{:S(2)}) %collective-permute-start.43) | collective-permute-done | bytes 524320 | tf_op jit(solution)/shard_map/ppermute | solution.py:871
  136.0 2.7 collective-permute-start.46
  140.3 9.7 %collective-permute-done.46.refs_9_ = bf16[128,1024]{1,0:T(8,128)(2,1)S(1)} collective-permute-done((bf16[128,1024]{1,0:T(8,128)(2,1)S(1)}, bf16[128,1024]{1,0:T(8,128)(2,1)S(1)}, u32[]{:S(2)}, u32[]{:S(2)}) %collective-permute-start.46) | collective-permute-done | bytes 262176 | tf_op jit(solution)/shard_map/ppermute | solution.py:981
  152.1 5.2 %collective-permute-done.47.refs_10_ = bf16[128,1024]{1,0:T(8,128)(2,1)S(1)} collective-permute-done((bf16[128,1024]{1,0:T(8,128)(2,1)S(1)}, bf16[128,1024]{1,0:T(8,128)(2,1)S(1)}, u32[]{:S(2)}, u32[]{:S(2)}) %collective-permute-start.47) | collective-permute-done | bytes 262176 | tf_op jit(solution)/shard_map/ppermute | solution.py:871
  158.8 3.4 %link_back.1 = (f32[256,1024]{1,0:T(8,128)S(1)}, f32[256,1024]{1,0:T(8,128)S(1)}, bf16[256,1024]{1,0:T(8,128)(2,1)S(1)}, bf16[256,1024]{1,0:T(8,128)(2,1)S(1)}, ...) custom-call(s32[6]{0:T(128)S(1)} %stack.31.place_ref, bf16[512,1024]{1,0:T(8,128)(2,1)S(1)} %get-tuple-element.233.link_ref, ...), custom_call_target="tpu_custom_call" | custom-call | bytes 1024 | tf_op jit(solution)/shard_map/link_back/pallas_call | solution.py:76
  173.9 4.5 %feed_grads.1 = (bf16[1024,1024]{1,0:T(8,128)(2,1)S(1)}, bf16[1024,1024]{1,0:T(8,128)(2,1)S(1)}, f32[1,1024]{1,0:T(1,128)S(1)}) custom-call(bf16[256,1024]{1,0:T(8,128)(2,1)S(1)} %get-tuple-element.221.refs_0_, bf16[256,1024]{1,0:T(8,128)(2,1)S(1)} %get-tuple-element.228.refs_1_, bf16[256,1024]{1,0:T(8,128)(2,1)S(1)} %get-tuple-element.229.refs_2_, ...), custom_call_target="tpu_custom_call" | custom-call | bytes 1024 | tf_op jit(solution)/shard_map/feed_grads/pallas_call | solution.py:76
  180.9 3.3 %collective-permute-done.58.b_ref = bf16[256,1024]{1,0:T(8,128)(2,1)S(1)} collective-permute-done((bf16[256,1024]{1,0:T(8,128)(2,1)S(1)}, bf16[256,1024]{1,0:T(8,128)(2,1)S(1)}, u32[]{:S(2)}, u32[]{:S(2)}) %collective-permute-start.58) | collective-permute-done | bytes 524320 | tf_op jit(solution)/shard_map/ppermute | solution.py:871
  187.0 6.7 %attention_backward.2 = (bf16[512,256]{1,0:T(8,128)(2,1)S(1)}, f32[1024,256]{1,0:T(8,128)S(1)}, f32[1024,256]{1,0:T(8,128)S(1)}, f32[256,1024]{1,0:T(8,128)S(1)}, f32[1,256]{1,0:T(1,128)S(1)}) custom-call(bf16[1024,768]{1,0:T(8,128)(2,1)S(1)} %add_convert_fusion.qkv_ref, bf16[256,1024]{1,0:T(8,128)(2,1)S(1)} %get-tuple-element.204.w_ref, ...), custom_call_target="tpu_custom_call" | custom-call | bytes 1024 | tf_op jit(solution)/shard_map/attention_backward/pallas_call | solution.py:76
  197.4 7.2 %attention_backward.3 = (bf16[1024,768]{1,0:T(8,128)(2,1)S(1)}, bf16[256,1024]{1,0:T(8,128)(2,1)S(1)}, f32[1,512]{1,0:T(1,128)S(1)}) custom-call(bf16[1024,768]{1,0:T(8,128)(2,1)S(1)} %add_convert_fusion.qkv_ref, bf16[256,1024]{1,0:T(8,128)(2,1)S(1)} %get-tuple-element.204.w_ref, f32[1024,8]{1,0:T(8,128)S(1)} %get-tuple-element.205.sk_ref.table_ref, ...), custom_call_target="tpu_custom_call" | custom-call | bytes 1024 | tf_op jit(solution)/shard_map/attention_backward/pallas_call | solution.py:76
  212.7 3.7 %collective-permute-done.68 = bf16[6,128,128]{2,1,0:T(8,128)(2,1)S(1)} collective-permute-done((bf16[6,128,128]{2,1,0:T(8,128)(2,1)S(1)}, bf16[6,128,128]{2,1,0:T(8,128)(2,1)S(1)}, u32[]{:S(2)}, u32[]{:S(2)}) %collective-permute-start.68) | collective-permute-done | bytes 196640 | tf_op jit(solution)/shard_map/ppermute | solution.py:1081
  252.2 2.5 collective-permute-start.91
  259.7 3.2 %collective-permute-start.87 = (f32[16,1024]{1,0:T(8,128)S(1)}, f32[16,1024]{1,0:T(8,128)S(1)}, u32[]{:S(2)}, u32[]{:S(2)}) collective-permute-start(f32[16,1024]{1,0:T(8,128)S(1)} %add.101), channel_id=1, source_target_pairs={{0,16},{4,20},{8,24},{12,28},{16,0},{20,4},{24,8},{28,12},{1,17},{... | collective-permute-start | bytes 196616 | tf_op jit(solution)/shard_map/ppermute | solution.py:1102
  276.9 6.3 %optimize.1 = (f32[24,128,128]{2,1,0:T(8,128)}, f32[24,128,128]{2,1,0:T(8,128)}, f32[24,128,128]{2,1,0:T(8,128)}, f32[24,128,128]{2,1,0:T(8,128)}) custom-call(bf16[6,128,128]{2,1,0:T(8,128)(2,1)S(1)} %collective-permute-done.92.refs_0_, bf16[6,128,128]{2,1,0:T(8,128)(2,1)S(1)} %collective-permute-done.94.refs_1_, ...), custom_call_target="tpu_custom_call" | custom-call | bytes 1024 | tf_op jit(solution)/shard_map/optimize/pallas_call | solution.py:379
  (287 shorter events, 169.7 us)
Async XLA Ops:
  2.4 8.7 %collective-permute-start = (bf16[6,128,128]{2,1,0:T(8,128)(2,1)S(1)}, bf16[6,128,128]{2,1,0:T(8,128)(2,1)S(1)}, u32[]{:S(2)}, u32[]{:S(2)}) collective-permute-start(bf16[6,128,128]{2,1,0:T(8,128)(2,1)S(1)} %get-tuple-element.387.refs_0_), channel_id=1, source_target_pairs={{0,8},{8,16},{16,24},{24,28},{28,20},{20,12},{12,4},{4,0},{1,9},{9... | collective-permute-start | bytes 589832 | tf_op jit(solution)/shard_map/ppermute | solution.py:902
  5.5 9.9 %collective-permute-start.14 = (bf16[6,128,128]{2,1,0:T(8,128)(2,1)S(1)}, bf16[6,128,128]{2,1,0:T(8,128)(2,1)S(1)}, u32[]{:S(2)}, u32[]{:S(2)}) collective-permute-start(bf16[6,128,128]{2,1,0:T(8,128)(2,1)S(1)} %get-tuple-element.385.refs_16_), channel_id=1, source_target_pairs={{0,8},{8,16},{16,24},{24,28},{28,20},{20,12},{12,4},{4,0},{1,9},{9... | collective-permute-start | bytes 589832 | tf_op jit(solution)/shard_map/ppermute | solution.py:902
  7.5 10.1 %collective-permute-start.21 = (bf16[6,128,128]{2,1,0:T(8,128)(2,1)S(1)}, bf16[6,128,128]{2,1,0:T(8,128)(2,1)}, u32[]{:S(2)}, u32[]{:S(2)}) collective-permute-start(bf16[6,128,128]{2,1,0:T(8,128)(2,1)S(1)} %get-tuple-element.384.refs_24_), channel_id=1, source_target_pairs={{8,0},{16,8},{24,16},{28,24},{20,28},{12,20},{4,12},{0,4},{9,1},{1... | collective-permute-start | bytes 589832 | tf_op jit(solution)/shard_map/ppermute | solution.py:902
  11.2 9.0 %collective-permute-start.1 = (bf16[6,128,128]{2,1,0:T(8,128)(2,1)S(1)}, bf16[6,128,128]{2,1,0:T(8,128)(2,1)}, u32[]{:S(2)}, u32[]{:S(2)}) collective-permute-start(bf16[6,128,128]{2,1,0:T(8,128)(2,1)S(1)} %collective-permute-done.refs_1_), channel_id=1, source_target_pairs={{0,8},{8,16},{16,24},{24,28},{28,20},{20,12},{12,4},{4,0},{1,9},{9... | collective-permute-start | bytes 589832 | tf_op jit(solution)/shard_map/ppermute | solution.py:902
  13.3 8.8 %collective-permute-start.8 = (bf16[6,128,128]{2,1,0:T(8,128)(2,1)S(1)}, bf16[6,128,128]{2,1,0:T(8,128)(2,1)}, u32[]{:S(2)}, u32[]{:S(2)}) collective-permute-start(bf16[6,128,128]{2,1,0:T(8,128)(2,1)S(1)} %collective-permute-done.7.refs_9_), channel_id=1, source_target_pairs={{8,0},{16,8},{24,16},{28,24},{20,28},{12,20},{4,12},{0,4},{9,1},{1... | collective-permute-start | bytes 589832 | tf_op jit(solution)/shard_map/ppermute | solution.py:902
  78.9 14.8 %collective-permute-start.30 = (bf16[256,1024]{1,0:T(8,128)(2,1)S(1)}, bf16[256,1024]{1,0:T(8,128)(2,1)S(1)}, u32[]{:S(2)}, u32[]{:S(2)}) collective-permute-start(bf16[256,1024]{1,0:T(8,128)(2,1)S(1)} %add_low.15.a_ref), channel_id=1, source_target_pairs={{0,2},{1,3},{2,0},{3,1},{4,6},{5,7},{6,4},{7,5},{8,10},{9,11},{10,... | collective-permute-start | bytes 1572872 | tf_op jit(solution)/shard_map/ppermute | solution.py:871
  88.7 15.4 %collective-permute-start.35 = (bf16[256,1024]{1,0:T(8,128)(2,1)S(1)}, bf16[256,1024]{1,0:T(8,128)(2,1)S(1)}, u32[]{:S(2)}, u32[]{:S(2)}) collective-permute-start(bf16[256,1024]{1,0:T(8,128)(2,1)S(1)} %add_low.16.a_ref), channel_id=1, source_target_pairs={{0,2},{1,3},{2,0},{3,1},{4,6},{5,7},{6,4},{7,5},{8,10},{9,11},{10,... | collective-permute-start | bytes 1572872 | tf_op jit(solution)/shard_map/ppermute | solution.py:871
  109.7 14.8 %collective-permute-start.41 = (bf16[256,1024]{1,0:T(8,128)(2,1)S(1)}, bf16[256,1024]{1,0:T(8,128)(2,1)S(1)}, u32[]{:S(2)}, u32[]{:S(2)}) collective-permute-start(bf16[256,1024]{1,0:T(8,128)(2,1)S(1)} %add_low.17.a_ref), channel_id=1, source_target_pairs={{0,2},{1,3},{2,0},{3,1},{4,6},{5,7},{6,4},{7,5},{8,10},{9,11},{10,... | collective-permute-start | bytes 1572872 | tf_op jit(solution)/shard_map/ppermute | solution.py:871
  111.4 23.5 %collective-permute-start.43 = (bf16[256,1024]{1,0:T(8,128)(2,1)S(1)}, bf16[256,1024]{1,0:T(8,128)(2,1)S(1)}, u32[]{:S(2)}, u32[]{:S(2)}) collective-permute-start(bf16[256,1024]{1,0:T(8,128)(2,1)S(1)} %add_low.18.a_ref), channel_id=1, source_target_pairs={{0,2},{1,3},{2,0},{3,1},{4,6},{5,7},{6,4},{7,5},{8,10},{9,11},{10,... | collective-permute-start | bytes 1572872 | tf_op jit(solution)/shard_map/ppermute | solution.py:871
  125.7 13.2 %collective-permute-start.44 = (bf16[128,1024]{1,0:T(8,128)(2,1)S(1)}, bf16[128,1024]{1,0:T(8,128)(2,1)S(1)}, u32[]{:S(2)}, u32[]{:S(2)}) collective-permute-start(bf16[128,1024]{1,0:T(8,128)(2,1)S(1)} %get-tuple-element.243), channel_id=1, source_target_pairs={{0,16},{4,20},{8,24},{12,28},{16,0},{20,4},{24,8},{28,12},{1,17},{... | collective-permute-start | bytes 786440 | tf_op jit(solution)/shard_map/ppermute | solution.py:981
  136.0 14.0 %collective-permute-start.46 = (bf16[128,1024]{1,0:T(8,128)(2,1)S(1)}, bf16[128,1024]{1,0:T(8,128)(2,1)S(1)}, u32[]{:S(2)}, u32[]{:S(2)}) collective-permute-start(bf16[128,1024]{1,0:T(8,128)(2,1)S(1)} %get-tuple-element.244), channel_id=1, source_target_pairs={{0,16},{4,20},{8,24},{12,28},{16,0},{20,4},{24,8},{28,12},{1,17},{... | collective-permute-start | bytes 786440 | tf_op jit(solution)/shard_map/ppermute | solution.py:981
  138.8 13.2 %collective-permute-start.45 = (bf16[128,1024]{1,0:T(8,128)(2,1)S(1)}, bf16[128,1024]{1,0:T(8,128)(2,1)S(1)}, u32[]{:S(2)}, u32[]{:S(2)}) collective-permute-start(bf16[128,1024]{1,0:T(8,128)(2,1)S(1)} %collective-permute-done.44.refs_7_), channel_id=1, source_target_pairs={{0,2},{1,3},{2,0},{3,1},{4,6},{5,7},{6,4},{7,5},{8,10},{9,11},{10,... | collective-permute-start | bytes 786440 | tf_op jit(solution)/shard_map/ppermute | solution.py:871
  169.4 14.8 %collective-permute-start.58 = (bf16[256,1024]{1,0:T(8,128)(2,1)S(1)}, bf16[256,1024]{1,0:T(8,128)(2,1)S(1)}, u32[]{:S(2)}, u32[]{:S(2)}) collective-permute-start(bf16[256,1024]{1,0:T(8,128)(2,1)S(1)} %add_low.20.a_ref), channel_id=1, source_target_pairs={{0,2},{1,3},{2,0},{3,1},{4,6},{5,7},{6,4},{7,5},{8,10},{9,11},{10,... | collective-permute-start | bytes 1572872 | tf_op jit(solution)/shard_map/ppermute | solution.py:871
  171.0 23.6 %collective-permute-start.59 = (bf16[256,1024]{1,0:T(8,128)(2,1)S(1)}, bf16[256,1024]{1,0:T(8,128)(2,1)S(1)}, u32[]{:S(2)}, u32[]{:S(2)}) collective-permute-start(bf16[256,1024]{1,0:T(8,128)(2,1)S(1)} %add_low.19.a_ref), channel_id=1, source_target_pairs={{0,2},{1,3},{2,0},{3,1},{4,6},{5,7},{6,4},{7,5},{8,10},{9,11},{10,... | collective-permute-start | bytes 1572872 | tf_op jit(solution)/shard_map/ppermute | solution.py:871
  210.7 9.9 %collective-permute-start.66 = (bf16[6,128,128]{2,1,0:T(8,128)(2,1)S(1)}, bf16[6,128,128]{2,1,0:T(8,128)(2,1)S(1)}, u32[]{:S(2)}, u32[]{:S(2)}) collective-permute-start(bf16[6,128,128]{2,1,0:T(8,128)(2,1)S(1)} %get-tuple-element.305), channel_id=1, source_target_pairs={{0,8},{8,16},{16,24},{24,28},{28,20},{20,12},{12,4},{4,0},{1,9},{9... | collective-permute-start | bytes 589832 | tf_op jit(solution)/shard_map/ppermute | solution.py:1081
  212.4 10.0 %collective-permute-start.65 = (bf16[6,128,128]{2,1,0:T(8,128)(2,1)S(1)}, bf16[6,128,128]{2,1,0:T(8,128)(2,1)S(1)}, u32[]{:S(2)}, u32[]{:S(2)}) collective-permute-start(bf16[6,128,128]{2,1,0:T(8,128)(2,1)S(1)} %get-tuple-element.303), channel_id=1, source_target_pairs={{8,0},{16,8},{24,16},{28,24},{20,28},{12,20},{4,12},{0,4},{9,1},{1... | collective-permute-start | bytes 589832 | tf_op jit(solution)/shard_map/ppermute | solution.py:1081
  222.9 9.9 %collective-permute-start.77 = (f32[16,1024]{1,0:T(8,128)S(1)}, f32[16,1024]{1,0:T(8,128)S(1)}, u32[]{:S(2)}, u32[]{:S(2)}) collective-permute-start(f32[16,1024]{1,0:T(8,128)S(1)} %add_biases.1), channel_id=1, source_target_pairs={{0,4},{4,0},{8,12},{12,8},{16,20},{20,16},{24,28},{28,24},{1,5},{5... | collective-permute-start | bytes 196616 | tf_op jit(solution)/shard_map/ppermute | solution.py:1102
  225.2 10.0 %collective-permute-start.88 = (bf16[512,1024]{1,0:T(8,128)(2,1)S(1)}, bf16[512,1024]{1,0:T(8,128)(2,1)S(1)}, u32[]{:S(2)}, u32[]{:S(2)}) collective-permute-start(bf16[512,1024]{1,0:T(8,128)(2,1)S(1)} %convolution_convert_fusion.1), channel_id=1, source_target_pairs={{0,1},{1,0},{2,3},{3,2},{4,5},{5,4},{6,7},{7,6},{8,9},{9,8},{10,11... | collective-permute-start | bytes 3145736 | tf_op jit(solution)/shard_map/ppermute | solution.py:868
  235.5 24.2 %collective-permute-start.89 = (bf16[512,1024]{1,0:T(8,128)(2,1)S(1)}, bf16[512,1024]{1,0:T(8,128)(2,1)S(1)}, u32[]{:S(2)}, u32[]{:S(2)}) collective-permute-start(bf16[512,1024]{1,0:T(8,128)(2,1)S(1)} %add_low.29), channel_id=1, source_target_pairs={{0,2},{1,3},{2,0},{3,1},{4,6},{5,7},{6,4},{7,5},{8,10},{9,11},{10,... | collective-permute-start | bytes 3145736 | tf_op jit(solution)/shard_map/ppermute | solution.py:871
  249.6 9.7 %collective-permute-start.82 = (bf16[6,128,128]{2,1,0:T(8,128)(2,1)S(1)}, bf16[6,128,128]{2,1,0:T(8,128)(2,1)S(1)}, u32[]{:S(2)}, u32[]{:S(2)}) collective-permute-start(bf16[6,128,128]{2,1,0:T(8,128)(2,1)S(1)} %add_low.24), channel_id=1, source_target_pairs={{8,0},{16,8},{24,16},{28,24},{20,28},{12,20},{4,12},{0,4},{9,1},{1... | collective-permute-start | bytes 589832 | tf_op jit(solution)/shard_map/ppermute | solution.py:1081
  252.2 11.3 %collective-permute-start.91 = (bf16[6,128,128]{2,1,0:T(8,128)(2,1)S(1)}, bf16[6,128,128]{2,1,0:T(8,128)(2,1)S(1)}, u32[]{:S(2)}, u32[]{:S(2)}) collective-permute-start(bf16[6,128,128]{2,1,0:T(8,128)(2,1)S(1)} %add_low.25), channel_id=1, source_target_pairs={{0,8},{8,16},{16,24},{24,28},{28,20},{20,12},{12,4},{4,0},{1,9},{9... | collective-permute-start | bytes 589832 | tf_op jit(solution)/shard_map/ppermute | solution.py:1081
  256.4 9.0 %collective-permute-start.95 = (bf16[6,128,128]{2,1,0:T(8,128)(2,1)S(1)}, bf16[6,128,128]{2,1,0:T(8,128)(2,1)S(1)}, u32[]{:S(2)}, u32[]{:S(2)}) collective-permute-start(bf16[6,128,128]{2,1,0:T(8,128)(2,1)S(1)} %add_low.27), channel_id=1, source_target_pairs={{0,8},{8,16},{16,24},{24,28},{28,20},{20,12},{12,4},{4,0},{1,9},{9... | collective-permute-start | bytes 589832 | tf_op jit(solution)/shard_map/ppermute | solution.py:1081
  263.6 9.5 %collective-permute-start.92 = (bf16[6,128,128]{2,1,0:T(8,128)(2,1)S(1)}, bf16[6,128,128]{2,1,0:T(8,128)(2,1)S(1)}, u32[]{:S(2)}, u32[]{:S(2)}) collective-permute-start(bf16[6,128,128]{2,1,0:T(8,128)(2,1)S(1)} %add_convert_fusion.4), channel_id=1, source_target_pairs={{0,8},{8,16},{16,24},{24,28},{28,20},{20,12},{12,4},{4,0},{1,9},{9... | collective-permute-start | bytes 589832 | tf_op jit(solution)/shard_map/ppermute | solution.py:1081
  265.5 10.0 %collective-permute-start.96 = (bf16[6,128,128]{2,1,0:T(8,128)(2,1)S(1)}, bf16[6,128,128]{2,1,0:T(8,128)(2,1)S(1)}, u32[]{:S(2)}, u32[]{:S(2)}) collective-permute-start(bf16[6,128,128]{2,1,0:T(8,128)(2,1)S(1)} %add_convert_fusion.2), channel_id=1, source_target_pairs={{0,8},{8,16},{16,24},{24,28},{28,20},{20,12},{12,4},{4,0},{1,9},{9... | collective-permute-start | bytes 589832 | tf_op jit(solution)/shard_map/ppermute | solution.py:1081
  (90 other events, 607.9 us)

commit v5 on v4

--- a/solution.py
+++ b/solution.py
@@ -1085,7 +1085,7 @@
                     local = after(local, travelling[k - 1])
                 if k == 0 and step in (2, 4):
                     local = after(local, small_came)
-                if step in (3, 4):
+                if step == 4:
                     came = add_low(came, [local])
                 else:
                     came = (came.astype(wide) + local.astype(wide)).astype(low)

time: 288 us -> 295 us (1.024)
  waiting for transfers between devices: 105 us -> 113 us
    ppermute x9, waiting for transfers between devices: 37.7 us -> 44.7 us  [chip_swap(): return lax.ppermute(value, 'mp', chip_pairs)]
    pallas_call x45 -> x41, Pallas kernels: 65.9 us -> 65.7 us  [vmem_call(): pl.pallas_call(kernel, in_specs=specs, out_specs=[vmem] * len(outs), out_...]
where the time goes in v5:
time: 295 us; the launch traced here: 291 us
  waiting for transfers between devices  113 us (38%)
  starting transfers between devices  89.6 us (30%)
  Pallas kernels  75.9 us (26%)
  matrix products  5.74 us (2%)
  other arithmetic  3.41 us (1%)
    pallas_call x41, Pallas kernels, vmem_call(): pl.pallas_call(kernel, in_specs=specs, out_specs=[vmem] * len(outs), out_...  65.7 us
    ppermute x9, waiting for transfers between devices, chip_swap(): return lax.ppermute(value, 'mp', chip_pairs)  44.7 us
    ppermute x28, waiting for transfers between devices, body(): arrived[k].append(lax.ppermute(arrived[k][-1], 'dp', routes[k % 2]))  31.6 us
    ppermute x28, starting transfers between devices, body(): came = lax.ppermute(travelling[k], 'dp', routes[k % 2])  31.2 us
    ppermute x28, starting transfers between devices, body(): arrived[k].append(lax.ppermute(arrived[k][-1], 'dp', routes[k % 2]))  29.9 us
    ppermute x28, waiting for transfers between devices, body(): came = lax.ppermute(travelling[k], 'dp', routes[k % 2])  23.2 us
    ppermute x9, starting transfers between devices, chip_swap(): return lax.ppermute(value, 'mp', chip_pairs)  12 us
    ppermute x2, waiting for transfers between devices, body(): mine = lax.ppermute(out_piece, 'dp', exchange)  9.88 us
  transfers between devices with their start and end apart: 99, of which 50 were waited for; matrix products, arithmetic and copies ran while one was open for 1% of the time, Pallas kernels for 17%

profile of v5, /device:TPU:0, one launch (start us, length us, event | category | flops | bytes accessed | tf_op | source)
XLA Modules:
  0.0 290.8 jit_solution(18199313325314013677)
XLA Ops:
  2.4 3.1 %collective-permute-start = (bf16[6,128,128]{2,1,0:T(8,128)(2,1)S(1)}, bf16[6,128,128]{2,1,0:T(8,128)(2,1)S(1)}, u32[]{:S(2)}, u32[]{:S(2)}) collective-permute-start(bf16[6,128,128]{2,1,0:T(8,128)(2,1)S(1)} %get-tuple-element.387.refs_0_), channel_id=1, source_target_pairs={{0,8},{8,16},{16,24},{24,28},{28,20},{20,12},{12,4},{4,0},{1,9},{9... | collective-permute-start | bytes 589832 | tf_op jit(solution)/shard_map/ppermute | solution.py:902
  7.7 3.5 %collective-permute-done.refs_1_ = bf16[6,128,128]{2,1,0:T(8,128)(2,1)S(1)} collective-permute-done((bf16[6,128,128]{2,1,0:T(8,128)(2,1)S(1)}, bf16[6,128,128]{2,1,0:T(8,128)(2,1)S(1)}, u32[]{:S(2)}, u32[]{:S(2)}) %collective-permute-start) | collective-permute-done | bytes 196640 | tf_op jit(solution)/shard_map/ppermute | solution.py:902
  66.6 3.2 %assemble.1 = (bf16[1024,768]{1,0:T(8,128)(2,1)S(1)}, bf16[256,1024]{1,0:T(8,128)(2,1)S(1)}, bf16[1024,1024]{1,0:T(8,128)(2,1)S(1)}, bf16[1024,1024]{1,0:T(8,128)(2,1)S(1)}) custom-call(s32[6]{0:T(128)S(1)} %stack.31.place_ref, s32[192]{0:T(256)S(1)} %bitcast.17, bf16[6,128,128]{2,1,0:T(8,128)(2,1)S(1)} %get-tuple-element.387.refs_0_, ...), custom_call_target="tpu_custom_call" | custom-call | bytes 1024 | tf_op jit(solution)/shard_map/assemble/pallas_call | solution.py:76
  71.6 3.3 %attention_tile.4 = (bf16[256,256]{1,0:T(8,128)(2,1)S(1)}, f32[4,256]{1,0:T(4,128)S(1)}, bf16[128,1024]{1,0:T(8,128)(2,1)S(1)}, bf16[128,1024]{1,0:T(8,128)(2,1)S(1)}) custom-call(bf16[1024,768]{1,0:T(8,128)(2,1)S(1)} %add_convert_fusion.qkv_ref, bf16[256,1024]{1,0:T(8,128)(2,1)S(1)} %get-tuple-element.204.w_ref, ...), custom_call_target="tpu_custom_call" | custom-call | bytes 1024 | tf_op jit(solution)/shard_map/attention_tile/pallas_call | solution.py:76
  75.5 3.3 %attention_tile.5 = (bf16[256,256]{1,0:T(8,128)(2,1)S(1)}, f32[4,256]{1,0:T(4,128)S(1)}, f32[256,1024]{1,0:T(8,128)S(1)}) custom-call(bf16[1024,768]{1,0:T(8,128)(2,1)S(1)} %add_convert_fusion.qkv_ref, bf16[256,1024]{1,0:T(8,128)(2,1)S(1)} %get-tuple-element.204.w_ref, f32[1024,8]{1,0:T(8,128)S(1)} %get-tuple-element.205.sk_ref.table_ref, ...), custom_call_target="tpu_custom_call" | custom-call | bytes 1024 | tf_op jit(solution)/shard_map/attention_tile/pallas_call | solution.py:76
  80.5 3.3 %attention_tile.6 = (bf16[256,256]{1,0:T(8,128)(2,1)S(1)}, f32[4,256]{1,0:T(4,128)S(1)}, bf16[64,1024]{1,0:T(8,128)(2,1)S(1)}, bf16[64,1024]{1,0:T(8,128)(2,1)S(...) custom-call(bf16[1024,768]{1,0:T(8,128)(2,1)S(1)} %add_convert_fusion.qkv_ref, ...), custom_call_target="tpu_custom_call" | custom-call | bytes 1024 | tf_op jit(solution)/shard_map/attention_tile/pallas_call | solution.py:76
  84.9 3.7 %attention_tile.7 = (bf16[256,256]{1,0:T(8,128)(2,1)S(1)}, f32[4,256]{1,0:T(4,128)S(1)}, f32[256,1024]{1,0:T(8,128)S(1)}) custom-call(bf16[1024,768]{1,0:T(8,128)(2,1)S(1)} %add_convert_fusion.qkv_ref, bf16[256,1024]{1,0:T(8,128)(2,1)S(1)} %get-tuple-element.204.w_ref, f32[1024,8]{1,0:T(8,128)S(1)} %get-tuple-element.205.sk_ref.table_ref, ...), custom_call_target="tpu_custom_call" | custom-call | bytes 1024 | tf_op jit(solution)/shard_map/attention_tile/pallas_call | solution.py:76
  89.4 4.4 %collective-permute-done.30.b_ref = bf16[256,1024]{1,0:T(8,128)(2,1)S(1)} collective-permute-done((bf16[256,1024]{1,0:T(8,128)(2,1)S(1)}, bf16[256,1024]{1,0:T(8,128)(2,1)S(1)}, u32[]{:S(2)}, u32[]{:S(2)}) %collective-permute-start.30) | collective-permute-done | bytes 524320 | tf_op jit(solution)/shard_map/ppermute | solution.py:871
  98.6 5.5 %collective-permute-done.35.b_ref = bf16[256,1024]{1,0:T(8,128)(2,1)S(1)} collective-permute-done((bf16[256,1024]{1,0:T(8,128)(2,1)S(1)}, bf16[256,1024]{1,0:T(8,128)(2,1)S(1)}, u32[]{:S(2)}, u32[]{:S(2)}) %collective-permute-start.35) | collective-permute-done | bytes 524320 | tf_op jit(solution)/shard_map/ppermute | solution.py:871
  112.8 11.7 %collective-permute-done.41.b_ref = bf16[256,1024]{1,0:T(8,128)(2,1)S(1)} collective-permute-done((bf16[256,1024]{1,0:T(8,128)(2,1)S(1)}, bf16[256,1024]{1,0:T(8,128)(2,1)S(1)}, u32[]{:S(2)}, u32[]{:S(2)}) %collective-permute-start.41) | collective-permute-done | bytes 524320 | tf_op jit(solution)/shard_map/ppermute | solution.py:871
  125.7 2.7 collective-permute-start.44
  128.3 6.6 %collective-permute-done.43.b_ref = bf16[256,1024]{1,0:T(8,128)(2,1)S(1)} collective-permute-done((bf16[256,1024]{1,0:T(8,128)(2,1)S(1)}, bf16[256,1024]{1,0:T(8,128)(2,1)S(1)}, u32[]{:S(2)}, u32[]{:S(2)}) %collective-permute-start.43) | collective-permute-done | bytes 524320 | tf_op jit(solution)/shard_map/ppermute | solution.py:871
  136.0 2.7 collective-permute-start.46
  140.3 9.7 %collective-permute-done.46.refs_9_ = bf16[128,1024]{1,0:T(8,128)(2,1)S(1)} collective-permute-done((bf16[128,1024]{1,0:T(8,128)(2,1)S(1)}, bf16[128,1024]{1,0:T(8,128)(2,1)S(1)}, u32[]{:S(2)}, u32[]{:S(2)}) %collective-permute-start.46) | collective-permute-done | bytes 262176 | tf_op jit(solution)/shard_map/ppermute | solution.py:981
  152.1 5.2 %collective-permute-done.47.refs_10_ = bf16[128,1024]{1,0:T(8,128)(2,1)S(1)} collective-permute-done((bf16[128,1024]{1,0:T(8,128)(2,1)S(1)}, bf16[128,1024]{1,0:T(8,128)(2,1)S(1)}, u32[]{:S(2)}, u32[]{:S(2)}) %collective-permute-start.47) | collective-permute-done | bytes 262176 | tf_op jit(solution)/shard_map/ppermute | solution.py:871
  158.8 3.4 %link_back.1 = (f32[256,1024]{1,0:T(8,128)S(1)}, f32[256,1024]{1,0:T(8,128)S(1)}, bf16[256,1024]{1,0:T(8,128)(2,1)S(1)}, bf16[256,1024]{1,0:T(8,128)(2,1)S(1)}, ...) custom-call(s32[6]{0:T(128)S(1)} %stack.31.place_ref, bf16[512,1024]{1,0:T(8,128)(2,1)S(1)} %get-tuple-element.233.link_ref, ...), custom_call_target="tpu_custom_call" | custom-call | bytes 1024 | tf_op jit(solution)/shard_map/link_back/pallas_call | solution.py:76
  173.9 4.5 %feed_grads.1 = (bf16[1024,1024]{1,0:T(8,128)(2,1)S(1)}, bf16[1024,1024]{1,0:T(8,128)(2,1)S(1)}, f32[1,1024]{1,0:T(1,128)S(1)}) custom-call(bf16[256,1024]{1,0:T(8,128)(2,1)S(1)} %get-tuple-element.221.refs_0_, bf16[256,1024]{1,0:T(8,128)(2,1)S(1)} %get-tuple-element.228.refs_1_, bf16[256,1024]{1,0:T(8,128)(2,1)S(1)} %get-tuple-element.229.refs_2_, ...), custom_call_target="tpu_custom_call" | custom-call | bytes 1024 | tf_op jit(solution)/shard_map/feed_grads/pallas_call | solution.py:76
  180.9 3.3 %collective-permute-done.58.b_ref = bf16[256,1024]{1,0:T(8,128)(2,1)S(1)} collective-permute-done((bf16[256,1024]{1,0:T(8,128)(2,1)S(1)}, bf16[256,1024]{1,0:T(8,128)(2,1)S(1)}, u32[]{:S(2)}, u32[]{:S(2)}) %collective-permute-start.58) | collective-permute-done | bytes 524320 | tf_op jit(solution)/shard_map/ppermute | solution.py:871
  187.0 6.7 %attention_backward.2 = (bf16[512,256]{1,0:T(8,128)(2,1)S(1)}, f32[1024,256]{1,0:T(8,128)S(1)}, f32[1024,256]{1,0:T(8,128)S(1)}, f32[256,1024]{1,0:T(8,128)S(1)}, f32[1,256]{1,0:T(1,128)S(1)}) custom-call(bf16[1024,768]{1,0:T(8,128)(2,1)S(1)} %add_convert_fusion.qkv_ref, bf16[256,1024]{1,0:T(8,128)(2,1)S(1)} %get-tuple-element.204.w_ref, ...), custom_call_target="tpu_custom_call" | custom-call | bytes 1024 | tf_op jit(solution)/shard_map/attention_backward/pallas_call | solution.py:76
  197.4 7.2 %attention_backward.3 = (bf16[1024,768]{1,0:T(8,128)(2,1)S(1)}, bf16[256,1024]{1,0:T(8,128)(2,1)S(1)}, f32[1,512]{1,0:T(1,128)S(1)}) custom-call(bf16[1024,768]{1,0:T(8,128)(2,1)S(1)} %add_convert_fusion.qkv_ref, bf16[256,1024]{1,0:T(8,128)(2,1)S(1)} %get-tuple-element.204.w_ref, f32[1024,8]{1,0:T(8,128)S(1)} %get-tuple-element.205.sk_ref.table_ref, ...), custom_call_target="tpu_custom_call" | custom-call | bytes 1024 | tf_op jit(solution)/shard_map/attention_backward/pallas_call | solution.py:76
  212.7 3.7 %collective-permute-done.68 = bf16[6,128,128]{2,1,0:T(8,128)(2,1)S(1)} collective-permute-done((bf16[6,128,128]{2,1,0:T(8,128)(2,1)S(1)}, bf16[6,128,128]{2,1,0:T(8,128)(2,1)S(1)}, u32[]{:S(2)}, u32[]{:S(2)}) %collective-permute-start.68) | collective-permute-done | bytes 196640 | tf_op jit(solution)/shard_map/ppermute | solution.py:1081
  252.2 2.5 collective-permute-start.91
  259.6 7.0 %collective-permute-done.89 = bf16[512,1024]{1,0:T(8,128)(2,1)S(1)} collective-permute-done((bf16[512,1024]{1,0:T(8,128)(2,1)S(1)}, bf16[512,1024]{1,0:T(8,128)(2,1)S(1)}, u32[]{:S(2)}, u32[]{:S(2)}) %collective-permute-start.89) | collective-permute-done | bytes 1048608 | tf_op jit(solution)/shard_map/ppermute | solution.py:871
  283.5 6.3 %optimize.1 = (f32[24,128,128]{2,1,0:T(8,128)}, f32[24,128,128]{2,1,0:T(8,128)}, f32[24,128,128]{2,1,0:T(8,128)}, f32[24,128,128]{2,1,0:T(8,128)}) custom-call(bf16[6,128,128]{2,1,0:T(8,128)(2,1)S(1)} %collective-permute-done.92.refs_0_, bf16[6,128,128]{2,1,0:T(8,128)(2,1)S(1)} %collective-permute-done.94.refs_1_, ...), custom_call_target="tpu_custom_call" | custom-call | bytes 1024 | tf_op jit(solution)/shard_map/optimize/pallas_call | solution.py:379
  (287 shorter events, 172.5 us)
Async XLA Ops:
  5.5 9.9 %collective-permute-start.14 = (bf16[6,128,128]{2,1,0:T(8,128)(2,1)S(1)}, bf16[6,128,128]{2,1,0:T(8,128)(2,1)S(1)}, u32[]{:S(2)}, u32[]{:S(2)}) collective-permute-start(bf16[6,128,128]{2,1,0:T(8,128)(2,1)S(1)} %get-tuple-element.385.refs_16_), channel_id=1, source_target_pairs={{0,8},{8,16},{16,24},{24,28},{28,20},{20,12},{12,4},{4,0},{1,9},{9... | collective-permute-start | bytes 589832 | tf_op jit(solution)/shard_map/ppermute | solution.py:902
  7.5 10.1 %collective-permute-start.21 = (bf16[6,128,128]{2,1,0:T(8,128)(2,1)S(1)}, bf16[6,128,128]{2,1,0:T(8,128)(2,1)}, u32[]{:S(2)}, u32[]{:S(2)}) collective-permute-start(bf16[6,128,128]{2,1,0:T(8,128)(2,1)S(1)} %get-tuple-element.384.refs_24_), channel_id=1, source_target_pairs={{8,0},{16,8},{24,16},{28,24},{20,28},{12,20},{4,12},{0,4},{9,1},{1... | collective-permute-start | bytes 589832 | tf_op jit(solution)/shard_map/ppermute | solution.py:902
  78.9 14.8 %collective-permute-start.30 = (bf16[256,1024]{1,0:T(8,128)(2,1)S(1)}, bf16[256,1024]{1,0:T(8,128)(2,1)S(1)}, u32[]{:S(2)}, u32[]{:S(2)}) collective-permute-start(bf16[256,1024]{1,0:T(8,128)(2,1)S(1)} %add_low.11.a_ref), channel_id=1, source_target_pairs={{0,2},{1,3},{2,0},{3,1},{4,6},{5,7},{6,4},{7,5},{8,10},{9,11},{10,... | collective-permute-start | bytes 1572872 | tf_op jit(solution)/shard_map/ppermute | solution.py:871
  88.7 15.4 %collective-permute-start.35 = (bf16[256,1024]{1,0:T(8,128)(2,1)S(1)}, bf16[256,1024]{1,0:T(8,128)(2,1)S(1)}, u32[]{:S(2)}, u32[]{:S(2)}) collective-permute-start(bf16[256,1024]{1,0:T(8,128)(2,1)S(1)} %add_low.12.a_ref), channel_id=1, source_target_pairs={{0,2},{1,3},{2,0},{3,1},{4,6},{5,7},{6,4},{7,5},{8,10},{9,11},{10,... | collective-permute-start | bytes 1572872 | tf_op jit(solution)/shard_map/ppermute | solution.py:871
  109.7 14.8 %collective-permute-start.41 = (bf16[256,1024]{1,0:T(8,128)(2,1)S(1)}, bf16[256,1024]{1,0:T(8,128)(2,1)S(1)}, u32[]{:S(2)}, u32[]{:S(2)}) collective-permute-start(bf16[256,1024]{1,0:T(8,128)(2,1)S(1)} %add_low.13.a_ref), channel_id=1, source_target_pairs={{0,2},{1,3},{2,0},{3,1},{4,6},{5,7},{6,4},{7,5},{8,10},{9,11},{10,... | collective-permute-start | bytes 1572872 | tf_op jit(solution)/shard_map/ppermute | solution.py:871
  111.4 23.5 %collective-permute-start.43 = (bf16[256,1024]{1,0:T(8,128)(2,1)S(1)}, bf16[256,1024]{1,0:T(8,128)(2,1)S(1)}, u32[]{:S(2)}, u32[]{:S(2)}) collective-permute-start(bf16[256,1024]{1,0:T(8,128)(2,1)S(1)} %add_low.14.a_ref), channel_id=1, source_target_pairs={{0,2},{1,3},{2,0},{3,1},{4,6},{5,7},{6,4},{7,5},{8,10},{9,11},{10,... | collective-permute-start | bytes 1572872 | tf_op jit(solution)/shard_map/ppermute | solution.py:871
  125.7 13.2 %collective-permute-start.44 = (bf16[128,1024]{1,0:T(8,128)(2,1)S(1)}, bf16[128,1024]{1,0:T(8,128)(2,1)S(1)}, u32[]{:S(2)}, u32[]{:S(2)}) collective-permute-start(bf16[128,1024]{1,0:T(8,128)(2,1)S(1)} %get-tuple-element.243), channel_id=1, source_target_pairs={{0,16},{4,20},{8,24},{12,28},{16,0},{20,4},{24,8},{28,12},{1,17},{... | collective-permute-start | bytes 786440 | tf_op jit(solution)/shard_map/ppermute | solution.py:981
  136.0 14.0 %collective-permute-start.46 = (bf16[128,1024]{1,0:T(8,128)(2,1)S(1)}, bf16[128,1024]{1,0:T(8,128)(2,1)S(1)}, u32[]{:S(2)}, u32[]{:S(2)}) collective-permute-start(bf16[128,1024]{1,0:T(8,128)(2,1)S(1)} %get-tuple-element.244), channel_id=1, source_target_pairs={{0,16},{4,20},{8,24},{12,28},{16,0},{20,4},{24,8},{28,12},{1,17},{... | collective-permute-start | bytes 786440 | tf_op jit(solution)/shard_map/ppermute | solution.py:981
  138.8 13.2 %collective-permute-start.45 = (bf16[128,1024]{1,0:T(8,128)(2,1)S(1)}, bf16[128,1024]{1,0:T(8,128)(2,1)S(1)}, u32[]{:S(2)}, u32[]{:S(2)}) collective-permute-start(bf16[128,1024]{1,0:T(8,128)(2,1)S(1)} %collective-permute-done.44.refs_7_), channel_id=1, source_target_pairs={{0,2},{1,3},{2,0},{3,1},{4,6},{5,7},{6,4},{7,5},{8,10},{9,11},{10,... | collective-permute-start | bytes 786440 | tf_op jit(solution)/shard_map/ppermute | solution.py:871
  169.4 14.8 %collective-permute-start.58 = (bf16[256,1024]{1,0:T(8,128)(2,1)S(1)}, bf16[256,1024]{1,0:T(8,128)(2,1)S(1)}, u32[]{:S(2)}, u32[]{:S(2)}) collective-permute-start(bf16[256,1024]{1,0:T(8,128)(2,1)S(1)} %add_low.16.a_ref), channel_id=1, source_target_pairs={{0,2},{1,3},{2,0},{3,1},{4,6},{5,7},{6,4},{7,5},{8,10},{9,11},{10,... | collective-permute-start | bytes 1572872 | tf_op jit(solution)/shard_map/ppermute | solution.py:871
  171.0 23.6 %collective-permute-start.59 = (bf16[256,1024]{1,0:T(8,128)(2,1)S(1)}, bf16[256,1024]{1,0:T(8,128)(2,1)S(1)}, u32[]{:S(2)}, u32[]{:S(2)}) collective-permute-start(bf16[256,1024]{1,0:T(8,128)(2,1)S(1)} %add_low.15.a_ref), channel_id=1, source_target_pairs={{0,2},{1,3},{2,0},{3,1},{4,6},{5,7},{6,4},{7,5},{8,10},{9,11},{10,... | collective-permute-start | bytes 1572872 | tf_op jit(solution)/shard_map/ppermute | solution.py:871
  210.7 9.9 %collective-permute-start.66 = (bf16[6,128,128]{2,1,0:T(8,128)(2,1)S(1)}, bf16[6,128,128]{2,1,0:T(8,128)(2,1)S(1)}, u32[]{:S(2)}, u32[]{:S(2)}) collective-permute-start(bf16[6,128,128]{2,1,0:T(8,128)(2,1)S(1)} %get-tuple-element.305), channel_id=1, source_target_pairs={{0,8},{8,16},{16,24},{24,28},{28,20},{20,12},{12,4},{4,0},{1,9},{9... | collective-permute-start | bytes 589832 | tf_op jit(solution)/shard_map/ppermute | solution.py:1081
  212.4 10.0 %collective-permute-start.65 = (bf16[6,128,128]{2,1,0:T(8,128)(2,1)S(1)}, bf16[6,128,128]{2,1,0:T(8,128)(2,1)S(1)}, u32[]{:S(2)}, u32[]{:S(2)}) collective-permute-start(bf16[6,128,128]{2,1,0:T(8,128)(2,1)S(1)} %get-tuple-element.303), channel_id=1, source_target_pairs={{8,0},{16,8},{24,16},{28,24},{20,28},{12,20},{4,12},{0,4},{9,1},{1... | collective-permute-start | bytes 589832 | tf_op jit(solution)/shard_map/ppermute | solution.py:1081
  222.9 9.9 %collective-permute-start.77 = (f32[16,1024]{1,0:T(8,128)S(1)}, f32[16,1024]{1,0:T(8,128)S(1)}, u32[]{:S(2)}, u32[]{:S(2)}) collective-permute-start(f32[16,1024]{1,0:T(8,128)S(1)} %add_biases.1), channel_id=1, source_target_pairs={{0,4},{4,0},{8,12},{12,8},{16,20},{20,16},{24,28},{28,24},{1,5},{5... | collective-permute-start | bytes 196616 | tf_op jit(solution)/shard_map/ppermute | solution.py:1102
  225.2 16.1 %collective-permute-start.88 = (bf16[512,1024]{1,0:T(8,128)(2,1)S(1)}, bf16[512,1024]{1,0:T(8,128)(2,1)S(1)}, u32[]{:S(2)}, u32[]{:S(2)}) collective-permute-start(bf16[512,1024]{1,0:T(8,128)(2,1)S(1)} %convolution_convert_fusion.1), channel_id=1, source_target_pairs={{0,1},{1,0},{2,3},{3,2},{4,5},{5,4},{6,7},{7,6},{8,9},{9,8},{10,11... | collective-permute-start | bytes 3145736 | tf_op jit(solution)/shard_map/ppermute | solution.py:868
  235.3 9.7 %collective-permute-start.80 = (bf16[6,128,128]{2,1,0:T(8,128)(2,1)S(1)}, bf16[6,128,128]{2,1,0:T(8,128)(2,1)S(1)}, u32[]{:S(2)}, u32[]{:S(2)}) collective-permute-start(bf16[6,128,128]{2,1,0:T(8,128)(2,1)S(1)} %add_convert_fusion.11), channel_id=1, source_target_pairs={{8,0},{16,8},{24,16},{28,24},{20,28},{12,20},{4,12},{0,4},{9,1},{1... | collective-permute-start | bytes 589832 | tf_op jit(solution)/shard_map/ppermute | solution.py:1081
  243.2 23.4 %collective-permute-start.89 = (bf16[512,1024]{1,0:T(8,128)(2,1)S(1)}, bf16[512,1024]{1,0:T(8,128)(2,1)S(1)}, u32[]{:S(2)}, u32[]{:S(2)}) collective-permute-start(bf16[512,1024]{1,0:T(8,128)(2,1)S(1)} %add_low.21), channel_id=1, source_target_pairs={{0,2},{1,3},{2,0},{3,1},{4,6},{5,7},{6,4},{7,5},{8,10},{9,11},{10,... | collective-permute-start | bytes 3145736 | tf_op jit(solution)/shard_map/ppermute | solution.py:871
  249.6 9.7 %collective-permute-start.82 = (bf16[6,128,128]{2,1,0:T(8,128)(2,1)S(1)}, bf16[6,128,128]{2,1,0:T(8,128)(2,1)S(1)}, u32[]{:S(2)}, u32[]{:S(2)}) collective-permute-start(bf16[6,128,128]{2,1,0:T(8,128)(2,1)S(1)} %add_convert_fusion.5), channel_id=1, source_target_pairs={{8,0},{16,8},{24,16},{28,24},{20,28},{12,20},{4,12},{0,4},{9,1},{1... | collective-permute-start | bytes 589832 | tf_op jit(solution)/shard_map/ppermute | solution.py:1081
  252.2 17.2 %collective-permute-start.91 = (bf16[6,128,128]{2,1,0:T(8,128)(2,1)S(1)}, bf16[6,128,128]{2,1,0:T(8,128)(2,1)S(1)}, u32[]{:S(2)}, u32[]{:S(2)}) collective-permute-start(bf16[6,128,128]{2,1,0:T(8,128)(2,1)S(1)} %add_low.17), channel_id=1, source_target_pairs={{0,8},{8,16},{16,24},{24,28},{28,20},{20,12},{12,4},{4,0},{1,9},{9... | collective-permute-start | bytes 589832 | tf_op jit(solution)/shard_map/ppermute | solution.py:1081
  255.2 14.3 %collective-permute-start.93 = (bf16[6,128,128]{2,1,0:T(8,128)(2,1)S(1)}, bf16[6,128,128]{2,1,0:T(8,128)(2,1)S(1)}, u32[]{:S(2)}, u32[]{:S(2)}) collective-permute-start(bf16[6,128,128]{2,1,0:T(8,128)(2,1)S(1)} %add_low.18), channel_id=1, source_target_pairs={{8,0},{16,8},{24,16},{28,24},{20,28},{12,20},{4,12},{0,4},{9,1},{1... | collective-permute-start | bytes 589832 | tf_op jit(solution)/shard_map/ppermute | solution.py:1081
  256.4 15.6 %collective-permute-start.95 = (bf16[6,128,128]{2,1,0:T(8,128)(2,1)S(1)}, bf16[6,128,128]{2,1,0:T(8,128)(2,1)S(1)}, u32[]{:S(2)}, u32[]{:S(2)}) collective-permute-start(bf16[6,128,128]{2,1,0:T(8,128)(2,1)S(1)} %add_low.19), channel_id=1, source_target_pairs={{0,8},{8,16},{16,24},{24,28},{28,20},{20,12},{12,4},{4,0},{1,9},{9... | collective-permute-start | bytes 589832 | tf_op jit(solution)/shard_map/ppermute | solution.py:1081
  259.4 12.7 %collective-permute-start.97 = (bf16[6,128,128]{2,1,0:T(8,128)(2,1)S(1)}, bf16[6,128,128]{2,1,0:T(8,128)(2,1)S(1)}, u32[]{:S(2)}, u32[]{:S(2)}) collective-permute-start(bf16[6,128,128]{2,1,0:T(8,128)(2,1)S(1)} %add_low.20), channel_id=1, source_target_pairs={{8,0},{16,8},{24,16},{28,24},{20,28},{12,20},{4,12},{0,4},{9,1},{1... | collective-permute-start | bytes 589832 | tf_op jit(solution)/shard_map/ppermute | solution.py:1081
  272.0 9.6 %collective-permute-start.96 = (bf16[6,128,128]{2,1,0:T(8,128)(2,1)S(1)}, bf16[6,128,128]{2,1,0:T(8,128)(2,1)S(1)}, u32[]{:S(2)}, u32[]{:S(2)}) collective-permute-start(bf16[6,128,128]{2,1,0:T(8,128)(2,1)S(1)} %add_convert_fusion.2), channel_id=1, source_target_pairs={{0,8},{8,16},{16,24},{24,28},{28,20},{20,12},{12,4},{4,0},{1,9},{9... | collective-permute-start | bytes 589832 | tf_op jit(solution)/shard_map/ppermute | solution.py:1081
  274.2 9.2 %collective-permute-start.94 = (bf16[6,128,128]{2,1,0:T(8,128)(2,1)S(1)}, bf16[6,128,128]{2,1,0:T(8,128)(2,1)S(1)}, u32[]{:S(2)}, u32[]{:S(2)}) collective-permute-start(bf16[6,128,128]{2,1,0:T(8,128)(2,1)S(1)} %add_convert_fusion.3), channel_id=1, source_target_pairs={{8,0},{16,8},{24,16},{28,24},{20,28},{12,20},{4,12},{0,4},{9,1},{1... | collective-permute-start | bytes 589832 | tf_op jit(solution)/shard_map/ppermute | solution.py:1081
  (90 other events, 612.2 us)
